TPU v7x, 32 devices: a whole 2x2x4 slice. The times are simulated.
32 devices in a mesh: ctx: 8 (over z, y), fsdp: 4 (over x, core).
Axes of the slice: x: 2, y: 2, z: 4, core: 2. Of those that a mesh axis runs over, the one named last changes fastest.
Arguments:
- inputs: float32 [12288, 768], P(('ctx', 'fsdp')), may hold values from -6 to 6
- out_grad: float32 [12288, 768], P(('ctx', 'fsdp')), may hold values from -6 to 6
- vectors: float32 [4, 768], replicated
- block_order: int32 [4, 32], P('fsdp'), may hold values from 0 to 31, as said below
- seq_lengths: int32 [4, 4], P('fsdp'), may hold values from 1 to 1536, 3072 in all within a row
- expert_ids: int32 [12288, 2], P(('ctx', 'fsdp')), may hold values from 0 to 11, all different within a row; in each aligned block of 384 rows (0 to 383, 384 to 767, ...) at most 96 rows name the same one
- attn_weights: bfloat16 [144, 128, 128], P('fsdp')
- attn_left: float32 [144, 128, 128], P('fsdp'), as said below
- attn_right: float32 [144, 128, 128], P('fsdp'), as said below
- attn_left_root: float32 [144, 128, 128], P('fsdp'), as said below
- attn_right_root: float32 [144, 128, 128], P('fsdp'), as said below
- expert_weights: bfloat16 [8, 288, 128, 128], P('fsdp', 'ctx')
- expert_left: float32 [8, 288, 128, 128], P('fsdp', 'ctx'), as said below
- expert_right: float32 [8, 288, 128, 128], P('fsdp', 'ctx'), as said below
- expert_left_root: float32 [8, 288, 128, 128], P('fsdp', 'ctx'), as said below
- expert_right_root: float32 [8, 288, 128, 128], P('fsdp', 'ctx'), as said below
- router_weights: bfloat16 [768, 12], replicated, may hold values from -0.15625 to 0.15625
- router_left: float32 [6, 128, 128], replicated, as said below
- router_right: float32 [6, 12, 12], replicated, as said below
- router_left_root: float32 [6, 128, 128], replicated, as said below
- router_right_root: float32 [6, 12, 12], replicated, as said below
Outputs:
- output: float32 [12288, 768], P(('ctx', 'fsdp'))
- input_grad: float32 [12288, 768], P(('ctx', 'fsdp'))
- vector_grads: float32 [4, 768], replicated
- vector_new: float32 [4, 768], replicated
- attn_grads: float32 [144, 128, 128], P('fsdp')
- attn_left_new: float32 [144, 128, 128], P('fsdp')
- attn_right_new: float32 [144, 128, 128], P('fsdp')
- attn_new: float32 [144, 128, 128], P('fsdp')
- expert_grads: float32 [8, 288, 128, 128], P('fsdp', 'ctx')
- expert_left_new: float32 [8, 288, 128, 128], P('fsdp', 'ctx')
- expert_right_new: float32 [8, 288, 128, 128], P('fsdp', 'ctx')
- expert_new: float32 [8, 288, 128, 128], P('fsdp', 'ctx')
- router_grads: float32 [768, 12], replicated
- router_left_new: float32 [6, 128, 128], replicated
- router_right_new: float32 [6, 12, 12], replicated
- router_new: float32 [768, 12], replicated
Inputs may be any that keep to these rules, and one draw needn't show every extreme that they name: On device c of ctx in group g, rows k * 96 to (k + 1) * 96 - 1 hold the places from block_order[g, c * 4 + k] * 96 on, in order; each row of block_order is a permutation of 0 to 31 whose entry c * 4 + k lies between k * 8 and (k + 1) * 8 - 1. `seq_lengths`: row g sums to 3072; its largest entry is 1536. `expert_ids`: A token's two ids differ. Ids below 8 are feed-forward experts, 8 the zero expert, 9 the copy expert, higher ones constant experts. Among the rows of one device no id appears more than 96 times, and some id reaches 96. `attn_left`: symmetric. `attn_right`: symmetric. `attn_left_root`: symmetric. `attn_right_root`: symmetric. `expert_left`: symmetric. `expert_right`: symmetric. `expert_left_root`: symmetric. `expert_right_root`: symmetric. `router_left`: symmetric. `router_right`: symmetric. `router_left_root`: symmetric. `router_right_root`: symmetric.
All inputs are finite; a program needn't handle non-finite values.
Results may differ from a plain program's by a relative error of at most 0.01.
The roundings to bfloat16 on the way count: a program that leaves them out, or rounds other values in their place, can miss the bound.
Values may be sent and summed in bfloat16 or wider, within the bound.
No kernel may reach another device: no remote copies, remote signals or barrier semaphores. Data moves between devices by JAX's collectives and lax.ppermute only.
A program may use at most 256 MiB of HBM per device.

v0:
```python
import jax
import jax.numpy as jnp
from jax import lax
from jax.sharding import PartitionSpec as P

D = 768
HEADS = 12
HDIM = 64
EXPERTS = 8
ZEROS = 4
BS = 128
SLOTS = 4


EPSILON = 1e-06
SCORE_SCALE = 0.125
STAT_DECAY = 0.5
RATE_PROJECT = 0.4
RATE_OUTPUT = 3.0
RATE_EXPERT = 0.4
RATE_ROUTER = 0.2
RATE_VECTOR = 0.1
MASKED_SCORE = -1e30
PRECISE = lax.Precision.HIGHEST


def to_matrix(blocks, height, breadth):
    block_height = blocks.shape[1]
    block_breadth = blocks.shape[2]
    shaped = blocks.reshape(
        height // block_height, breadth // block_breadth, block_height, block_breadth
    )
    return shaped.transpose(0, 2, 1, 3).reshape(height, breadth)


def to_blocks(matrix, block_height, block_breadth):
    height = matrix.shape[0]
    breadth = matrix.shape[1]
    shaped = matrix.reshape(
        height // block_height, block_height, breadth // block_breadth, block_breadth
    )
    return shaped.transpose(0, 2, 1, 3).reshape(-1, block_height, block_breadth)


def normalize_parts(values, scaling):
    factor = lax.rsqrt(jnp.mean(values * values, axis=-1, keepdims=True) + EPSILON)
    return (values * factor * scaling, factor)


def normalize_back(values, factor, scaling, gradient):
    unit_rows = values * factor
    scaled = gradient * scaling
    value_grad = factor * (
        scaled - unit_rows * jnp.mean(scaled * unit_rows, axis=-1, keepdims=True)
    )
    return (value_grad, jnp.sum(gradient * unit_rows, axis=0))


def block_length(length):
    stride = length
    while stride > 768 and stride % 2 == 0:
        stride = stride // 2
    return stride


def sweep(update, running, pieces, first_row):
    length = pieces[0].shape[0]
    stride = block_length(length)

    def advance(counter, state_now):
        offset = counter * stride
        parts_now = tuple(
            (lax.dynamic_slice_in_dim(member, offset, stride, 0) for member in pieces)
        )
        return update(state_now, parts_now, first_row + offset)

    return lax.fori_loop(0, length // stride, advance, running)


def shampoo_step(weights, gradient, left_stat, right_stat, left_root, right_root, step_rates):
    left_new = STAT_DECAY * left_stat + (1.0 - STAT_DECAY) * jnp.einsum(
        "nij,nkj->nik", gradient, gradient, precision=PRECISE
    )
    right_new = STAT_DECAY * right_stat + (1.0 - STAT_DECAY) * jnp.einsum(
        "nji,njk->nik", gradient, gradient, precision=PRECISE
    )
    turned = jnp.einsum("nij,njk->nik", gradient, right_root, precision=PRECISE)
    direction = jnp.einsum("nij,njk->nik", left_root, turned, precision=PRECISE)
    return (left_new, right_new, weights - step_rates * direction)


def body(
    inputs,
    out_grad,
    vectors,
    block_order,
    seq_lengths,
    expert_ids,
    attn_weights,
    attn_left,
    attn_right,
    attn_left_root,
    attn_right_root,
    expert_weights,
    expert_left,
    expert_right,
    expert_left_root,
    expert_right_root,
    router_weights,
    router_left,
    router_right,
    router_left_root,
    router_right_root,
):
    row_count = inputs.shape[0]
    ctx_count = lax.axis_size("ctx")
    fsdp_count = lax.axis_size("fsdp")
    group_rows = row_count * ctx_count
    tokens_all = group_rows * fsdp_count
    ctx_place = lax.axis_index("ctx")
    part_rows = row_count // SLOTS
    offsets = jnp.arange(part_rows, dtype=jnp.int32)
    places = (block_order[0][:, None] * part_rows + offsets[None, :]).reshape(group_rows)
    sequence_ends = jnp.cumsum(seq_lengths[0])
    documents = jnp.sum((places[:, None] >= sequence_ends[None, :]).astype(jnp.int32), axis=1)
    own_places = lax.dynamic_slice_in_dim(places, ctx_place * row_count, row_count)
    own_documents = lax.dynamic_slice_in_dim(documents, ctx_place * row_count, row_count)
    per_side = D // BS
    attn_all = lax.all_gather(attn_weights, "fsdp", axis=0, tiled=True)
    w_project = to_matrix(attn_all[: 3 * per_side * per_side], D, 3 * D)
    w_output = to_matrix(attn_all[3 * per_side * per_side :], D, D)
    expert_all = lax.all_gather(expert_weights, "ctx", axis=1, tiled=True)
    local_slices = expert_all.shape[0]
    third_part = expert_all.shape[1] // 3
    slice_width = third_part // per_side * BS
    w_gate = jax.vmap(lambda blocks: to_matrix(blocks[:third_part], D, slice_width))(expert_all)
    w_up = jax.vmap(lambda blocks: to_matrix(blocks[third_part : 2 * third_part], D, slice_width))(
        expert_all
    )
    w_down = jax.vmap(lambda blocks: to_matrix(blocks[2 * third_part :], slice_width, D))(
        expert_all
    )
    split_count = local_slices * fsdp_count // EXPERTS
    capacity = row_count // 4
    first_norm, first_factor = normalize_parts(inputs, vectors[0])
    first_low = first_norm.astype(jnp.bfloat16)
    projected = jnp.dot(first_low, w_project, preferred_element_type=jnp.float32).astype(
        jnp.bfloat16
    )
    queries = projected[:, :D].reshape(row_count, HEADS, HDIM)
    key_rows = projected[:, D : 2 * D]
    value_rows = projected[:, 2 * D :]
    key_all, value_all = (
        lax.all_gather(key_rows, "ctx", axis=0, tiled=True),
        lax.all_gather(value_rows, "ctx", axis=0, tiled=True),
    )

    def scored(key_piece, first_row):
        length = key_piece.shape[0]
        scores = (
            jnp.einsum(
                "qhd,khd->hqk",
                queries,
                key_piece.reshape(length, HEADS, HDIM),
                preferred_element_type=jnp.float32,
            )
            * SCORE_SCALE
        )
        key_places = lax.dynamic_slice_in_dim(places, first_row, length)
        key_documents = lax.dynamic_slice_in_dim(documents, first_row, length)
        allowed = (own_documents[:, None] == key_documents[None, :]) & (
            key_places[None, :] <= own_places[:, None]
        )
        return (scores, allowed[None])

    def gather_stats(state_now, parts_now, first_row):
        row_peak, row_total = state_now
        scores, allowed = scored(parts_now[0], first_row)
        scores = jnp.where(allowed, scores, MASKED_SCORE)
        new_peak = jnp.maximum(row_peak, jnp.max(scores, axis=-1))
        shifted = jnp.where(allowed, scores - new_peak[:, :, None], MASKED_SCORE)
        row_total = row_total * jnp.exp(row_peak - new_peak) + jnp.sum(jnp.exp(shifted), axis=-1)
        return (new_peak, row_total)

    start_state = (
        jnp.full((HEADS, row_count), MASKED_SCORE, jnp.float32),
        jnp.zeros((HEADS, row_count), jnp.float32),
    )
    row_peak, row_total = sweep(gather_stats, start_state, (key_all,), 0)

    def probabilities(key_piece, first_row):
        scores, allowed = scored(key_piece, first_row)
        shifted = jnp.where(allowed, scores - row_peak[:, :, None], MASKED_SCORE)
        return jnp.exp(shifted) / row_total[:, :, None]

    def gather_values(state_now, parts_now, first_row):
        weights = probabilities(parts_now[0], first_row).astype(jnp.bfloat16)
        length = parts_now[1].shape[0]
        return state_now + jnp.einsum(
            "hqk,khd->qhd",
            weights,
            parts_now[1].reshape(length, HEADS, HDIM),
            preferred_element_type=jnp.float32,
        )

    attended_raw = sweep(
        gather_values, jnp.zeros((row_count, HEADS, HDIM), jnp.float32), (key_all, value_all), 0
    )
    attended = attended_raw.reshape(row_count, D).astype(jnp.bfloat16)
    middle = inputs + jnp.dot(attended, w_output, preferred_element_type=jnp.float32)
    second, second_factor = normalize_parts(middle, vectors[1])
    second_low = second.astype(jnp.bfloat16)
    logits = jnp.dot(second_low, router_weights, preferred_element_type=jnp.float32)
    route_gates = jax.nn.softmax(jnp.take_along_axis(logits, expert_ids, axis=1), axis=-1)
    numbers = jnp.arange(EXPERTS, dtype=jnp.int32)
    chosen = jnp.any(expert_ids[:, :, None] == numbers[None, None, :], axis=1).astype(jnp.int32)
    row_ranks = jnp.cumsum(chosen, axis=0) - 1
    clipped = jnp.minimum(expert_ids, EXPERTS - 1)
    is_real = expert_ids < EXPERTS
    targets = jnp.where(
        is_real,
        clipped * capacity + jnp.take_along_axis(row_ranks, clipped, axis=1),
        EXPERTS * capacity,
    ).reshape(-1)
    reading = jnp.minimum(targets, EXPERTS * capacity - 1)
    real_rows = is_real.reshape(-1).astype(jnp.float32)

    def to_owners(rows_data):
        flat_buffer = (
            jnp.zeros((EXPERTS * capacity, D), jnp.bfloat16).at[targets].set(rows_data, mode="drop")
        )
        return jnp.repeat(flat_buffer.reshape(EXPERTS, capacity, D), split_count, axis=0)

    def from_owners(returned):
        summed = jnp.sum(
            returned.reshape(EXPERTS, split_count, capacity, D).astype(jnp.float32), axis=1
        ).reshape(EXPERTS * capacity, D)
        return (summed[reading] * real_rows[:, None]).reshape(row_count, 2, D)

    send_rows = jnp.repeat(second_low, 2, axis=0)
    received = lax.all_to_all(to_owners(send_rows), "fsdp", split_axis=0, concat_axis=0, tiled=True)
    item_count = received.shape[1]
    grouped = received.reshape(fsdp_count, local_slices, item_count, D)
    gate_proj = jnp.einsum("fsmd,sdh->fsmh", grouped, w_gate, preferred_element_type=jnp.float32)
    up_proj = jnp.einsum("fsmd,sdh->fsmh", grouped, w_up, preferred_element_type=jnp.float32)
    activated = (jax.nn.silu(gate_proj) * up_proj).astype(jnp.bfloat16)
    result = jnp.einsum(
        "fsmh,shd->fsmd", activated, w_down, preferred_element_type=jnp.float32
    ).astype(jnp.bfloat16)
    returned = lax.all_to_all(
        result.reshape(fsdp_count * local_slices, item_count, D),
        "fsdp",
        split_axis=0,
        concat_axis=0,
        tiled=True,
    )
    keep_shape = (fsdp_count * local_slices, item_count, slice_width)
    returned, received, gate_proj, up_proj, activated = (
        returned,
        received,
        gate_proj.reshape(keep_shape),
        up_proj.reshape(keep_shape),
        activated.reshape(keep_shape),
    )
    expert_rows = from_owners(returned)
    const_numbers = EXPERTS + 2 + jnp.arange(ZEROS - 2, dtype=jnp.int32)
    const_member = (expert_ids[:, :, None] == const_numbers[None, None, :]).astype(jnp.float32)
    copy_member = (expert_ids == EXPERTS + 1).astype(jnp.float32)
    route_values = (
        expert_rows
        + copy_member[:, :, None] * second[:, None, :]
        + jnp.einsum("rkc,cd->rkd", const_member, vectors[2:], precision=PRECISE)
    )
    output = middle + jnp.sum(route_gates[:, :, None] * route_values, axis=1)
    gate_grad = jnp.sum(out_grad[:, None, :] * route_values, axis=2)
    picked_grad = route_gates * (
        gate_grad - jnp.sum(route_gates * gate_grad, axis=1, keepdims=True)
    )
    route_count = EXPERTS + ZEROS
    route_member = (
        expert_ids[:, :, None] == jnp.arange(route_count, dtype=jnp.int32)[None, None, :]
    ).astype(jnp.float32)
    logit_grad = jnp.sum(route_member * picked_grad[:, :, None], axis=1)
    router_local = jnp.dot(second_low.astype(jnp.float32).T, logit_grad, precision=PRECISE)
    second_grad = jnp.dot(logit_grad, router_weights.astype(jnp.float32).T, precision=PRECISE)
    second_grad = second_grad + jnp.sum(route_gates * copy_member, axis=1)[:, None] * out_grad
    const_grad = jnp.einsum("rkc,rk,rd->cd", const_member, route_gates, out_grad, precision=PRECISE)
    grad_rows = (route_gates[:, :, None] * out_grad[:, None, :]).astype(jnp.bfloat16).reshape(-1, D)
    arrived = lax.all_to_all(to_owners(grad_rows), "fsdp", split_axis=0, concat_axis=0, tiled=True)
    item_count = arrived.shape[1]
    owner_shape = (fsdp_count, local_slices, item_count, slice_width)
    grouped_grad = arrived.reshape(fsdp_count, local_slices, item_count, D)
    gate_now = gate_proj.reshape(owner_shape)
    up_now = up_proj.reshape(owner_shape)
    activated_now = activated.reshape(owner_shape)
    entered = received.reshape(fsdp_count, local_slices, item_count, D)
    inner_grad = jnp.einsum(
        "fsmd,shd->fsmh", grouped_grad, w_down, preferred_element_type=jnp.float32
    )
    sigmoid_gate = jax.nn.sigmoid(gate_now)
    up_grad = (inner_grad * (gate_now * sigmoid_gate)).astype(jnp.bfloat16)
    gate_grad_rows = (
        inner_grad * up_now * (sigmoid_gate * (1.0 + gate_now * (1.0 - sigmoid_gate)))
    ).astype(jnp.bfloat16)
    input_back = jnp.einsum(
        "fsmh,sdh->fsmd", gate_grad_rows, w_gate, preferred_element_type=jnp.float32
    ) + jnp.einsum("fsmh,sdh->fsmd", up_grad, w_up, preferred_element_type=jnp.float32)
    input_back = input_back.astype(jnp.bfloat16).reshape(fsdp_count * local_slices, item_count, D)
    back_rows = lax.all_to_all(input_back, "fsdp", split_axis=0, concat_axis=0, tiled=True)
    second_grad = second_grad + jnp.sum(from_owners(back_rows), axis=1)
    gate_weight_grad = jnp.einsum(
        "fsmd,fsmh->sdh", entered, gate_grad_rows, preferred_element_type=jnp.float32
    )
    up_weight_grad = jnp.einsum(
        "fsmd,fsmh->sdh", entered, up_grad, preferred_element_type=jnp.float32
    )
    down_weight_grad = jnp.einsum(
        "fsmh,fsmd->shd", activated_now, grouped_grad, preferred_element_type=jnp.float32
    )

    def slice_blocks(gate_matrix, up_matrix, down_matrix):
        return jnp.concatenate(
            [
                to_blocks(gate_matrix, BS, BS),
                to_blocks(up_matrix, BS, BS),
                to_blocks(down_matrix, BS, BS),
            ],
            axis=0,
        )

    expert_local = jax.vmap(slice_blocks)(gate_weight_grad, up_weight_grad, down_weight_grad)
    expert_grads = lax.psum_scatter(expert_local, "ctx", scatter_dimension=1, tiled=True)
    middle_part, second_gain_grad = normalize_back(middle, second_factor, vectors[1], second_grad)
    middle_grad = out_grad + middle_part
    middle_low = middle_grad.astype(jnp.bfloat16)
    output_weight_grad = jnp.einsum(
        "rd,re->de", attended, middle_low, preferred_element_type=jnp.float32
    )
    attended_grad = (
        jnp.einsum("re,de->rd", middle_low, w_output, preferred_element_type=jnp.float32)
        .astype(jnp.bfloat16)
        .reshape(row_count, HEADS, HDIM)
    )
    row_delta = jnp.sum(attended_grad.astype(jnp.float32) * attended_raw, axis=2).T

    def gather_grads(state_now, parts_now, first_row):
        query_grad, key_terms = state_now
        key_piece, value_piece = parts_now
        length = key_piece.shape[0]
        key_heads = key_piece.reshape(length, HEADS, HDIM)
        value_heads = value_piece.reshape(length, HEADS, HDIM)
        weights = probabilities(key_piece, first_row)
        prob_grad = jnp.einsum(
            "qhd,khd->hqk", attended_grad, value_heads, preferred_element_type=jnp.float32
        )
        score_grad = (weights * (prob_grad - row_delta[:, :, None])).astype(jnp.bfloat16)
        query_grad = query_grad + SCORE_SCALE * jnp.einsum(
            "hqk,khd->qhd", score_grad, key_heads, preferred_element_type=jnp.float32
        )
        key_grad = SCORE_SCALE * jnp.einsum(
            "hqk,qhd->khd", score_grad, queries, preferred_element_type=jnp.float32
        )
        value_grad = jnp.einsum(
            "hqk,qhd->khd",
            weights.astype(jnp.bfloat16),
            attended_grad,
            preferred_element_type=jnp.float32,
        )
        segment = jnp.concatenate(
            [key_grad.reshape(length, D), value_grad.reshape(length, D)], axis=1
        )
        return (query_grad, lax.dynamic_update_slice_in_dim(key_terms, segment, first_row, 0))

    query_zero = jnp.zeros((row_count, HEADS, HDIM), jnp.float32)
    start_back = (query_zero, jnp.zeros((group_rows, 2 * D), jnp.float32))
    back_state = sweep(
        gather_grads,
        start_back,
        (
            lax.all_gather(key_rows, "ctx", axis=0, tiled=True),
            lax.all_gather(value_rows, "ctx", axis=0, tiled=True),
        ),
        jnp.int32(0),
    )
    query_grad = back_state[0]
    pair_grad = lax.psum_scatter(back_state[1], "ctx", scatter_dimension=0, tiled=True)
    project_grad = jnp.concatenate([query_grad.reshape(row_count, D), pair_grad], axis=1).astype(
        jnp.bfloat16
    )
    project_weight_grad = jnp.einsum(
        "rd,re->de", first_low, project_grad, preferred_element_type=jnp.float32
    )
    first_grad = jnp.einsum(
        "re,de->rd", project_grad, w_project, preferred_element_type=jnp.float32
    )
    input_part, first_gain_grad = normalize_back(inputs, first_factor, vectors[0], first_grad)
    input_grad = middle_grad + input_part
    attn_local = jnp.concatenate(
        [to_blocks(project_weight_grad, BS, BS), to_blocks(output_weight_grad, BS, BS)], axis=0
    )
    attn_grads = lax.psum(
        lax.psum_scatter(attn_local, "fsdp", scatter_dimension=0, tiled=True), "ctx"
    )
    vector_local = jnp.concatenate(
        [first_gain_grad[None], second_gain_grad[None], const_grad], axis=0
    )
    router_grads, vector_grads = lax.psum((router_local, vector_local), ("ctx", "fsdp"))
    per_device = attn_weights.shape[0]
    block_numbers = lax.axis_index("fsdp") * per_device + jnp.arange(per_device, dtype=jnp.int32)
    attn_rates = jnp.where(block_numbers < 3 * per_side * per_side, RATE_PROJECT, RATE_OUTPUT)[
        :, None, None
    ]
    attn_left_new, attn_right_new, attn_new = shampoo_step(
        attn_weights.astype(jnp.float32),
        attn_grads,
        attn_left,
        attn_right,
        attn_left_root,
        attn_right_root,
        attn_rates,
    )
    flat_shape = (-1, BS, BS)
    expert_left_flat, expert_right_flat, expert_flat = shampoo_step(
        expert_weights.astype(jnp.float32).reshape(flat_shape),
        expert_grads.reshape(flat_shape),
        expert_left.reshape(flat_shape),
        expert_right.reshape(flat_shape),
        expert_left_root.reshape(flat_shape),
        expert_right_root.reshape(flat_shape),
        RATE_EXPERT,
    )
    expert_left_new = expert_left_flat.reshape(expert_left.shape)
    expert_right_new = expert_right_flat.reshape(expert_right.shape)
    expert_new = expert_flat.reshape(expert_weights.shape)
    router_left_new, router_right_new, router_moved = shampoo_step(
        to_blocks(router_weights.astype(jnp.float32), BS, route_count),
        to_blocks(router_grads, BS, route_count),
        router_left,
        router_right,
        router_left_root,
        router_right_root,
        RATE_ROUTER,
    )
    router_new = to_matrix(router_moved, D, route_count)
    vector_new = vectors - RATE_VECTOR * float(tokens_all) ** (-0.5) * vector_grads
    return (
        output,
        input_grad,
        vector_grads,
        vector_new,
        attn_grads,
        attn_left_new,
        attn_right_new,
        attn_new,
        expert_grads,
        expert_left_new,
        expert_right_new,
        expert_new,
        router_grads,
        router_left_new,
        router_right_new,
        router_new,
    )


def solution(mesh):
    in_specs = (
        P(("ctx", "fsdp"), None),
        P(("ctx", "fsdp"), None),
        P(),
        P("fsdp", None),
        P("fsdp", None),
        P(("ctx", "fsdp"), None),
        P("fsdp", None, None),
        P("fsdp", None, None),
        P("fsdp", None, None),
        P("fsdp", None, None),
        P("fsdp", None, None),
        P("fsdp", "ctx", None, None),
        P("fsdp", "ctx", None, None),
        P("fsdp", "ctx", None, None),
        P("fsdp", "ctx", None, None),
        P("fsdp", "ctx", None, None),
        P(),
        P(),
        P(),
        P(),
        P(),
    )
    out_specs = (
        P(("ctx", "fsdp"), None),
        P(("ctx", "fsdp"), None),
        P(),
        P(),
        P("fsdp", None, None),
        P("fsdp", None, None),
        P("fsdp", None, None),
        P("fsdp", None, None),
        P("fsdp", "ctx", None, None),
        P("fsdp", "ctx", None, None),
        P("fsdp", "ctx", None, None),
        P("fsdp", "ctx", None, None),
        P(),
        P(),
        P(),
        P(),
    )
    return jax.shard_map(body, mesh=mesh, in_specs=in_specs, out_specs=out_specs, check_vma=False)
```

profile of v0, /device:TPU:0, one launch (start us, length us, event | category | flops | bytes accessed | tf_op | source)
XLA Modules:
  0.0 2693.4 jit_solution(5633216954979251842)
XLA Ops:
  10.8 39.0 %all-gather.5.cloned.1.call-done = bf16[144,128,128]{2,1,0:T(8,128)(2,1)} async-done(((bf16[36,128,128]{2,1,0:T(8,128)(2,1)}), bf16[144,128,128]{2,1,0:T(8,128)(2,1)}) %all-gather.5.cloned.1.call-update) | async-done | bytes 4718608 | tf_op jit(solution)/shard_map/all_gather | solution.py:129
  87.1 50.7 %all-gather.7.cloned.1.call-done = bf16[3072,768]{1,0:T(8,128)(2,1)} async-done(((bf16[384,768]{1,0:T(8,128)(2,1)}), bf16[3072,768]{1,0:T(8,128)(2,1)}) %all-gather.7.cloned.1.call-update) | async-done | bytes 4718608 | tf_op jit(solution)/shard_map/all_gather | solution.py:155
  144.3 74.2 %all-gather.9.cloned.1.call-done = bf16[3072,768]{1,0:T(8,128)(2,1)} async-done(((bf16[384,768]{1,0:T(8,128)(2,1)}), bf16[3072,768]{1,0:T(8,128)(2,1)}) %all-gather.9.cloned.1.call-update) | async-done | bytes 4718608 | tf_op jit(solution)/shard_map/all_gather | solution.py:154
  225.2 72.0 %while.46 = (s32[]{:T(128)}, f32[12,384]{1,0:T(8,128)S(1)}, f32[12,384]{1,0:T(8,128)S(1)}, s32[384]{0:T(512)S(1)}, s32[3072]{0:T(1024)}, /*index=5*/s32[3072]{0:...) while((s32[]{:T(128)}, f32[12,384]{1,0:T(8,128)S(1)}, ...), condition=%wide.region_6.7_spmd.clone, body=%wide.region_3.6_spmd.clone.sunk | while | flops 482204160 | bytes 33586376 | solution.py:77
  297.2 51.8 %while.47 = (s32[]{:T(128)}, f32[384,12,64]{0,2,1:T(8,128)}, bf16[3072,768]{0,1:T(8,128)(2,1)}, s32[384]{0:T(512)S(1)}, s32[3072]{0:T(1024)}, /*index=5*/s32[307...) while((s32[]{:T(128)}, f32[384,12,64]{0,2,1:T(8,128)}, ...), condition=%wide.region_8.9_spmd.clone, body=%wide.region_7.8_spmd.clone.sunk | while | flops 925138944 | bytes 10675417 | solution.py:77
  380.6 10.6 scatter_custom_fusion.1
  391.2 189.4 %all-gather.11.cloned.1.call-done = bf16[2,288,128,128]{3,2,1,0:T(8,128)(2,1)} async-done(((bf16[2,36,128,128]{3,2,1,0:T(8,128)(2,1)}), bf16[2,288,128,128]{3,2,1,0:T(8,128)(2,1)}) %all-gather.11.cloned.1.call-update) | async-done | bytes 18874384 | tf_op jit(solution)/shard_map/all_gather | solution.py:132
  580.6 15.1 fusion.108
  603.4 10.3 reshape.748
  633.9 10.4 reshape.747
  644.3 9.1 copy.271
  653.4 10.3 reshape.649
  672.2 11.4 fusion.22
  771.9 157.5 %while.48 = (s32[]{:T(128)}, f32[384,12,64]{0,2,1:T(8,128)}, f32[3072,1536]{0,1:T(8,128)}, bf16[3072,768]{0,1:T(8,128)(2,1)}, s32[384]{0:T(512)S(1)}, /*index=5*...) while((s32[]{:T(128)}, f32[384,12,64]{0,2,1:T(8,128)}, ...), condition=%wide.region_26.27_spmd.clone, body=%wide.region_25.26_spmd.clone.sunk | while | flops 2296774656 | bytes 138907136 | solution.py:77
  915.4 9.0 fusion.209
  936.3 305.6 %reduce-scatter.6.cloned.1.call-done = f32[384,1536]{0,1:T(8,128)} async-done(((f32[3072,1536]{0,1:T(8,128)}), f32[384,1536]{0,1:T(8,128)}) %reduce-scatter.6.cloned.1.call-update) | async-done | bytes 2359312 | tf_op jit(solution)/shard_map/reduce_scatter | solution.py:386
  1249.8 9.1 reshape.659
  1276.5 10.2 fusion.73
  1286.7 14.1 copy.349
  1300.8 12.8 copy.295
  1313.7 10.5 fusion.43
  1324.2 12.5 copy.348
  1336.7 13.2 copy.292
  1358.0 12.2 copy.347
  1370.2 12.9 copy.290
  1383.1 25.8 pad_maximum_fusion
  1431.3 45.7 %all-reduce.1 = (f32[4,768]{1,0:T(4,128)}, f32[768,12]{0,1:T(8,128)}) all-reduce(f32[4,768]{1,0:T(4,128)} %pad_maximum_fusion.5, f32[768,12]{0,1:T(8,128)} %fusion.115), channel_id=1, replica_groups=mesh['ctx'=8,'fsdp'=4] {'ctx','fsdp'}, use_global_device_ids=true, to_apply=%region_31.32 | all-reduce | flops 12288 | bytes 98304 | tf_op jit(solution)/shard_map/psum | solution.py:407
  1491.2 1109.4 %all-reduce.5.cloned.1.call-done = (f32[36,128,128]{2,1,0:T(8,128)}, f32[2,288,128,128]{3,2,1,0:T(8,128)}) async-done(((f32[36,128,128]{2,1,0:T(8,128)}, f32[2,288,128,128]{3,2,1,0:T(8,128)}), (f32[36,128,128]{2,1,0:T(8,128)}, f32[2,288,128,128]{3,2,1,0:T(8,128)})) %all-reduce.5.cloned.1.call-update) | async-done | bytes 40108048 | tf_op jit(solution)/shard_map/psum | solution.py:401
  2600.6 9.7 add_multiply_fusion.1
  2632.3 14.9 fusion.39
  2647.3 9.9 fusion.38
  2665.4 11.6 bitcast_subtract_fusion
  (501 shorter events, 596.8 us)
Async XLA Ops:
  7.2 2608.4 %copy-start = (f32[36,128,128]{2,1,0:T(8,128)S(1)}, f32[36,128,128]{2,1,0:T(8,128)}, u32[]{:S(2)}) copy-start(f32[36,128,128]{2,1,0:T(8,128)} %param.37) | copy-start | bytes 7077892
  7.2 42.6 %all-gather.5.cloned.1.call-start = ((), (), s32[]{:S(2)}) async-start(), calls=%async_computation.6 | async-start | bytes 5898240 | tf_op jit(solution)/shard_map/all_gather | solution.py:129
  7.9 129.8 %all-gather.7.cloned.1.call-start = ((), (), s32[]{:S(2)}) async-start(), calls=%async_computation.7 | async-start | bytes 5308416 | tf_op jit(solution)/shard_map/all_gather | solution.py:155
  9.4 44.9 %copy-start.58 = (f32[768]{0:T(1024)}, f32[768]{0:T(1024)S(1)}, u32[]{:S(2)}) copy-start(f32[768]{0:T(1024)S(1)} %get-tuple-element.958) | copy-start | bytes 9220
  10.8 43.4 %copy-start.72 = (f32[384]{0:T(512)}, f32[384]{0:T(512)S(1)}, u32[]{:S(2)}) copy-start(f32[384]{0:T(512)S(1)} %add_rsqrt_fusion.1) | copy-start | bytes 4612
  57.7 160.9 %all-gather.9.cloned.1.call-start = ((), (), s32[]{:S(2)}) async-start(), calls=%async_computation.8 | async-start | bytes 5308416 | tf_op jit(solution)/shard_map/all_gather | solution.py:154
  58.4 522.2 %all-gather.11.cloned.1.call-start = ((), (), s32[]{:S(2)}) async-start(), calls=%async_computation.9 | async-start | bytes 21233664 | tf_op jit(solution)/shard_map/all_gather | solution.py:132
  144.3 80.8 %copy-start.33 = (f32[12,384]{1,0:T(8,128)S(1)}, f32[12,384]{1,0:T(8,128)}, u32[]{:S(2)}) copy-start(f32[12,384]{1,0:T(8,128)} %custom-call.4) | copy-start | bytes 55300
  144.3 80.8 %copy-start.42 = (f32[12,384]{1,0:T(8,128)S(1)}, f32[12,384]{1,0:T(8,128)}, u32[]{:S(2)}) copy-start(f32[12,384]{1,0:T(8,128)} %custom-call.5) | copy-start | bytes 55300
  144.3 80.8 %copy-start.45 = (s32[384]{0:T(512)S(1)}, s32[384]{0:T(512)}, u32[]{:S(2)}) copy-start(s32[384]{0:T(512)} %dynamic_slice.84) | copy-start | bytes 4612
  144.3 80.8 %copy-start.48 = (s32[384]{0:T(512)S(1)}, s32[384]{0:T(512)}, u32[]{:S(2)}) copy-start(s32[384]{0:T(512)} %dynamic_slice.83) | copy-start | bytes 4612
  355.6 17.1 copy-start.24
  368.3 245.5 %all-to-all-start = ((bf16[8,96,768]{2,1,0:T(8,128)(2,1)}), bf16[8,96,768]{2,1,0:T(8,128)(2,1)}, u32[]{:S(2)}, u32[]{:S(2)}) async-start(bf16[8,96,768]{2,1,0:T(8,128)(2,1)} %bitcast.443), calls=%async_computation | async-start | bytes 2359296 | tf_op jit(solution)/shard_map/all_to_all | solution.py:241
  380.3 215.4 %copy-start.74 = (f32[384]{0:T(512)}, f32[384]{0:T(512)S(1)}, u32[]{:S(2)}) copy-start(f32[384]{0:T(512)S(1)} %fusion.101) | copy-start | bytes 4612
  380.3 215.4 %copy-start.67 = (f32[384,2]{0,1:T(2,128)}, f32[384,2]{0,1:T(2,128)S(1)}, u32[]{:S(2)}) copy-start(f32[384,2]{0,1:T(2,128)S(1)} %fusion.100) | copy-start | bytes 9220
  613.7 58.5 %all-to-all-start.2 = ((bf16[8,96,768]{2,1,0:T(8,128)(2,1)}), bf16[8,96,768]{2,1,0:T(8,128)(2,1)S(1)}, u32[]{:S(2)}, u32[]{:S(2)}) async-start(bf16[8,96,768]{2,1,0:T(8,128)(2,1)} %bitcast.442), calls=%async_computation.2 | async-start | bytes 2359296 | tf_op jit(solution)/shard_map/all_to_all | solution.py:289
  697.3 19.4 all-to-all-start.3
  716.6 20.2 all-to-all-start.1
  720.9 521.0 %reduce-scatter.6.cloned.1.call-start = ((), (), s32[]{:S(2)}) async-start(), calls=%async_computation.10 | async-start | bytes 21233664 | tf_op jit(solution)/shard_map/reduce_scatter | solution.py:386
  929.4 479.5 %reduce-scatter.8.cloned.1.call-start = ((), (), s32[]{:S(2)}) async-start(), calls=%async_computation.11 | async-start | bytes 11796480 | tf_op jit(solution)/shard_map/reduce_scatter | solution.py:402
  936.3 308.4 %copy-start.16 = (f32[384,768]{1,0:T(8,128)S(1)}, f32[384,768]{1,0:T(8,128)}, u32[]{:S(2)}) copy-start(f32[384,768]{1,0:T(8,128)} %param.27) | copy-start | bytes 3538948
  936.3 308.4 %copy-start.59 = (f32[768]{0:T(1024)S(1)}, f32[768]{0:T(1024)}, u32[]{:S(2)}) copy-start(f32[768]{0:T(1024)} %copy-done.58) | copy-start | bytes 9220
  936.3 308.4 %copy-start.73 = (f32[384]{0:T(512)S(1)}, f32[384]{0:T(512)}, u32[]{:S(2)}) copy-start(f32[384]{0:T(512)} %copy-done.72) | copy-start | bytes 4612
  1275.3 1325.3 %all-reduce.5.cloned.1.call-start = ((), (), s32[]{:S(2)}) async-start(), calls=%async_computation.12 | async-start | bytes 80216064 | tf_op jit(solution)/shard_map/psum | solution.py:401
  1430.7 57.5 %copy-start.17 = (f32[384,768]{1,0:T(8,128)S(1)}, f32[384,768]{1,0:T(8,128)}, u32[]{:S(2)}) copy-start(f32[384,768]{1,0:T(8,128)} %param.27) | copy-start | bytes 3538948
  2629.4 17.8 slice-start.8
  2632.2 24.9 copy-start.3
  2632.2 24.9 slice-start.6
  2632.2 33.1 %slice-start.2 = ((s8[4718592]{0:T(1024)(128)(4,1)}), s8[4194304]{0:T(1024)(128)(4,1)S(1)}, s32[]{:S(2)}) async-start(s8[4718592]{0:T(1024)(128)(4,1)} %bitcast.425), calls=%async_computation.15 | async-start | bytes 8388608
  2632.3 33.1 %slice-start.10 = ((s8[4718592]{0:T(1024)(128)(4,1)}), s8[4194304]{0:T(1024)(128)(4,1)S(1)}, s32[]{:S(2)}) async-start(s8[4718592]{0:T(1024)(128)(4,1)} %bitcast.450), calls=%async_computation.23 | async-start | bytes 8388608
  2647.2 18.1 slice-start.3
  2647.2 18.1 slice-start.11
  (105 other events, 521.7 us)
Sparse Core Ops, SparseCore 0:
  9.6 40.1 all-gather.4
  57.8 79.8 all-gather.6
  140.5 78.0 all-gather.8
  219.9 360.5 all-gather.10
  929.5 312.3 reduce-scatter.5
  1275.4 77.4 reduce-scatter.7
  1409.0 1191.4 all-reduce.4
where the time goes:
time: 2700 us; the launch traced here: 2690 us
  waiting for transfers between devices  1780 us (66%)
  matrix products  366 us (14%)
  local copies, waits for them, and re-layouts  345 us (13%)
  other arithmetic  121 us (4%)
  blocking collectives  45.7 us (2%)
    psum x1, waiting for transfers between devices, body(): lax.psum(lax.psum_scatter(attn_local, 'fsdp', scatter_dimension=0, tiled=...  1110 us
    reduce_scatter x1, waiting for transfers between devices, body(): lax.psum_scatter(back_state[1], 'ctx', scatter_dimension=0, tiled=True)  306 us
    all_gather x1, waiting for transfers between devices, body(): expert_all = lax.all_gather(expert_weights, 'ctx', axis=1, tiled=True)  189 us
    unnamed x189, local copies, waits for them, and re-layouts  79.7 us
    all_gather x1, waiting for transfers between devices, body(): lax.all_gather(key_rows, 'ctx', axis=0, tiled=True)  74.2 us
  transfers between devices with their start and end apart: 11, of which 8 were waited for; matrix products, arithmetic and copies ran while one was open for 18% of the time, Pallas kernels for 0%

commit v1 on v0

v1 whole, which is shorter than its diff:
```python
import functools

import jax
import jax.numpy as jnp
from jax import lax
from jax.experimental import pallas as pl
from jax.experimental.pallas import tpu as pltpu
from jax.sharding import PartitionSpec as P

D = 768
HEADS = 12
HDIM = 64
EXPERTS = 8
ZEROS = 4
BS = 128
SLOTS = 4
HEAD_GROUPS = 4
GROUP_WIDTH = HEADS // HEAD_GROUPS * HDIM
GROUP_HEADS = HEADS // HEAD_GROUPS
CHUNK = 256
TILE = 256
SUB = 32

EPSILON = 1e-06
SCORE_SCALE = 0.125
STAT_DECAY = 0.5
RATE_PROJECT = 0.4
RATE_OUTPUT = 3.0
RATE_EXPERT = 0.4
RATE_ROUTER = 0.2
RATE_VECTOR = 0.1
MASKED_SCORE = -1e30
PRECISE = lax.Precision.HIGHEST
F32 = jnp.float32
LOW = jnp.bfloat16
VMEM_LIMIT = 56 * 1024 * 1024


def to_matrix(blocks, height, breadth):
    block_height = blocks.shape[1]
    block_breadth = blocks.shape[2]
    shaped = blocks.reshape(
        height // block_height, breadth // block_breadth, block_height, block_breadth
    )
    return shaped.transpose(0, 2, 1, 3).reshape(height, breadth)


def to_blocks(matrix, block_height, block_breadth):
    height = matrix.shape[0]
    breadth = matrix.shape[1]
    shaped = matrix.reshape(
        height // block_height, block_height, breadth // block_breadth, block_breadth
    )
    return shaped.transpose(0, 2, 1, 3).reshape(-1, block_height, block_breadth)


def normalize_parts(values, scaling):
    factor = lax.rsqrt(jnp.mean(values * values, axis=-1, keepdims=True) + EPSILON)
    return (values * factor * scaling, factor)


def normalize_back(values, factor, scaling, gradient):
    unit_rows = values * factor
    scaled = gradient * scaling
    value_grad = factor * (
        scaled - unit_rows * jnp.mean(scaled * unit_rows, axis=-1, keepdims=True)
    )
    return (value_grad, jnp.sum(gradient * unit_rows, axis=0))


def dot(left, right, left_dim=1, right_dim=0):
    return lax.dot_general(
        left, right, (((left_dim,), (right_dim,)), ((), ())), preferred_element_type=F32
    )


def vmem_spec():
    return pl.BlockSpec(memory_space=pltpu.VMEM)


def smem_spec():
    return pl.BlockSpec(memory_space=pltpu.SMEM)


def params():
    return pltpu.CompilerParams(vmem_limit_bytes=VMEM_LIMIT)


def project_kernel(rows_in, gain, places, shards):
    rows = rows_in.shape[0]
    owners = len(shards) - 1
    depth = D // owners
    breadth = 3 * D
    block_rows = depth // BS
    block_columns = breadth // BS
    pair = 2 * GROUP_WIDTH

    def kernel(places_ref, rows_ref, gain_ref, *refs):
        shard_refs = refs[: owners + 1]
        first_out, factor_out, query_out, pair_out, matrix, first_s = refs[owners + 1 :]
        for number, shard in enumerate(shard_refs):
            owner = places_ref[number]

            @pl.when(owner < owners)
            def _(owner=owner, shard=shard):
                for row in range(block_rows):
                    for column in range(block_columns):
                        matrix[
                            owner, row * BS : (row + 1) * BS, column * BS : (column + 1) * BS
                        ] = shard[row * block_columns + column]

        def norm(tile, carry):
            at = pl.ds(pl.multiple_of(tile * SUB, SUB), SUB)
            values = rows_ref[at, :]
            factor = lax.rsqrt(jnp.mean(values * values, axis=1, keepdims=True) + EPSILON)
            first = (values * factor * gain_ref[...]).astype(LOW)
            factor_out[at, :] = factor
            first_out[at, :] = first
            for owner in range(owners):
                first_s[owner, at, :] = first[:, owner * depth : (owner + 1) * depth]
            return carry

        lax.fori_loop(0, rows // SUB, norm, 0)
        for tile in range(breadth // pair):
            at = slice(tile * pair, (tile + 1) * pair)
            total = dot(first_s[0], matrix[0, :, at])
            for owner in range(1, owners):
                total = total + dot(first_s[owner], matrix[owner, :, at])
            total = total.astype(LOW)
            part = tile * pair // D
            group = tile * pair % D // GROUP_WIDTH
            for side in range(2):
                piece = total[:, side * GROUP_WIDTH : (side + 1) * GROUP_WIDTH]
                if part == 0:
                    query_out[group + side] = jnp.concatenate(
                        [piece[: rows // 2], piece[rows // 2 :]], axis=1
                    )
                else:
                    pair_out[
                        group + side, :, (part - 1) * GROUP_WIDTH : part * GROUP_WIDTH
                    ] = piece

    return pl.pallas_call(
        kernel,
        in_specs=[smem_spec()] + [vmem_spec()] * (owners + 3),
        out_specs=[vmem_spec()] * 5,
        out_shape=[
            jax.ShapeDtypeStruct((rows, D), LOW),
            jax.ShapeDtypeStruct((rows, 1), F32),
            jax.ShapeDtypeStruct((HEAD_GROUPS, rows // 2, pair), LOW),
            jax.ShapeDtypeStruct((HEAD_GROUPS, rows, pair), LOW),
            jax.ShapeDtypeStruct((owners, depth, breadth), LOW),
        ],
        scratch_shapes=[pltpu.VMEM((owners, rows, depth), LOW)],
        compiler_params=params(),
        cost_estimate=pl.CostEstimate(
            flops=2 * rows * D, bytes_accessed=1_000_000, transcendentals=0
        ),
        name="project",
    )(places, rows_in, gain, *shards)


def head_masks(value):
    lane = lax.broadcasted_iota(jnp.int32, (1, GROUP_WIDTH), 1)
    return [
        jnp.where(lane // HDIM == head, value, 0.0).astype(F32) for head in range(GROUP_HEADS)
    ]


def stack_heads(rows, masks):
    return jnp.concatenate([rows * mask.astype(rows.dtype) for mask in masks], axis=0)


def packed_at(slot, block_rows):
    first_row = slot % 2 * block_rows
    first_lane = slot // 2 * GROUP_WIDTH
    return slice(first_row, first_row + block_rows), slice(first_lane, first_lane + GROUP_WIDTH)


def pack_rows(values):
    groups, rows, width = values.shape
    return values.reshape(groups, 2, rows // 2, width).transpose(0, 2, 1, 3).reshape(
        groups, rows // 2, 2 * width
    )


def unpack_rows(values):
    groups, rows, width = values.shape
    return values.reshape(groups, rows, 2, width // 2).transpose(0, 2, 1, 3).reshape(
        groups, 2 * rows, width // 2
    )


def fill_sorted(kpb, sources, key_sorted, value_sorted, block_rows, block_count):
    key_sorted[0:CHUNK, :] = jnp.zeros((CHUNK, GROUP_WIDTH), LOW)
    value_sorted[0:CHUNK, :] = jnp.zeros((CHUNK, GROUP_WIDTH), LOW)
    for number, source in enumerate(sources):

        def fill(item, carry, source=source, number=number):
            from_row = pl.multiple_of(item % SLOTS * block_rows, block_rows)
            to_row = pl.multiple_of(CHUNK + kpb[number, item] * block_rows, 32)
            rows = source[item // SLOTS, pl.ds(from_row, block_rows), :]
            key_sorted[pl.ds(to_row, block_rows), :] = rows[:, 0:GROUP_WIDTH]
            value_sorted[pl.ds(to_row, block_rows), :] = rows[:, GROUP_WIDTH:]
            return carry

        lax.fori_loop(0, block_count, fill, 0)


def list_steps(kpb, ends, sequences, block_rows, block_count, block_of, place_of):
    def one_block(item, first_step):
        first = kpb[0, item] * block_rows
        lowest = jnp.int32(0)
        for sequence in range(sequences):
            ending = ends[sequence]
            lowest = jnp.where(first >= ending, ending, lowest)
        top = first + block_rows
        count = (top - lowest + CHUNK - 1) // CHUNK

        def one_step(step, carry):
            block_of[first_step + step] = item
            place_of[first_step + step] = top - (step + 1) * CHUNK
            return carry

        lax.fori_loop(0, count, one_step, 0)
        return first_step + count

    return lax.fori_loop(0, block_count, one_block, jnp.int32(0))


def fill_limits(kpb, ends, sequences, block_rows, item, start_s, place_s):
    for tile in range(GROUP_HEADS * block_rows // SUB):
        within = tile * SUB % block_rows
        places = (
            kpb[0, item] * block_rows
            + within
            + lax.broadcasted_iota(jnp.int32, (SUB, BS), 0)
        )
        starts = jnp.zeros_like(places)
        for sequence in range(sequences):
            ending = ends[sequence]
            starts = jnp.where(places >= ending, ending, starts)
        at_rows = slice(tile * SUB, (tile + 1) * SUB)
        start_s[item, at_rows, :] = starts
        place_s[item, at_rows, :] = places


def pipeline(total, scores, middle, products):
    scores(jnp.int32(0), 0)

    def pair(number, carry):
        step = 2 * number
        scores(step + 1, 1)
        middle(step, 0)
        products(step - 1, 1)
        scores(step + 2, 0)
        middle(step + 1, 1)
        products(step, 0)
        return carry

    lax.fori_loop(0, (total + 2) // 2, pair, 0)


def tile_slices(count):
    return [slice(tile * SUB, (tile + 1) * SUB) for tile in range(count)]


def attend_kernel(sources_count, block_rows, sequences, *refs):
    kpb, ends, queries = refs[:3]
    sources = refs[3 : 3 + sources_count]
    raw_out, low_out, lse_out, key_sorted, value_sorted, query_s, start_s, place_s = refs[
        3 + sources_count : 11 + sources_count
    ]
    best_s, total_s, gathered_s, score_0, score_1, weight_0, weight_1, fade_0, fade_1 = refs[
        11 + sources_count : 20 + sources_count
    ]
    block_of, place_of = refs[20 + sources_count :]
    score_s, weight_s, fade_s = (score_0, score_1), (weight_0, weight_1), (fade_0, fade_1)
    block_count = queries.shape[0] * SLOTS
    stacked = GROUP_HEADS * block_rows
    tiles = tile_slices(stacked // SUB)
    fill_sorted(kpb, sources, key_sorted, value_sorted, block_rows, block_count)
    total = list_steps(kpb, ends, sequences, block_rows, block_count, block_of, place_of)
    masks = head_masks(SCORE_SCALE)
    plain = head_masks(1.0)

    def load(group, carry):
        for slot in range(SLOTS):
            rows, lanes = packed_at(slot, block_rows)
            query_s[group * SLOTS + slot] = stack_heads(queries[group, rows, lanes], masks)
        return carry

    lax.fori_loop(0, block_count // SLOTS, load, 0)

    def prepare(item, carry):
        fill_limits(kpb, ends, sequences, block_rows, item, start_s, place_s)
        best_s[item] = jnp.full((stacked, BS), MASKED_SCORE, F32)
        total_s[item] = jnp.zeros((stacked, BS), F32)
        gathered_s[item] = jnp.zeros((stacked, GROUP_WIDTH), F32)
        return carry

    lax.fori_loop(0, block_count, prepare, 0)
    weight_1[...] = jnp.zeros_like(weight_1)
    fade_1[...] = jnp.ones_like(fade_1)

    def find(step):
        inside = jnp.clip(step, 0, total - 1)
        return block_of[inside], place_of[inside]

    def scores(step, side):
        item, low_place = find(step)
        at = pl.multiple_of(low_place + CHUNK, 32)
        score_s[side][...] = dot(query_s[item], key_sorted[pl.ds(at, CHUNK), :], 1, 1)

    def middle(step, side):
        item, low_place = find(step)
        low_place = jnp.where(step < total, low_place, -(1 << 24))
        lanes = low_place + lax.broadcasted_iota(jnp.int32, (1, BS), 1)
        for rows in tiles:
            starts, places = start_s[item, rows, :], place_s[item, rows, :]
            parts = []
            for part in range(CHUNK // BS):
                key_places = lanes + part * BS
                allowed = (key_places >= starts) & (key_places <= places)
                found = score_s[side][rows, part * BS : (part + 1) * BS]
                parts.append(jnp.where(allowed, found, MASKED_SCORE))
            best = best_s[item, rows, :]
            top = jnp.max(functools.reduce(jnp.maximum, parts), axis=1, keepdims=True)
            peak = jnp.maximum(best, top)
            fade = jnp.exp(best - peak)
            so_far = total_s[item, rows, :] * fade
            for part, found in enumerate(parts):
                weights = jnp.exp(found - peak)
                so_far = so_far + weights
                weight_s[side][rows, part * BS : (part + 1) * BS] = weights.astype(LOW)
            best_s[item, rows, :] = peak
            total_s[item, rows, :] = so_far
            fade_s[side][rows, :] = fade

    def products(step, side):
        item, low_place = find(step)
        at = pl.multiple_of(low_place + CHUNK, 32)
        fade = fade_s[side][...]
        fade = jnp.concatenate([fade, fade[:, : GROUP_WIDTH - BS]], axis=1)
        gathered_s[item] = gathered_s[item] * fade + dot(
            weight_s[side][...], value_sorted[pl.ds(at, CHUNK), :]
        )

    pipeline(total, scores, middle, products)

    def finish(group, carry):
        for slot in range(SLOTS):
            item = group * SLOTS + slot
            rows, lanes = packed_at(slot, block_rows)
            sums = jnp.sum(total_s[item], axis=1, keepdims=True)
            gathered = gathered_s[item] / sums
            result = jnp.zeros((block_rows, GROUP_WIDTH), F32)
            for head in range(GROUP_HEADS):
                result = result + (
                    plain[head] * gathered[head * block_rows : (head + 1) * block_rows]
                )
            raw_out[group, slot * block_rows : (slot + 1) * block_rows, :] = result
            low_out[group, rows, lanes] = result.astype(LOW)
            lse_out[item] = best_s[item][:, 0:1] + jnp.log(sums)
        return carry

    lax.fori_loop(0, block_count // SLOTS, finish, 0)


def attend_sizes(queries, pairs):
    groups, rows, _ = pairs[0].shape
    block_rows = rows // SLOTS
    all_rows = groups * rows * len(pairs)
    blocks = groups * SLOTS
    stacked = GROUP_HEADS * block_rows
    return groups, rows, block_rows, all_rows, blocks, stacked


def attend(kpb, ends, queries, pairs):
    groups, rows, block_rows, all_rows, blocks, stacked = attend_sizes(queries, pairs)
    steps = blocks * (all_rows // CHUNK + 1)
    return pl.pallas_call(
        functools.partial(attend_kernel, len(pairs), block_rows, ends.shape[0]),
        in_specs=[smem_spec()] * 2 + [vmem_spec()] * (1 + len(pairs)),
        out_specs=[vmem_spec()] * 3,
        out_shape=[
            jax.ShapeDtypeStruct((groups, rows, GROUP_WIDTH), F32),
            jax.ShapeDtypeStruct((groups, rows // 2, 2 * GROUP_WIDTH), LOW),
            jax.ShapeDtypeStruct((blocks, stacked, 1), F32),
        ],
        scratch_shapes=[
            pltpu.VMEM((CHUNK + all_rows, GROUP_WIDTH), LOW),
            pltpu.VMEM((CHUNK + all_rows, GROUP_WIDTH), LOW),
            pltpu.VMEM((blocks, stacked, GROUP_WIDTH), LOW),
            pltpu.VMEM((blocks, stacked, BS), jnp.int32),
            pltpu.VMEM((blocks, stacked, BS), jnp.int32),
            pltpu.VMEM((blocks, stacked, BS), F32),
            pltpu.VMEM((blocks, stacked, BS), F32),
            pltpu.VMEM((blocks, stacked, GROUP_WIDTH), F32),
            pltpu.VMEM((stacked, CHUNK), F32),
            pltpu.VMEM((stacked, CHUNK), F32),
            pltpu.VMEM((stacked, CHUNK), LOW),
            pltpu.VMEM((stacked, CHUNK), LOW),
            pltpu.VMEM((stacked, BS), F32),
            pltpu.VMEM((stacked, BS), F32),
            pltpu.SMEM((steps,), jnp.int32),
            pltpu.SMEM((steps,), jnp.int32),
        ],
        compiler_params=params(),
        cost_estimate=pl.CostEstimate(
            flops=groups * rows * HDIM,
            bytes_accessed=1_000_000,
            transcendentals=0,
        ),
        name="attend_forward",
    )(kpb, ends, queries, *pairs)


def attend_back_kernel(sources_count, block_rows, sequences, *refs):
    kpb, ends, queries = refs[:3]
    sources = refs[3 : 3 + sources_count]
    out_grad, raw, lse = refs[3 + sources_count : 6 + sources_count]
    query_out = refs[6 + sources_count]
    pair_outs = refs[7 + sources_count : 7 + 2 * sources_count]
    rest = refs[7 + 2 * sources_count :]
    key_sorted, value_sorted, key_grad, value_grad, query_s, grad_s, query_grad = rest[:7]
    start_s, place_s, shift_s, delta_s = rest[7:11]
    score_s, back_s, weight_s, change_s = rest[11:13], rest[13:15], rest[15:17], rest[17:19]
    block_of, place_of = rest[19:]
    block_count = queries.shape[0] * SLOTS
    stacked = GROUP_HEADS * block_rows
    tiles = tile_slices(stacked // SUB)
    fill_sorted(kpb, sources, key_sorted, value_sorted, block_rows, block_count)
    total = list_steps(kpb, ends, sequences, block_rows, block_count, block_of, place_of)
    key_grad[...] = jnp.zeros_like(key_grad)
    value_grad[...] = jnp.zeros_like(value_grad)
    weight_s[1][...] = jnp.zeros_like(weight_s[1])
    change_s[1][...] = jnp.zeros_like(change_s[1])
    masks = head_masks(SCORE_SCALE)
    plain = head_masks(1.0)

    def load(group, carry):
        for slot in range(SLOTS):
            item = group * SLOTS + slot
            rows, lanes = packed_at(slot, block_rows)
            query_s[item] = stack_heads(queries[group, rows, lanes], masks)
            grad = stack_heads(out_grad[group, rows, lanes], plain)
            grad_s[item] = grad
            values = raw[group, slot * block_rows : (slot + 1) * block_rows, :]
            delta = jnp.sum(
                grad.astype(F32) * jnp.concatenate([values] * GROUP_HEADS, axis=0),
                axis=1,
                keepdims=True,
            )
            delta_s[item] = jnp.broadcast_to(delta, (stacked, BS))
        return carry

    lax.fori_loop(0, block_count // SLOTS, load, 0)

    def prepare(item, carry):
        shift_s[item] = jnp.broadcast_to(lse[item], (stacked, BS))
        query_grad[item] = jnp.zeros((stacked, GROUP_WIDTH), F32)
        fill_limits(kpb, ends, sequences, block_rows, item, start_s, place_s)
        return carry

    lax.fori_loop(0, block_count, prepare, 0)

    def find(step):
        inside = jnp.clip(step, 0, total - 1)
        return block_of[inside], place_of[inside]

    def scores(step, side):
        item, low_place = find(step)
        at = pl.ds(pl.multiple_of(low_place + CHUNK, 32), CHUNK)
        score_s[side][...] = dot(query_s[item], key_sorted[at, :], 1, 1)
        back_s[side][...] = dot(grad_s[item], value_sorted[at, :], 1, 1)

    def middle(step, side):
        item, low_place = find(step)
        low_place = jnp.where(step < total, low_place, -(1 << 24))
        lanes = low_place + lax.broadcasted_iota(jnp.int32, (1, BS), 1)
        for rows in tiles:
            starts, places = start_s[item, rows, :], place_s[item, rows, :]
            shift, delta = shift_s[item, rows, :], delta_s[item, rows, :]
            for part in range(CHUNK // BS):
                at_lanes = slice(part * BS, (part + 1) * BS)
                key_places = lanes + part * BS
                allowed = (key_places >= starts) & (key_places <= places)
                found = score_s[side][rows, at_lanes] - shift
                weights = jnp.exp(jnp.where(allowed, found, MASKED_SCORE))
                weight_s[side][rows, at_lanes] = weights.astype(LOW)
                change = weights * (back_s[side][rows, at_lanes] - delta)
                change_s[side][rows, at_lanes] = change.astype(LOW)

    def products(step, side):
        item, low_place = find(step)
        at = pl.ds(pl.multiple_of(low_place + CHUNK, 32), CHUNK)
        value_grad[at, :] += dot(weight_s[side][...], grad_s[item], 0, 0)
        key_grad[at, :] += dot(change_s[side][...], query_s[item], 0, 0)
        query_grad[item] += dot(change_s[side][...], key_sorted[at, :])

    pipeline(total, scores, middle, products)

    def finish(item, carry):
        at = pl.ds(pl.multiple_of(item % SLOTS * block_rows, block_rows), block_rows)
        result = jnp.zeros((block_rows, GROUP_WIDTH), F32)
        for head in range(GROUP_HEADS):
            result = result + masks[head] * (
                query_grad[item, head * block_rows : (head + 1) * block_rows, :]
            )
        query_out[item // SLOTS, at, :] = result.astype(LOW)
        return carry

    lax.fori_loop(0, block_count, finish, 0)
    for number, target in enumerate(pair_outs):

        def drain(item, carry, number=number, target=target):
            to_row = pl.multiple_of(item % SLOTS * block_rows, block_rows)
            from_row = pl.multiple_of(CHUNK + kpb[number, item] * block_rows, 32)
            pair = jnp.concatenate(
                [
                    key_grad[pl.ds(from_row, block_rows), :],
                    value_grad[pl.ds(from_row, block_rows), :],
                ],
                axis=1,
            )
            target[item // SLOTS, pl.ds(to_row, block_rows), :] = pair.astype(target.dtype)
            return carry

        lax.fori_loop(0, block_count, drain, 0)


def attend_back(kpb, ends, queries, pairs, out_grad, raw, lse):
    groups, rows, block_rows, all_rows, blocks, stacked = attend_sizes(queries, pairs)
    steps = blocks * (all_rows // CHUNK + 1)
    limit = pltpu.VMEM((blocks, stacked, BS), jnp.int32)
    row_values = pltpu.VMEM((blocks, stacked, BS), F32)
    sorted_low = pltpu.VMEM((CHUNK + all_rows, GROUP_WIDTH), LOW)
    sorted_sum = pltpu.VMEM((CHUNK + all_rows, GROUP_WIDTH), F32)
    stacked_low = pltpu.VMEM((blocks, stacked, GROUP_WIDTH), LOW)
    square = pltpu.VMEM((stacked, CHUNK), F32)
    square_low = pltpu.VMEM((stacked, CHUNK), LOW)
    return pl.pallas_call(
        functools.partial(attend_back_kernel, len(pairs), block_rows, ends.shape[0]),
        in_specs=[smem_spec()] * 2 + [vmem_spec()] * (4 + len(pairs)),
        out_specs=[vmem_spec()] * (1 + len(pairs)),
        out_shape=[
            jax.ShapeDtypeStruct((groups, rows, GROUP_WIDTH), LOW),
            jax.ShapeDtypeStruct((groups, rows, 2 * GROUP_WIDTH), F32),
        ]
        + [jax.ShapeDtypeStruct((groups, rows, 2 * GROUP_WIDTH), LOW) for _ in pairs[1:]],
        scratch_shapes=[sorted_low] * 2
        + [sorted_sum] * 2
        + [stacked_low] * 2
        + [pltpu.VMEM((blocks, stacked, GROUP_WIDTH), F32)]
        + [limit] * 2
        + [row_values] * 2
        + [square] * 4
        + [square_low] * 4
        + [pltpu.SMEM((steps,), jnp.int32)] * 2,
        compiler_params=params(),
        cost_estimate=pl.CostEstimate(
            flops=groups * rows * HDIM,
            bytes_accessed=1_000_000,
            transcendentals=0,
        ),
        name="attend_backward",
    )(kpb, ends, queries, *pairs, out_grad, raw, lse)


def side_blocks():
    return D // BS


def bring(places, sources, held, done):
    copies = []
    for number, source in enumerate(sources):
        size = source.shape[0]
        target = held.at[pl.ds(places[number] * size, size)]
        copies.append(pltpu.make_async_copy(source, target, done.at[number]))
    for copy in copies:
        copy.start()
    for copy in copies:
        copy.wait()


def wide_tile(held, first, hidden_blocks, step):
    rows = []
    for row in range(side_blocks()):
        at = first + row * hidden_blocks + 2 * step
        rows.append(jnp.concatenate([held[at], held[at + 1]], axis=1))
    return jnp.concatenate(rows, axis=0)


def tall_tile(held, first, step):
    side = side_blocks()
    rows = []
    for half in range(2):
        at = first + (2 * step + half) * side
        rows.append(jnp.concatenate([held[at + column] for column in range(side)], axis=1))
    return jnp.concatenate(rows, axis=0)


def expert_sizes(weights):
    total = sum(array.shape[0] for array in weights[1])
    return total, total // (3 * side_blocks())


def expert_forward(rows_in, weights):
    rows = rows_in.shape[0]
    places, sources = weights
    count = len(sources)
    total_blocks, hidden_blocks = expert_sizes(weights)
    up_first = side_blocks() * hidden_blocks

    def kernel(places_ref, rows_ref, *refs):
        source_refs = refs[:count]
        result, gate_o, up_o, inner_o, total, held, done = refs[count:]
        step = pl.program_id(0)

        @pl.when(step == 0)
        def _():
            bring(places_ref, source_refs, held, done)
            total[...] = jnp.zeros_like(total)

        gate_tile = wide_tile(held, 0, hidden_blocks, step)
        up_tile = wide_tile(held, up_first, hidden_blocks, step)
        down_tile = tall_tile(held, 2 * up_first, step)

        for number in range(rows // TILE):
            first = number * TILE
            at = pl.ds(first, TILE)
            entering = rows_ref[at, :]
            gate_o[at, :] = dot(entering, gate_tile)
            up_o[at, :] = dot(entering, up_tile)
            for sub in range(TILE // SUB):
                now = pl.ds(first + sub * SUB, SUB)
                gate = gate_o[now, :]
                inner_o[now, :] = (gate * jax.nn.sigmoid(gate) * up_o[now, :]).astype(LOW)
            total[at, :] += dot(inner_o[at, :], down_tile)

        @pl.when(step == pl.num_programs(0) - 1)
        def _():
            result[...] = total[...].astype(LOW)

    fixed = pl.BlockSpec((rows, D), lambda step: (0, 0))
    hidden = pl.BlockSpec((rows, TILE), lambda step: (0, step))
    hidden_size = (rows, hidden_blocks * BS)
    return pl.pallas_call(
        kernel,
        grid=(hidden_blocks // 2,),
        in_specs=[smem_spec(), fixed] + [pl.BlockSpec(memory_space=pl.ANY)] * count,
        out_specs=[fixed] + [hidden] * 3,
        out_shape=[
            jax.ShapeDtypeStruct((rows, D), LOW),
            jax.ShapeDtypeStruct(hidden_size, F32),
            jax.ShapeDtypeStruct(hidden_size, F32),
            jax.ShapeDtypeStruct(hidden_size, LOW),
        ],
        scratch_shapes=[
            pltpu.VMEM((rows, D), F32),
            pltpu.VMEM((total_blocks, BS, BS), LOW),
            pltpu.SemaphoreType.DMA((count,)),
        ],
        compiler_params=params(),
        cost_estimate=pl.CostEstimate(
            flops=6 * rows * D * hidden_blocks * BS,
            bytes_accessed=6 * D * hidden_blocks * BS + 4 * rows * D,
            transcendentals=0,
        ),
        name="expert_forward",
    )(places, rows_in, *sources)


def expert_row_grads(grads_in, gate_in, up_in, weights):
    rows = grads_in.shape[0]
    places, sources = weights
    count = len(sources)
    total_blocks, hidden_blocks = expert_sizes(weights)
    up_first = side_blocks() * hidden_blocks

    def kernel(places_ref, grads_ref, gate_i, up_i, *refs):
        source_refs = refs[:count]
        back, gate_s, up_s, total, inner_grad_s, held, done = refs[count:]
        step = pl.program_id(0)

        @pl.when(step == 0)
        def _():
            bring(places_ref, source_refs, held, done)
            total[...] = jnp.zeros_like(total)

        gate_tile = wide_tile(held, 0, hidden_blocks, step)
        up_tile = wide_tile(held, up_first, hidden_blocks, step)
        down_tile = tall_tile(held, 2 * up_first, step)

        for number in range(rows // TILE):
            first = number * TILE
            at = pl.ds(first, TILE)
            inner_grad_s[at, :] = dot(grads_ref[at, :], down_tile, 1, 1)
            for sub in range(TILE // SUB):
                now = pl.ds(first + sub * SUB, SUB)
                gate = gate_i[now, :]
                inner_grad = inner_grad_s[now, :]
                sigmoid = jax.nn.sigmoid(gate)
                up_s[now, :] = (inner_grad * (gate * sigmoid)).astype(LOW)
                gate_s[now, :] = (
                    inner_grad * up_i[now, :] * (sigmoid * (1.0 + gate * (1.0 - sigmoid)))
                ).astype(LOW)
            total[at, :] += dot(gate_s[at, :], gate_tile, 1, 1) + dot(
                up_s[at, :], up_tile, 1, 1
            )

        @pl.when(step == pl.num_programs(0) - 1)
        def _():
            back[...] = total[...].astype(LOW)

    fixed = pl.BlockSpec((rows, D), lambda step: (0, 0))
    hidden = pl.BlockSpec((rows, TILE), lambda step: (0, step))
    hidden_shape = jax.ShapeDtypeStruct((rows, hidden_blocks * BS), LOW)
    return pl.pallas_call(
        kernel,
        grid=(hidden_blocks // 2,),
        in_specs=[smem_spec(), fixed, hidden, hidden]
        + [pl.BlockSpec(memory_space=pl.ANY)] * count,
        out_specs=[fixed] + [hidden] * 2,
        out_shape=[jax.ShapeDtypeStruct((rows, D), LOW)] + [hidden_shape] * 2,
        scratch_shapes=[
            pltpu.VMEM((rows, D), F32),
            pltpu.VMEM((rows, TILE), F32),
            pltpu.VMEM((total_blocks, BS, BS), LOW),
            pltpu.SemaphoreType.DMA((count,)),
        ],
        compiler_params=params(),
        cost_estimate=pl.CostEstimate(
            flops=6 * rows * D * hidden_blocks * BS,
            bytes_accessed=12 * D * hidden_blocks * BS + 6 * rows * D,
            transcendentals=0,
        ),
        name="expert_row_grads",
    )(places, grads_in, gate_in, up_in, *sources)


def expert_weight_grads(places, rows_in, grads_in, gate_grads, up_grads, inner, sizes):
    rows = rows_in.shape[0]
    hidden_blocks = gate_grads.shape[1] // BS
    side = side_blocks()
    total_blocks = 3 * side * hidden_blocks
    count = len(sizes)
    pieces = sum(len(group) for group in sizes)

    def kernel(places_ref, rows_ref, grads_ref, gate_s, up_s, inner_s, *refs):
        outs = refs[:count]
        turned, held, done = refs[count:]
        step = pl.program_id(0)

        @pl.when(step == 0)
        def _():
            turned[...] = rows_ref[...].T

        def wide_out(source, first):
            product = dot(turned[...], source[...]).astype(LOW)
            for row in range(side):
                for column in range(2):
                    held[first + row * hidden_blocks + 2 * step + column] = product[
                        row * BS : (row + 1) * BS, column * BS : (column + 1) * BS
                    ]

        wide_out(gate_s, 0)
        wide_out(up_s, side * hidden_blocks)
        product = dot(inner_s[...], grads_ref[...], 0, 0).astype(LOW)
        for half in range(2):
            for column in range(side):
                held[2 * side * hidden_blocks + (2 * step + half) * side + column] = product[
                    half * BS : (half + 1) * BS, column * BS : (column + 1) * BS
                ]

        @pl.when(step == pl.num_programs(0) - 1)
        def _():
            copies = []
            for target, group in zip(outs, sizes):
                first = 0
                for size in group:
                    number = len(copies)
                    source = held.at[pl.ds(places_ref[number] * size, size)]
                    into = target.at[pl.ds(first, size)]
                    copies.append(pltpu.make_async_copy(source, into, done.at[number]))
                    first += size
            for copy in copies:
                copy.start()
            for copy in copies:
                copy.wait()

    fixed = pl.BlockSpec((rows, D), lambda step: (0, 0))
    hidden = pl.BlockSpec((rows, TILE), lambda step: (0, step))
    return pl.pallas_call(
        kernel,
        grid=(hidden_blocks // 2,),
        in_specs=[smem_spec(), fixed, fixed] + [hidden] * 3,
        out_specs=[pl.BlockSpec(memory_space=pl.ANY)] * count,
        out_shape=[jax.ShapeDtypeStruct((sum(group), BS, BS), LOW) for group in sizes],
        scratch_shapes=[
            pltpu.VMEM((D, rows), LOW),
            pltpu.VMEM((total_blocks, BS, BS), LOW),
            pltpu.SemaphoreType.DMA((pieces,)),
        ],
        compiler_params=params(),
        cost_estimate=pl.CostEstimate(
            flops=6 * rows * D * hidden_blocks * BS,
            bytes_accessed=12 * D * hidden_blocks * BS + 6 * rows * D,
            transcendentals=0,
        ),
        name="expert_weight_grads",
    )(places, rows_in, grads_in, gate_grads, up_grads, inner)


def expert_half_grads(which, places, rows_in, grads_in, gate_grads, up_grads, inner, sizes):
    rows = rows_in.shape[0]
    hidden_blocks = gate_grads.shape[1] // BS
    side = side_blocks()
    middle_row = side // 2
    total_blocks = 3 * side * hidden_blocks // 2
    count = len(sizes)
    pieces = sum(len(group) for group in sizes)

    def kernel(which_ref, places_ref, rows_ref, grads_ref, gate_s, up_s, inner_s, *refs):
        outs = refs[:count]
        turned, held, done = refs[count:]
        step = pl.program_id(0)

        @pl.when(step == 0)
        def _():
            turned[...] = rows_ref[...].T

        def wide_out(source, first_row, last_row, first):
            product = dot(turned[first_row * BS : last_row * BS, :], source[...]).astype(LOW)
            for row in range(last_row - first_row):
                for column in range(2):
                    held[first + row * hidden_blocks + 2 * step + column] = product[
                        row * BS : (row + 1) * BS, column * BS : (column + 1) * BS
                    ]

        @pl.when(which_ref[0] == 0)
        def _():
            wide_out(gate_s, 0, side, 0)
            wide_out(up_s, 0, middle_row, side * hidden_blocks)

        @pl.when(which_ref[0] == 1)
        def _():
            wide_out(up_s, middle_row, side, 0)
            product = dot(inner_s[...], grads_ref[...], 0, 0).astype(LOW)
            for half in range(2):
                for column in range(side):
                    held[middle_row * hidden_blocks + (2 * step + half) * side + column] = product[
                        half * BS : (half + 1) * BS, column * BS : (column + 1) * BS
                    ]

        @pl.when(step == pl.num_programs(0) - 1)
        def _():
            copies = []
            for target, group in zip(outs, sizes):
                first = 0
                for size in group:
                    number = len(copies)
                    source = held.at[pl.ds(places_ref[number] * size, size)]
                    into = target.at[pl.ds(first, size)]
                    copies.append(pltpu.make_async_copy(source, into, done.at[number]))
                    first += size
            for copy in copies:
                copy.start()
            for copy in copies:
                copy.wait()

    fixed = pl.BlockSpec((rows, D), lambda step: (0, 0))
    hidden = pl.BlockSpec((rows, TILE), lambda step: (0, step))
    return pl.pallas_call(
        kernel,
        grid=(hidden_blocks // 2,),
        in_specs=[smem_spec(), smem_spec(), fixed, fixed] + [hidden] * 3,
        out_specs=[pl.BlockSpec(memory_space=pl.ANY)] * count,
        out_shape=[jax.ShapeDtypeStruct((sum(group), BS, BS), LOW) for group in sizes],
        scratch_shapes=[
            pltpu.VMEM((D, rows), LOW),
            pltpu.VMEM((total_blocks, BS, BS), LOW),
            pltpu.SemaphoreType.DMA((pieces,)),
        ],
        compiler_params=params(),
        cost_estimate=pl.CostEstimate(
            flops=3 * rows * D * hidden_blocks * BS,
            bytes_accessed=6 * D * hidden_blocks * BS + 6 * rows * D,
            transcendentals=0,
        ),
        name="expert_half_grads",
    )(which, places, rows_in, grads_in, gate_grads, up_grads, inner)


def split_low(values):
    high = values.astype(LOW)
    return high, (values - high.astype(F32)).astype(LOW)


def renew(gradient, weights, left, right, left_root, right_root, rate):
    short = gradient.astype(LOW)
    left_new = STAT_DECAY * left + (1.0 - STAT_DECAY) * dot(short, short, 1, 1)
    right_new = STAT_DECAY * right + (1.0 - STAT_DECAY) * dot(short, short, 0, 0)
    high, rest = split_low(right_root)
    turned = (dot(short, high) + dot(short, rest)).astype(LOW)
    high, rest = split_low(left_root)
    direction = dot(high, turned) + dot(rest, turned)
    return (gradient, left_new, right_new, weights.astype(F32) - rate * direction)


def block_width(count):
    return 4 if count % 4 == 0 else 3 if count % 3 == 0 else 1


def shampoo_half(half, gradients, stats, filled):
    parts = len(gradients)
    count = gradients[0].shape[0]
    width = block_width(count)
    steps = count // width
    spec = pl.BlockSpec((width, BS, BS), lambda step, half: (half[0] * steps + step, 0, 0))
    grad_spec = pl.BlockSpec((width, BS, BS), lambda step, half: (step, 0, 0))

    def kernel(half_ref, *refs):
        for number in range(width):
            total = refs[0][number].astype(F32)
            for ref in refs[1:parts]:
                total = total + ref[number].astype(F32)
            now = [ref[number] for ref in refs[parts : parts + 5]]
            results = renew(total, *now, RATE_EXPERT)
            for target, result in zip(refs[-4:], results):
                target[number] = result

    shape = jax.ShapeDtypeStruct(stats[0].shape, F32)
    extra = list(filled or ())
    return pl.pallas_call(
        kernel,
        grid_spec=pltpu.PrefetchScalarGridSpec(
            num_scalar_prefetch=1,
            grid=(steps,),
            in_specs=[grad_spec] * parts
            + [spec] * 5
            + [pl.BlockSpec(memory_space=pl.ANY)] * len(extra),
            out_specs=[spec] * 4,
        ),
        out_shape=[shape] * 4,
        input_output_aliases={6 + parts + number: number for number in range(len(extra))},
        compiler_params=params(),
        cost_estimate=pl.CostEstimate(
            flops=count * 24 * BS * BS * BS,
            bytes_accessed=count * BS * BS * (34 + 2 * parts),
            transcendentals=0,
        ),
        name="shampoo_half",
    )(half, *gradients, *stats, *extra)


def shampoo(rates, gradient, stats):
    count = gradient.shape[0]
    width = block_width(count)
    spec = pl.BlockSpec((width, BS, BS), lambda step: (step, 0, 0))
    shape = jax.ShapeDtypeStruct((count, BS, BS), F32)

    def kernel(rates_ref, *refs):
        step = pl.program_id(0)
        for number in range(width):
            gradient_now, *stats_now = [ref[number] for ref in refs[:6]]
            results = renew(
                gradient_now.astype(F32), *stats_now, rates_ref[step * width + number]
            )
            for target, result in zip(refs[6:], results):
                target[number] = result

    return pl.pallas_call(
        kernel,
        grid=(count // width,),
        in_specs=[smem_spec()] + [spec] * 6,
        out_specs=[spec] * 4,
        out_shape=[shape] * 4,
        compiler_params=params(),
        cost_estimate=pl.CostEstimate(
            flops=count * 24 * BS * BS * BS,
            bytes_accessed=count * BS * BS * 38,
            transcendentals=0,
        ),
        name="shampoo_blocks",
    )(rates, gradient, *stats)


def shampoo_panel(turn, places, panels, stats):
    groups = len(panels)
    panel_rows = panels[0].shape[0]
    parts = 3
    breadth = groups * GROUP_WIDTH
    count = stats[0].shape[0]
    width = block_width(count)
    spec = pl.BlockSpec((width, BS, BS), lambda step, turn, places: (step, 0, 0))
    fixed = pl.BlockSpec(panels[0].shape, lambda step, turn, places: (0, 0))
    shape = jax.ShapeDtypeStruct((count, BS, BS), F32)
    per_part = breadth // BS
    per_row = parts * per_part
    side = D // BS

    def kernel(turn_ref, places_ref, *refs):
        step = pl.program_id(0)
        panel_refs = refs[:groups]
        stat_refs = refs[groups : groups + 5]
        outs = refs[groups + 5 : groups + 9]
        ordered, matrix = refs[groups + 9 :]

        @pl.when(step == 0)
        def _():
            for number, panel in enumerate(panel_refs):
                ordered[places_ref[number]] = panel[...]
            for part in range(parts):
                matrix[:, part * breadth : (part + 1) * breadth] = jnp.concatenate(
                    [
                        ordered[group, :, part * GROUP_WIDTH : (part + 1) * GROUP_WIDTH].astype(F32)
                        for group in range(groups)
                    ],
                    axis=1,
                )

        turned = turn_ref[0] == 1
        rate = jnp.where(turned, RATE_OUTPUT, RATE_PROJECT).astype(F32)
        for number in range(width):
            block = step * width + number
            row_now = jnp.where(turned, block % side % 2, block // per_row)
            column_now = jnp.where(
                turned, block % side // 2 * per_part + block // side, block % per_row
            )
            found = matrix[
                pl.ds(pl.multiple_of(row_now * BS, BS), BS),
                pl.ds(pl.multiple_of(column_now * BS, BS), BS),
            ]
            found = jnp.where(turned, found.T, found)
            results = renew(found, *[ref[number] for ref in stat_refs], rate)
            for target, result in zip(outs, results):
                target[number] = result

    return pl.pallas_call(
        kernel,
        grid_spec=pltpu.PrefetchScalarGridSpec(
            num_scalar_prefetch=2,
            grid=(count // width,),
            in_specs=[fixed] * groups + [spec] * 5,
            out_specs=[spec] * 4,
            scratch_shapes=[
                pltpu.VMEM((groups, *panels[0].shape), LOW),
                pltpu.VMEM((panel_rows, parts * breadth), F32),
            ],
        ),
        out_shape=[shape] * 4,
        compiler_params=params(),
        cost_estimate=pl.CostEstimate(
            flops=count * 24 * BS * BS * BS,
            bytes_accessed=count * BS * BS * 38,
            transcendentals=0,
        ),
        name="shampoo_panel",
    )(turn, places, *panels, *stats)


def shampoo_small(weights, gradient, left_stat, right_stat, left_root, right_root, step_rates):
    left_new = STAT_DECAY * left_stat + (1.0 - STAT_DECAY) * jnp.einsum(
        "nij,nkj->nik", gradient, gradient, precision=PRECISE
    )
    right_new = STAT_DECAY * right_stat + (1.0 - STAT_DECAY) * jnp.einsum(
        "nji,njk->nik", gradient, gradient, precision=PRECISE
    )
    turned = jnp.einsum("nij,njk->nik", gradient, right_root, precision=PRECISE)
    direction = jnp.einsum("nij,njk->nik", left_root, turned, precision=PRECISE)
    return (left_new, right_new, weights - step_rates * direction)


def shifted(values, axis, size, distance):
    return lax.ppermute(values, axis, [(i, (i + distance) % size) for i in range(size)])


def crossed(values, axes, size, distance):
    return lax.ppermute(values, axes, [(i, i ^ distance) for i in range(size)])


def direct_sum(values, axes, size):
    terms = [values] + [crossed(values, axes, size, step) for step in range(1, size)]
    while len(terms) > 1:
        terms = [terms[at] + terms[at + 1] for at in range(0, len(terms), 2)]
    return terms[0]


def everywhere_sum(values, sizes):
    a_size, b_size, c_size, f_size = sizes
    values = direct_sum(values, "f", f_size)
    values = direct_sum(values, "c", c_size)
    return direct_sum(values, ("a", "b"), a_size * b_size)


def body(
    sizes,
    inputs,
    out_grad,
    vectors,
    block_order,
    seq_lengths,
    expert_ids,
    attn_weights,
    attn_left,
    attn_right,
    attn_left_root,
    attn_right_root,
    expert_weights,
    expert_left,
    expert_right,
    expert_left_root,
    expert_right_root,
    router_weights,
    router_left,
    router_right,
    router_left_root,
    router_right_root,
):
    a_size, b_size, c_size, f_size = sizes
    rows = inputs.shape[0]
    capacity = rows // 4
    tokens_all = rows * a_size * b_size * c_size * f_size
    per_side = D // BS
    project_blocks = 3 * per_side * per_side
    a_place = lax.axis_index("a")
    c_place = lax.axis_index("c")
    f_place = lax.axis_index("f")
    per_device = attn_weights.shape[0]
    per = expert_weights.shape[1]
    shares = b_size * c_size
    local_slices = expert_weights.shape[0]

    by_panels = f_size == 4 and c_size == 2 and a_size == 2
    ends = jnp.cumsum(seq_lengths[0]).astype(jnp.int32)
    order = block_order[0].reshape(a_size * b_size, c_size, SLOTS)
    kpb = jnp.stack(
        [
            lax.dynamic_index_in_dim(order, (c_place - step) % c_size, 1, False).reshape(-1)
            for step in range(c_size)
        ]
    )

    split_count = expert_weights.shape[0] * f_size // EXPERTS
    numbers = jnp.arange(EXPERTS, dtype=jnp.int32)
    spots = (numbers % a_size) * f_size + numbers // a_size if split_count == 1 else numbers
    route_count = EXPERTS + ZEROS
    named = expert_ids[:, :, None] == jnp.arange(route_count, dtype=jnp.int32)[None, None, :]
    route_member = named.astype(F32)
    chosen = jnp.any(named[:, :, :EXPERTS], axis=1).astype(LOW)
    row_numbers = jnp.arange(rows, dtype=jnp.int32)
    before = (row_numbers[None, :] < row_numbers[:, None]).astype(LOW)
    ranks = jnp.dot(before, chosen, preferred_element_type=F32).astype(jnp.int32)
    slots = jnp.sum(
        jnp.where(named[:, :, :EXPERTS], (spots * capacity)[None, None, :] + ranks[:, None, :], 0),
        axis=2,
    )
    slots = jnp.where(expert_ids < EXPERTS, slots, -1)
    slot_numbers = jnp.arange(EXPERTS * capacity, dtype=jnp.int32)
    picks = [
        (slot_numbers[:, None] == slots[:, which][None, :]).astype(LOW) for which in range(2)
    ]
    picks_both = picks[0] + picks[1]

    def to_owners(buffer):
        buffer = buffer.astype(LOW).reshape(EXPERTS, capacity, D)
        if split_count > 1:
            buffer = jnp.repeat(buffer, split_count, axis=0)
        arrived = lax.all_to_all(buffer, ("a", "f"), split_axis=0, concat_axis=0, tiled=True)
        return arrived.reshape(-1, D)

    def return_rows(results):
        return lax.all_to_all(
            results.reshape(EXPERTS * split_count, -1, D),
            ("a", "f"),
            split_axis=0,
            concat_axis=0,
            tiled=True,
        )

    def from_owners(back, pick_matrices):
        back = back.reshape(EXPERTS, split_count, capacity, D)
        return [
            sum(
                dot(matrix, back[:, part].reshape(-1, D), 0, 0) for part in range(split_count)
            )
            for matrix in pick_matrices
        ]

    tie = lax.optimization_barrier
    share_place = lax.axis_index(("b", "c"))

    def over_groups(values):
        return lax.all_to_all(values, ("a", "b"), split_axis=0, concat_axis=0, tiled=True)

    def over_b(values):
        return crossed(values, "b", b_size, 1)

    def over_c(values):
        return crossed(values, "c", c_size, 1)

    if by_panels:
        group_place = lax.axis_index(("a", "b"))
        share_places = jnp.stack([share_place ^ step for step in range(shares)])
        first_spots, other_spots = a_place * shares + share_places, (
            (1 - a_place) * shares + share_places
        )

        def halves(values):
            return [values[: per // 2], values[per // 2 :]]

        own = jnp.where(a_place == 0, expert_weights[0], expert_weights[1])
        own_halves = halves(own)
        sent = jnp.where(a_place == 0, expert_weights[1], expert_weights[0])
        cuts = [slice(0, per // 2), slice(per // 2, per * 3 // 4), slice(per * 3 // 4, per)]
        across = crossed(attn_weights, "f", f_size, 2)
        own_c = over_c(own)
        got = [shifted(sent[cuts[0]], "a", 2, 1), None]
        own_b = [over_b(own_halves[0]), None]

        def both(spot):
            return [2 * spot, 2 * spot + 1]

        weight_places = [first_spots[0], first_spots[1]] + both(first_spots[2])
        weight_places += both(first_spots[3]) + both(other_spots[0]) + both(other_spots[1])
        weight_places += both(other_spots[2]) + both(other_spots[3])
        weight_places = jnp.stack(weight_places).astype(jnp.int32)
        kept_places = jnp.stack([share_places[step] for step in (0, 2, 1, 3)])
        given_places = [share_places[0], 2 * share_places[1], 2 * share_places[3]]
        given_places += [2 * share_places[2] + 1, 2 * share_places[3] + 1]
        given_places += [2 * share_places[2], 2 * share_places[1] + 1]
        kept_places = kept_places.astype(jnp.int32)
        given_places = jnp.stack(given_places).astype(jnp.int32)
        group_places = jnp.stack([group_place ^ step for step in range(HEAD_GROUPS)])
        group_places = group_places.astype(jnp.int32)
        shard_places = jnp.stack([f_place ^ step for step in range(f_size)]).astype(jnp.int32)
        (across, own_c, got[0], own_b[0], kpb, ends, *tables) = tie(
            (across, own_c, got[0], own_b[0], kpb, ends)
            + (weight_places, kept_places, given_places, group_places, shard_places)
        )
        weight_places, kept_places, given_places, group_places, shard_places = tables
        shards = [
            attn_weights,
            crossed(attn_weights, "f", f_size, 1),
            across,
            crossed(across, "f", f_size, 1),
        ]
        first_low, first_factor, own_queries, own_pairs, w_project = project_kernel(
            inputs, vectors[0:1], shard_places, shards
        )
        w_project = w_project.reshape(D, 3 * D)
        own_pairs, got_next = tie((own_pairs, shifted(sent[cuts[1]], "a", 2, 1)))
        own_b[1] = over_b(own_halves[1])
        own_bc = [over_c(own_b[0]), None]
        got_c = [over_c(got[0]), None]
        mine, own_b[1], own_bc[0], got_c[0] = tie(
            (over_groups(own_pairs), own_b[1], own_bc[0], got_c[0])
        )
        other = over_c(mine)
        queries = over_groups(own_queries)
        got_last = shifted(tie((sent[cuts[2]], mine))[0], "a", 2, 1)
        queries, other, got_last = tie((queries, other, got_last))
        got[1] = jnp.concatenate([got_next, got_last], axis=0)
        pairs = [mine, other]
        first_sent, own_b1, got_0, got_1 = tie((first_low, own_b[1], *got, queries))[:4]
        first_parts = [first_low, None, crossed(first_sent, ("a", "b"), HEAD_GROUPS, 2), None]
        own_bc[1] = over_c(own_b1)
        got_c[1] = over_c(got_1)
        got_b = [over_b(got_0), None]
        w_output = shards[3]
        for step in range(f_size - 1):
            w_output = jnp.where(f_place == 3 - step, shards[step], w_output)
        w_output = to_matrix(w_output, D, D)
        raw, low, lse = attend(kpb, ends, queries, pairs)
        raw, low, lse, first_parts[2], own_bc[1], got_c[1], got_b[0] = tie(
            (raw, low, lse, first_parts[2], own_bc[1], got_c[1], got_b[0])
        )
        got_b[1] = over_b(tie((got[1], low))[0])
    else:
        attn_all = lax.all_gather(attn_weights, "f", axis=0, tiled=True)
        w_project = to_matrix(attn_all[:project_blocks], D, 3 * D)
        w_output = to_matrix(attn_all[project_blocks:], D, D)
        first_norm, first_factor = normalize_parts(inputs, vectors[0])
        first_low = first_norm.astype(LOW)
        projected = jnp.dot(first_low, w_project, preferred_element_type=F32).astype(LOW)
        by_part = projected.reshape(rows, 3, HEAD_GROUPS, GROUP_WIDTH)
        own_queries = by_part[:, 0].transpose(1, 0, 2)
        own_pairs = (
            by_part[:, 1:].transpose(2, 0, 1, 3).reshape(HEAD_GROUPS, rows, 2 * GROUP_WIDTH)
        )
        mine = over_groups(own_pairs)
        pairs = [mine] + [shifted(mine, "c", c_size, step) for step in range(1, c_size)]
        queries = over_groups(pack_rows(own_queries))
        raw, low, lse = attend(kpb, ends, queries, pairs)
        weight_places = jnp.arange(local_slices, dtype=jnp.int32)
        weight_shares = [
            lax.all_gather(expert_weights[number], ("b", "c"), axis=0, tiled=True)
            for number in range(local_slices)
        ]
        weights = (weight_places, weight_shares)
    by_heads = unpack_rows(over_groups(low))
    attended = by_heads.transpose(1, 0, 2).reshape(rows, D)
    middle = inputs + jnp.dot(attended, w_output, preferred_element_type=F32)
    second, second_factor = normalize_parts(middle, vectors[1])
    second_low = second.astype(LOW)
    if by_panels:
        second_low, got_b[1] = tie((second_low, got_b[1]))
        first_sent, *got_bc = tie((first_low, *got_b, second_low))[:3]
        first_parts[1] = crossed(first_sent, ("a", "b"), HEAD_GROUPS, 1)
        got_bc = [over_c(part) for part in got_bc]

    logits = jnp.dot(second_low, router_weights, preferred_element_type=F32)
    picked_logits = jnp.sum(jnp.where(named, logits[:, None, :], 0.0), axis=2)
    route_gates = jax.nn.softmax(picked_logits, axis=-1)
    received = to_owners(dot(picks_both, second_low))
    grad_rows = [
        (route_gates[:, which][:, None] * out_grad).astype(LOW) for which in range(2)
    ]
    if by_panels:
        grad_rows[0], first_parts[1], *got_bc = tie((grad_rows[0], first_parts[1], *got_bc))
    arrived = to_owners(dot(picks[0], grad_rows[0]) + dot(picks[1], grad_rows[1]))
    if by_panels:
        weight_shares = [own, own_c, *own_b, *own_bc, *got, *got_c, *got_b, *got_bc]
        weights = (weight_places, weight_shares)
    result, gate_kept, up_kept, inner = expert_forward(received, weights)
    result = return_rows(result)
    back_rows, gate_grads, up_grads = expert_row_grads(arrived, gate_kept, up_kept, weights)
    if by_panels:
        full, part = per, per // 2
        half = a_place.astype(jnp.int32).reshape(1)
        given, hop_c, hop_b, near_b, near_c = expert_half_grads(
            1 - half,
            given_places,
            received,
            arrived,
            gate_grads,
            up_grads,
            inner,
            [(full,), (part, part), (part, part), (part,), (part,)],
        )
        first_parts[3] = over_b(tie((first_parts[2], arrived))[0])
        back_rows, result, near_b, gate_grads, up_grads, first_parts[3] = tie(
            (back_rows, result, near_b, gate_grads, up_grads, first_parts[3])
        )
        back_rows = return_rows(back_rows)
        kept, kept_far, kept_near, kept_next = expert_half_grads(
            half,
            kept_places,
            received,
            arrived,
            gate_grads,
            up_grads,
            inner,
            [(full,)] * 4,
        )
        back_rows, kept = tie((back_rows, kept))
        hop_c, hop_b = over_c(hop_c), over_b(hop_b)
    else:
        back_rows = return_rows(back_rows)
        grad_shares = expert_weight_grads(
            jnp.arange(shares, dtype=jnp.int32),
            received,
            arrived,
            gate_grads,
            up_grads,
            inner,
            [(per,)] * shares,
        )
    expert_rows = jnp.stack(from_owners(result, picks), axis=1)
    const_member = route_member[:, :, EXPERTS + 2 :]
    copy_member = route_member[:, :, EXPERTS + 1]
    route_values = (
        expert_rows
        + copy_member[:, :, None] * second[:, None, :]
        + jnp.einsum("rkc,cd->rkd", const_member, vectors[2:], precision=PRECISE)
    )
    output = middle + jnp.sum(route_gates[:, :, None] * route_values, axis=1)

    gate_grad = jnp.sum(out_grad[:, None, :] * route_values, axis=2)
    picked_grad = route_gates * (
        gate_grad - jnp.sum(route_gates * gate_grad, axis=1, keepdims=True)
    )
    logit_grad = jnp.sum(route_member * picked_grad[:, :, None], axis=1)
    router_local = lax.dot_general(
        logit_grad, second_low.astype(F32), (((0,), (0,)), ((), ())), precision=PRECISE
    )
    second_grad = jnp.dot(logit_grad, router_weights.astype(F32).T, precision=PRECISE)
    second_grad = second_grad + jnp.sum(route_gates * copy_member, axis=1)[:, None] * out_grad
    const_grad = jnp.einsum("rkc,rk,rd->cd", const_member, route_gates, out_grad, precision=PRECISE)
    second_grad = second_grad + from_owners(back_rows, [picks_both])[0]
    middle_part, second_gain_grad = normalize_back(middle, second_factor, vectors[1], second_grad)
    middle_grad = out_grad + middle_part
    middle_low = middle_grad.astype(LOW)

    flat = (-1, BS, BS)
    expert_stats = [
        item.reshape(flat)
        for item in (
            expert_weights,
            expert_left,
            expert_right,
            expert_left_root,
            expert_right_root,
        )
    ]

    attended_grad = dot(middle_low, w_output, 1, 1).astype(LOW)
    attended_grad = attended_grad.reshape(rows, HEAD_GROUPS, GROUP_WIDTH).transpose(1, 0, 2)
    attended_grad = over_groups(pack_rows(attended_grad))
    if by_panels:
        hop_c, hop_b = tie((hop_c, hop_b, middle_low))[:2]
        given_b = over_b((near_b.astype(F32) + hop_c[part:].astype(F32)).astype(LOW))
        given_c = (near_c.astype(F32) + hop_b[part:].astype(F32)).astype(LOW)
        kept_next = over_c(tie((kept_next, given_c))[0])
        given_c = over_c(given_c)
        early = jnp.concatenate([router_local, second_gain_grad[None], const_grad], axis=0)
        early = direct_sum(early, "f", f_size)
        early = direct_sum(early, ("a", "b"), HEAD_GROUPS)
        attended_grad, given_b, given_c, kept_next, early = tie(
            (attended_grad, given_b, given_c, kept_next, early)
        )
        kept_b = over_b((kept_far.astype(F32) + kept_next.astype(F32)).astype(LOW))
        taken = jnp.concatenate(
            [
                given[:part].astype(F32) + hop_c[:part].astype(F32) + given_b.astype(F32),
                given[part:].astype(F32) + hop_b[:part].astype(F32) + given_c.astype(F32),
            ],
            axis=0,
        )
        taken = shifted(taken.astype(LOW), "a", 2, 1)
        kept_near = over_c(tie((kept_near, attended_grad))[0])
        early = direct_sum(early, "c", c_size)
    back_outs = attend_back(kpb, ends, queries, pairs, attended_grad, raw, lse)
    if by_panels:
        *back_outs, kept_near, taken, early = tie((*back_outs, kept_near, taken, early))
        middle_late = tie((middle_low, back_outs[0]))[0]
        output_panels = jnp.einsum(
            "hrj,rd->hdj", by_heads, middle_late, preferred_element_type=F32
        ).astype(LOW)
        output_panels = over_groups(output_panels)
        expert_outs = shampoo_half(1 - half, [taken], expert_stats, None)
        first_parts = tie((*first_parts, back_outs[0]))[:HEAD_GROUPS]
        first_all = jnp.zeros((HEAD_GROUPS, rows, D), LOW)
        for step, part_rows in enumerate(first_parts):
            first_all = lax.dynamic_update_index_in_dim(
                first_all, part_rows, group_place ^ step, 0
            )
        first_all = first_all.reshape(-1, D)
    query_grad, pair_grad = back_outs[:2]
    for step in range(1, c_size):
        pair_grad = pair_grad + shifted(back_outs[1 + step], "c", c_size, -step).astype(F32)
    group_grad = jnp.concatenate([query_grad, pair_grad.astype(LOW)], axis=2)
    if by_panels:
        group_grad, output_panels, first_all, early, *expert_outs = tie(
            (group_grad, output_panels, first_all, early, *expert_outs)
        )
    if by_panels:
        panels = dot(first_all, group_grad.reshape(-1, 3 * GROUP_WIDTH), 0, 0).astype(LOW)
        group_grad, panels = tie((group_grad, panels))
    project_grad = (
        over_groups(group_grad)
        .reshape(HEAD_GROUPS, rows, 3, GROUP_WIDTH)
        .transpose(1, 2, 0, 3)
        .reshape(rows, 3 * D)
    )
    first_grad = dot(project_grad, w_project, 1, 1)
    input_part, first_gain_grad = normalize_back(inputs, first_factor, vectors[0], first_grad)
    input_grad = middle_grad + input_part

    everywhere = ("a", "b", "c", "f")
    if not by_panels:
        early = jnp.concatenate([router_local, second_gain_grad[None], const_grad], axis=0)
        early = everywhere_sum(early, sizes)
    late = direct_sum(first_gain_grad[None], "f", f_size)
    late = direct_sum(late, "c", c_size)
    late = direct_sum(late, ("a", "b"), a_size * b_size)

    attn_stats = (attn_weights, attn_left, attn_right, attn_left_root, attn_right_root)
    if by_panels:
        panels = panels.reshape(3, D // 3, 3 * GROUP_WIDTH)
        output_panels = jnp.sum(output_panels.astype(F32), axis=0).astype(LOW)
        output_panels = (
            output_panels.reshape(3, D // 3, GROUP_WIDTH)
            .transpose(1, 0, 2)
            .reshape(1, D // 3, 3 * GROUP_WIDTH)
        )
        panels = jnp.concatenate([panels, output_panels], axis=0)
        own_panels = [
            lax.dynamic_index_in_dim(panels, f_place ^ step, 0, False) for step in range(f_size)
        ]
        summed = own_panels[0].astype(F32)
        for step in range(1, f_size):
            summed = summed + crossed(own_panels[step], "f", f_size, step).astype(F32)
        summed = summed.astype(LOW)
        kept = [kept, kept_near, kept_b]
        summed = (summed.astype(F32) + crossed(summed, "c", 2, 1).astype(F32)).astype(LOW)
        group_panels = [
            crossed(summed, ("a", "b"), HEAD_GROUPS, step) for step in range(1, HEAD_GROUPS)
        ]
        kept[0] = tie((kept[0], summed))[0]
        expert_outs = shampoo_half(half, kept, expert_stats, expert_outs)
        late, early, *joined = tie((late, early, *group_panels, *expert_outs))
        group_panels, expert_outs = joined[: HEAD_GROUPS - 1], joined[HEAD_GROUPS - 1 :]
        turn = (f_place == 3).astype(jnp.int32).reshape(1)
        attn_outs = shampoo_panel(
            turn, group_places, [summed, *group_panels], attn_stats
        )
    else:
        output_weight_grad = dot(attended, middle_low, 0, 0)
        project_weight_grad = dot(first_low, project_grad, 0, 0)
        attn_local = jnp.concatenate(
            [to_blocks(project_weight_grad, BS, BS), to_blocks(output_weight_grad, BS, BS)],
            axis=0,
        )
        attn_sum = lax.psum(attn_local, everywhere)
        attn_gradient = lax.dynamic_slice_in_dim(attn_sum, f_place * per_device, per_device, 0)
        block_numbers = f_place * per_device + jnp.arange(per_device, dtype=jnp.int32)
        attn_rates = jnp.where(block_numbers < project_blocks, RATE_PROJECT, RATE_OUTPUT)
        attn_outs = shampoo(attn_rates.astype(F32), attn_gradient, attn_stats)
        expert_gradient = lax.psum_scatter(
            jnp.concatenate(grad_shares, axis=0).reshape(local_slices, -1, BS, BS).astype(F32),
            ("b", "c"),
            scatter_dimension=1,
            tiled=True,
        ).reshape(flat)
        expert_outs = shampoo(
            jnp.full((expert_gradient.shape[0],), RATE_EXPERT, F32), expert_gradient, expert_stats
        )
    expert_grads, expert_left_new, expert_right_new, expert_new = [
        item.reshape(expert_weights.shape) for item in expert_outs
    ]
    attn_grads, attn_left_new, attn_right_new, attn_new = attn_outs
    router_grads = early[:route_count].T
    vector_grads = jnp.concatenate([late, early[route_count:]], axis=0)
    router_left_new, router_right_new, router_moved = shampoo_small(
        to_blocks(router_weights.astype(F32), BS, route_count),
        to_blocks(router_grads, BS, route_count),
        router_left,
        router_right,
        router_left_root,
        router_right_root,
        RATE_ROUTER,
    )
    router_new = to_matrix(router_moved, D, route_count)
    vector_new = vectors - RATE_VECTOR * float(tokens_all) ** (-0.5) * vector_grads
    return (
        output,
        input_grad,
        vector_grads,
        vector_new,
        attn_grads,
        attn_left_new,
        attn_right_new,
        attn_new,
        expert_grads,
        expert_left_new,
        expert_right_new,
        expert_new,
        router_grads,
        router_left_new,
        router_right_new,
        router_new,
    )


def solution(mesh):
    ctx_size = mesh.shape["ctx"]
    f_size = mesh.shape["fsdp"]
    context = ("a", "b", "c")
    token_rows = P(context + ("f",), None)
    group_rows = P("f", None)
    attn = P("f", None, None)
    expert = P("f", context, None, None)
    in_specs = (
        (token_rows, token_rows, P(), group_rows, group_rows, token_rows)
        + (attn,) * 5
        + (expert,) * 5
        + (P(),) * 5
    )
    out_specs = (token_rows, token_rows, P(), P()) + (attn,) * 4 + (expert,) * 4 + (P(),) * 4

    def run(*arrays):
        local_slices = arrays[11].shape[0] // f_size
        a_size = 2 if local_slices == 2 else 1
        b_size = HEAD_GROUPS // a_size
        c_size = ctx_size // HEAD_GROUPS
        sizes = (a_size, b_size, c_size, f_size)
        fine_mesh = jax.sharding.Mesh(mesh.devices.reshape(sizes), ("a", "b", "c", "f"))
        return jax.shard_map(
            functools.partial(body, sizes),
            mesh=fine_mesh,
            in_specs=in_specs,
            out_specs=out_specs,
            check_vma=False,
        )(*arrays)

    return run
```

time: 2700 us -> 605 us (0.22)
  waiting for transfers between devices: 1780 us -> 214 us
  matrix products: 366 us -> 33.8 us
  local copies, waits for them, and re-layouts: 345 us -> 35.5 us
  Pallas kernels: 0 us -> 171 us
  other arithmetic: 121 us -> 27.5 us
  starting transfers between devices: 17 us -> 107 us
  blocking collectives: 45.7 us -> 0 us
    psum x1 -> x0, waiting for transfers between devices: 1110 us -> none  [body(): lax.psum(lax.psum_scatter(attn_local, 'fsdp', scatter_dimension=0, tiled=...]
    all_gather x4 -> x0, waiting for transfers between devices: 353 us -> none  [the longest x1 189 us: body(): expert_all = lax.all_gather(expert_weights, 'ctx', axis=1, tiled=True)]
    dot_general x58 -> x18, matrix products: 362 us -> 29.3 us  [the longest x9 20.4 us: dot(): lax.dot_general(left, right, (((left_dim,), (right_dim,)), ((), ())), pre...]
    reduce_scatter x2 -> x0, waiting for transfers between devices: 306 us -> none  [the longest x1 306 us: body(): lax.psum_scatter(back_state[1], 'ctx', scatter_dimension=0, tiled=True)]
    pallas_call x0 -> x10, Pallas kernels: none -> 171 us  [the longest x1 36.7 us: attend_back(): pl.pallas_call(functools.partial(attend_back_kernel, len(pairs), block_ro...]
    ppermute x0 -> x51, waiting for transfers between devices: none -> 161 us  [the longest x46 130 us: crossed(): return lax.ppermute(values, axes, [(i, i ^ distance) for i in range(size)])]
    unnamed x189 -> x112, local copies, waits for them, and re-layouts: 79.7 us -> 10.5 us
    ppermute x0 -> x51, starting transfers between devices: none -> 62.6 us  [the longest x46 54.5 us: crossed(): return lax.ppermute(values, axes, [(i, i ^ distance) for i in range(size)])]
  transfers between devices with their start and end apart: 11 -> 61, of which waited for: 8 -> 27; matrix products, arithmetic and copies ran while one was open for 18% -> 11% of each run, Pallas kernels for 0% -> 26%
where the time goes in v1:
time: 605 us; the launch traced here: 595 us
  waiting for transfers between devices  214 us (35%)
  Pallas kernels  171 us (28%)
  starting transfers between devices  107 us (18%)
  local copies, waits for them, and re-layouts  35.5 us (6%)
  matrix products  33.8 us (6%)
  other arithmetic  27.5 us (5%)
    ppermute x46, waiting for transfers between devices, crossed(): return lax.ppermute(values, axes, [(i, i ^ distance) for i in range(size)])  130 us
    ppermute x46, starting transfers between devices, crossed(): return lax.ppermute(values, axes, [(i, i ^ distance) for i in range(size)])  54.5 us
    all_to_all x6, waiting for transfers between devices, over_groups(): lax.all_to_all(values, ('a', 'b'), split_axis=0, concat_axis=0, tiled=True)  38.8 us
    pallas_call x1, Pallas kernels, attend_back(): pl.pallas_call(functools.partial(attend_back_kernel, len(pairs), block_ro...  36.7 us
    ppermute x5, waiting for transfers between devices, shifted(): lax.ppermute(values, axis, [(i, (i + distance) % size) for i in range(siz...  31.1 us
    pallas_call x2, Pallas kernels, shampoo_half(): pl.pallas_call(kernel, grid_spec=pltpu.PrefetchScalarGridSpec(num_scalar_...  26.7 us
    all_to_all x6, starting transfers between devices, over_groups(): lax.all_to_all(values, ('a', 'b'), split_axis=0, concat_axis=0, tiled=True)  25.2 us
    pallas_call x2, Pallas kernels, expert_half_grads(): pl.pallas_call(kernel, grid=(hidden_blocks // 2,), in_specs=[smem_spec(),...  24.4 us
  transfers between devices with their start and end apart: 61, of which 27 were waited for; matrix products, arithmetic and copies ran while one was open for 11% of the time, Pallas kernels for 26%

profile of v1, /device:TPU:0, one launch (start us, length us, event | category | flops | bytes accessed | tf_op | source)
XLA Modules:
  0.0 594.7 jit_solution(8344929584760945205)
XLA Ops:
  22.9 13.7 %collective-permute-done.3.refs_2_ = bf16[18,128,128]{2,1,0:T(8,128)(2,1)} collective-permute-done((bf16[18,128,128]{2,1,0:T(8,128)(2,1)}, bf16[18,128,128]{2,1,0:T(8,128)(2,1)}, u32[]{:S(2)}, u32[]{:S(2)}) %collective-permute-start.3) | collective-permute-done | bytes 589856 | tf_op jit(solution)/shard_map/ppermute | solution.py:1081
  42.8 8.9 %project.1 = (bf16[384,768]{1,0:T(8,128)(2,1)}, f32[384,1]{1,0:T(8,128)}, bf16[4,192,384]{2,1,0:T(8,128)(2,1)}, bf16[4,384,384]{2,1,0:T(8,128)(2,1)}, bf16[3,256,2304]{2,1,0:T(8,128)(2,1)}) custom-call(s32[4]{0:T(128)} %pad_add_fusion.2.places_ref, f32[384,768]{1,0:T(8,128)} %rows_ref.1, f32[1,768]{1,0:T(1,128)} %get-tuple-element.312.gain_ref, ...), custom_call_target="tpu_custom_call" | custom-call | flops 589824 | bytes 1000000 | tf_op jit(solution)/shard_map/project/pallas_call | solution.py:143
  51.7 4.4 collective-permute-done.6
  64.5 30.4 %collective-permute-done.7.refs_3_ = bf16[18,128,128]{2,1,0:T(8,128)(2,1)S(1)} collective-permute-done((bf16[18,128,128]{2,1,0:T(8,128)(2,1)S(1)}, bf16[18,128,128]{2,1,0:T(8,128)(2,1)S(1)}, u32[]{:S(2)}, u32[]{:S(2)}) %collective-permute-start.7) | collective-permute-done | bytes 589856 | tf_op jit(solution)/shard_map/ppermute | solution.py:1081
  105.0 17.8 %all-to-all-done.refs_2_ = bf16[4,192,384]{2,1,0:T(8,128)(2,1)S(1)} async-done(((bf16[4,192,384]{2,1,0:T(8,128)(2,1)}), bf16[4,192,384]{2,1,0:T(8,128)(2,1)S(1)}, u32[]{:S(2)}, u32[]{:S(2)}) %all-to-all-start) | async-done | bytes 589856 | tf_op jit(solution)/shard_map/all_to_all | solution.py:1196
  122.8 5.4 collective-permute-done.11
  134.2 19.7 %attend_forward.1 = (f32[4,384,192]{2,1,0:T(8,128)}, bf16[4,192,384]{2,1,0:T(8,128)(2,1)}, f32[16,288,1]{2,1,0:T(8,128)}) custom-call(s32[2,16]{1,0:T(2,128)} %pad_add_fusion.refs_0_, s32[4]{0:T(128)} %bitcast.208, bf16[4,192,384]{2,1,0:T(8,128)(2,1)} %copy-done.8, bf16[4,384,384]{2,1,0:T(8,128)(2,1)} %copy-done.5, bf16[4,384,384]{2,1,0:T(8,128)(2,1)} %copy-done.15), custom_call_target="tpu_custom_call" | custom-call | flops 98304 | bytes 1000000 | tf_op jit(solution)/shard_map/attend_forward/pallas_call | solution.py:382
  166.7 8.7 %all-to-all-done.2 = bf16[4,192,384]{2,1,0:T(8,128)(2,1)S(1)} async-done(((bf16[4,192,384]{2,1,0:T(8,128)(2,1)}), bf16[4,192,384]{2,1,0:T(8,128)(2,1)S(1)}, u32[]{:S(2)}, u32[]{:S(2)}) %all-to-all-start.2) | async-done | bytes 589856 | tf_op jit(solution)/shard_map/all_to_all | solution.py:1196
  180.5 4.9 collective-permute-done.16.refs_11_
  187.2 4.6 all-to-all-start.4
  196.5 21.8 %collective-permute-done.17 = bf16[384,768]{1,0:T(8,128)(2,1)} collective-permute-done((bf16[384,768]{1,0:T(8,128)(2,1)}, bf16[384,768]{1,0:T(8,128)(2,1)}, u32[]{:S(2)}, u32[]{:S(2)}) %collective-permute-start.17) | collective-permute-done | bytes 589856 | tf_op jit(solution)/shard_map/ppermute | solution.py:1081
  222.4 4.8 all-to-all-start.3
  227.2 19.1 %expert_forward.1 = (bf16[768,768]{1,0:T(8,128)(2,1)}, f32[768,2048]{1,0:T(8,128)}, f32[768,2048]{1,0:T(8,128)}, bf16[768,2048]{1,0:T(8,128)(2,1)}) custom-call(s32[14]{0:T(128)} %stack.103.places_ref, bf16[768,768]{1,0:T(8,128)(2,1)} %bitcast.34.rows_ref, bf16[36,128,128]{2,1,0:T(8,128)(2,1)} %bitcast.186, ...), custom_call_target="tpu_custom_call" | custom-call | flops 7247757312 | bytes 11796480 | tf_op jit(solution)/shard_map/expert_forward/pallas_call | solution.py:649
  246.3 10.4 %all-to-all-done.3 = bf16[8,96,768]{2,1,0:T(8,128)(2,1)} async-done(((bf16[8,96,768]{2,1,0:T(8,128)(2,1)}), bf16[8,96,768]{2,1,0:T(8,128)(2,1)}, u32[]{:S(2)}, u32[]{:S(2)}) %all-to-all-start.3) | async-done | bytes 1179680 | tf_op jit(solution)/shard_map/all_to_all | solution.py:1171
  261.1 20.2 %expert_row_grads.1 = (bf16[768,768]{1,0:T(8,128)(2,1)}, bf16[768,2048]{1,0:T(8,128)(2,1)}, bf16[768,2048]{1,0:T(8,128)(2,1)}) custom-call(s32[14]{0:T(128)} %stack.103.places_ref, bf16[768,768]{1,0:T(8,128)(2,1)} %bitcast.32.grads_ref, f32[768,2048]{1,0:T(8,128)} %get-tuple-element.187.gate_i, f32[768,2048]{1,0:T(8,128)} %get-tuple-element.188.up_i, ...), custom_call_target="tpu_custom_call" | custom-call | flops 7247757312 | bytes 22413312 | tf_op jit(solution)/shard_map/expert_row_grads/pallas_call | solution.py:720
  281.3 12.2 %expert_half_grads.2 = (bf16[36,128,128]{2,1,0:T(8,128)(2,1)}, bf16[36,128,128]{2,1,0:T(8,128)(2,1)}, bf16[36,128,128]{2,1,0:T(8,128)(2,1)}, bf16[18,128,128]{2,1,0:T(8,128)(2,1)}, bf16[18,128,128]{2,1,0:T(8,128)(2,1)}) custom-call(s32[1]{0:T(128)S(6)} %sub.58.which_ref.half_ref, s32[7]{0:T(128)} %stack.111.places_ref, bf16[768,768]{1,0:T(8,128)(2,1)} %bitcast.34.rows_ref, ...), custom_call_target="tpu_custom_call" | custom-call | flops 3623878656 | bytes 12976128 | tf_op jit(solution)/shard_map/expert_half_grads/pallas_call | solution.py:875
  293.5 5.4 all-to-all-start.6
  312.1 12.2 %expert_half_grads.3 = (bf16[36,128,128]{2,1,0:T(8,128)(2,1)}, bf16[36,128,128]{2,1,0:T(8,128)(2,1)}, bf16[36,128,128]{2,1,0:T(8,128)(2,1)}, bf16[36,128,128]{2,1,0:T(8,128)(2,1)}) custom-call(s32[1]{0:T(128)} %bitcast.36.which_ref.half_ref, s32[4]{0:T(128)} %get-tuple-element.200.places_ref, bf16[768,768]{1,0:T(8,128)(2,1)} %bitcast.34.rows_ref, ...), custom_call_target="tpu_custom_call" | custom-call | flops 3623878656 | bytes 12976128 | tf_op jit(solution)/shard_map/expert_half_grads/pallas_call | solution.py:875
  333.1 8.0 %collective-permute-done.22 = bf16[36,128,128]{2,1,0:T(8,128)(2,1)} collective-permute-done((bf16[36,128,128]{2,1,0:T(8,128)(2,1)}, bf16[36,128,128]{2,1,0:T(8,128)(2,1)}, u32[]{:S(2)}, u32[]{:S(2)}) %collective-permute-start.22) | collective-permute-done | bytes 1179680 | tf_op jit(solution)/shard_map/ppermute | solution.py:1081
  348.1 5.5 all-to-all-start.7
  363.7 16.0 %collective-permute-done.29 = f32[15,768]{1,0:T(8,128)S(1)} collective-permute-done((f32[15,768]{1,0:T(8,128)S(1)}, f32[15,768]{1,0:T(8,128)S(1)}, u32[]{:S(2)}, u32[]{:S(2)}) %collective-permute-start.29) | collective-permute-done | bytes 46112 | tf_op jit(solution)/shard_map/ppermute | solution.py:1081
  391.1 36.7 %attend_backward.1 = (bf16[4,384,192]{2,1,0:T(8,128)(2,1)}, f32[4,384,384]{2,1,0:T(8,128)}, bf16[4,384,384]{2,1,0:T(8,128)(2,1)}) custom-call(s32[2,16]{1,0:T(2,128)} %pad_add_fusion.refs_0_, s32[4]{0:T(128)} %bitcast.209, bf16[4,192,384]{2,1,0:T(8,128)(2,1)} %copy-done.8, bf16[4,384,384]{2,1,0:T(8,128)(2,1)} %copy-done.5, bf16[4,384,384]{2,1,0:T(8,128)(2,1)} %copy-done.15, ...), custom_call_target="tpu_custom_call" | custom-call | flops 98304 | bytes 1000000 | tf_op jit(solution)/shard_map/attend_backward/pallas_call | solution.py:543
  428.5 12.0 %collective-permute-done.33.refs_0_ = bf16[36,128,128]{2,1,0:T(8,128)(2,1)S(1)} collective-permute-done((bf16[36,128,128]{2,1,0:T(8,128)(2,1)S(1)}, bf16[36,128,128]{2,1,0:T(8,128)(2,1)S(1)}, u32[]{:S(2)}, u32[]{:S(2)}) %collective-permute-start.33) | collective-permute-done | bytes 1179680 | tf_op jit(solution)/shard_map/ppermute | solution.py:1077
  448.4 13.1 %shampoo_half.2 = (f32[72,128,128]{2,1,0:T(8,128)}, f32[72,128,128]{2,1,0:T(8,128)}, f32[72,128,128]{2,1,0:T(8,128)}, f32[72,128,128]{2,1,0:T(8,128)}) custom-call(s32[1]{0:T(128)S(6)} %sub.58.which_ref.half_ref, bf16[36,128,128]{2,1,0:T(8,128)(2,1)} %copy-done.25, bf16[72,128,128]{2,1,0:T(8,128)(2,1)} %bitcast.166, f32[72,128,128]{2,1,0:T(8,128)} %bitcast.168, ...), custom_call_target="tpu_custom_call" | custom-call | flops 1811939328 | bytes 21233664 | tf_op jit(solution)/shard_map/shampoo_half/pallas_call | solution.py:936
  467.5 7.2 %collective-permute-done.35 = bf16[4,384,384]{2,1,0:T(8,128)(2,1)S(1)} collective-permute-done((bf16[4,384,384]{2,1,0:T(8,128)(2,1)S(1)}, bf16[4,384,384]{2,1,0:T(8,128)(2,1)S(1)}, u32[]{:S(2)}, u32[]{:S(2)}) %collective-permute-start.35) | collective-permute-done | bytes 1179680 | tf_op jit(solution)/shard_map/ppermute | solution.py:1077
  475.9 4.6 convolution_convert_fusion.1
  482.7 5.0 all-to-all-start.9
  507.1 6.1 %collective-permute-done.45 = bf16[256,576]{1,0:T(8,128)(2,1)S(1)} collective-permute-done((bf16[256,576]{1,0:T(8,128)(2,1)S(1)}, bf16[256,576]{1,0:T(8,128)(2,1)S(1)}, u32[]{:S(2)}, u32[]{:S(2)}) %collective-permute-start.45) | collective-permute-done | bytes 294944 | tf_op jit(solution)/shard_map/ppermute | solution.py:1081
  515.8 12.3 %all-to-all-done.9 = bf16[4,384,576]{1,2,0:T(8,128)(2,1)S(1)} async-done(((bf16[4,384,576]{1,2,0:T(8,128)(2,1)}), bf16[4,384,576]{1,2,0:T(8,128)(2,1)S(1)}, u32[]{:S(2)}, u32[]{:S(2)}) %all-to-all-start.9) | async-done | bytes 1769504 | tf_op jit(solution)/shard_map/all_to_all | solution.py:1196
  542.3 9.7 %collective-permute-done.50.refs_2_ = bf16[36,128,128]{2,1,0:T(8,128)(2,1)} collective-permute-done((bf16[36,128,128]{2,1,0:T(8,128)(2,1)}, bf16[36,128,128]{2,1,0:T(8,128)(2,1)}, u32[]{:S(2)}, u32[]{:S(2)}) %collective-permute-start.50) | collective-permute-done | bytes 1179680 | tf_op jit(solution)/shard_map/ppermute | solution.py:1081
  552.0 13.6 %shampoo_half.3 = (f32[72,128,128]{2,1,0:T(8,128)}, f32[72,128,128]{2,1,0:T(8,128)}, f32[72,128,128]{2,1,0:T(8,128)}, f32[72,128,128]{2,1,0:T(8,128)}) custom-call(s32[1]{0:T(128)} %bitcast.36.which_ref.half_ref, bf16[36,128,128]{2,1,0:T(8,128)(2,1)} %get-tuple-element.250.refs_0_, ...), custom_call_target="tpu_custom_call", output_to_operand_aliasing={{0}: (9, {}), {1}: (10, {}), {2}: (11, {}), {3}: (12, {})} | custom-call | flops 1811939328 | bytes 23592960 | tf_op jit(solution)/shard_map/shampoo_half/pallas_call | solution.py:936
  579.4 15.0 %shampoo_panel.1 = (f32[36,128,128]{2,1,0:T(8,128)}, f32[36,128,128]{2,1,0:T(8,128)}, f32[36,128,128]{2,1,0:T(8,128)}, f32[36,128,128]{2,1,0:T(8,128)}) custom-call(s32[1]{0:T(128)} %bitcast.72.turn_ref, s32[4]{0:T(128)} %get-tuple-element.264.places_ref, bf16[256,576]{1,0:T(8,128)(2,1)} %copy-done.23, bf16[256,576]{1,0:T(8,128)(2,1)} %copy-done.33, ...), custom_call_target="tpu_custom_call" | custom-call | flops 1811939328 | bytes 22413312 | tf_op jit(solution)/shard_map/shampoo_panel/pallas_call | solution.py:1041
  (326 shorter events, 199.4 us)
Async XLA Ops:
  0.7 38.1 %collective-permute-start = (bf16[36,128,128]{2,1,0:T(8,128)(2,1)}, bf16[36,128,128]{2,1,0:T(8,128)(2,1)}, u32[]{:S(2)}, u32[]{:S(2)}) collective-permute-start(bf16[36,128,128]{2,1,0:T(8,128)(2,1)} %refs_4_.1), channel_id=1, source_target_pairs={{0,2},{1,3},{2,0},{3,1},{4,6},{5,7},{6,4},{7,5},{8,10},{9,11},{10,... | collective-permute-start | bytes 3538952 | tf_op jit(solution)/shard_map/ppermute | solution.py:1081
  3.7 36.8 %collective-permute-start.4 = (bf16[36,128,128]{2,1,0:T(8,128)(2,1)}, bf16[36,128,128]{2,1,0:T(8,128)(2,1)}, u32[]{:S(2)}, u32[]{:S(2)}) collective-permute-start(bf16[36,128,128]{2,1,0:T(8,128)(2,1)} %refs_4_.1), channel_id=1, source_target_pairs={{0,1},{1,0},{2,3},{3,2},{4,5},{5,4},{6,7},{7,6},{8,9},{9,8},{10,11... | collective-permute-start | bytes 3538952 | tf_op jit(solution)/shard_map/ppermute | solution.py:1081
  5.5 33.3 %collective-permute-start.1 = (bf16[36,128,128]{2,1,0:T(8,128)(2,1)S(1)}, bf16[36,128,128]{2,1,0:T(8,128)(2,1)}, u32[]{:S(2)}, u32[]{:S(2)}) collective-permute-start(bf16[36,128,128]{2,1,0:T(8,128)(2,1)S(1)} %bitcast.185), channel_id=1, source_target_pairs={{0,4},{4,0},{1,5},{5,1},{2,6},{6,2},{3,7},{7,3},{8,12},{12,8},{9,1... | collective-permute-start | bytes 3538952 | tf_op jit(solution)/shard_map/ppermute | solution.py:1081
  8.1 28.4 %collective-permute-start.3 = (bf16[18,128,128]{2,1,0:T(8,128)(2,1)}, bf16[18,128,128]{2,1,0:T(8,128)(2,1)}, u32[]{:S(2)}, u32[]{:S(2)}) collective-permute-start(bf16[18,128,128]{2,1,0:T(8,128)(2,1)} %get-tuple-element.311), channel_id=1, source_target_pairs={{0,8},{8,0},{1,9},{9,1},{2,10},{10,2},{3,11},{11,3},{4,12},{12,4},... | collective-permute-start | bytes 1769480 | tf_op jit(solution)/shard_map/ppermute | solution.py:1081
  9.8 28.9 %collective-permute-start.2 = (bf16[18,128,128]{2,1,0:T(8,128)(2,1)S(1)}, bf16[18,128,128]{2,1,0:T(8,128)(2,1)}, u32[]{:S(2)}, u32[]{:S(2)}) collective-permute-start(bf16[18,128,128]{2,1,0:T(8,128)(2,1)S(1)} %slice_bitcast_fusion.2), channel_id=1, source_target_pairs={{0,16},{16,0},{1,17},{17,1},{2,18},{18,2},{3,19},{19,3},{4,20},{20... | collective-permute-start | bytes 1769480 | tf_op jit(solution)/shard_map/ppermute | solution.py:1077
  56.8 39.2 %all-to-all-start.1 = ((bf16[4,384,384]{2,1,0:T(8,128)(2,1)}), bf16[4,384,384]{2,1,0:T(8,128)(2,1)S(1)}, u32[]{:S(2)}, u32[]{:S(2)}) async-start(bf16[4,384,384]{2,1,0:T(8,128)(2,1)} %get-tuple-element.152), calls=%async_computation.1 | async-start | bytes 2359296 | tf_op jit(solution)/shard_map/all_to_all | solution.py:1196
  60.5 34.4 %collective-permute-start.7 = (bf16[18,128,128]{2,1,0:T(8,128)(2,1)S(1)}, bf16[18,128,128]{2,1,0:T(8,128)(2,1)S(1)}, u32[]{:S(2)}, u32[]{:S(2)}) collective-permute-start(bf16[18,128,128]{2,1,0:T(8,128)(2,1)S(1)} %copy-done.31), channel_id=1, source_target_pairs={{0,8},{8,0},{1,9},{9,1},{2,10},{10,2},{3,11},{11,3},{4,12},{12,4},... | collective-permute-start | bytes 1769480 | tf_op jit(solution)/shard_map/ppermute | solution.py:1081
  62.5 32.5 %collective-permute-start.8 = (bf16[18,128,128]{2,1,0:T(8,128)(2,1)}, bf16[18,128,128]{2,1,0:T(8,128)(2,1)S(1)}, u32[]{:S(2)}, u32[]{:S(2)}) collective-permute-start(bf16[18,128,128]{2,1,0:T(8,128)(2,1)} %collective-permute-done.3.refs_2_), channel_id=1, source_target_pairs={{0,4},{4,0},{1,5},{5,1},{2,6},{6,2},{3,7},{7,3},{8,12},{12,8},{9,1... | collective-permute-start | bytes 1769480 | tf_op jit(solution)/shard_map/ppermute | solution.py:1081
  63.0 31.9 %collective-permute-start.9 = (bf16[18,128,128]{2,1,0:T(8,128)(2,1)}, bf16[18,128,128]{2,1,0:T(8,128)(2,1)}, u32[]{:S(2)}, u32[]{:S(2)}) collective-permute-start(bf16[18,128,128]{2,1,0:T(8,128)(2,1)} %collective-permute-done.2.refs_6_), channel_id=1, source_target_pairs={{0,4},{4,0},{1,5},{5,1},{2,6},{6,2},{3,7},{7,3},{8,12},{12,8},{9,1... | collective-permute-start | bytes 1769480 | tf_op jit(solution)/shard_map/ppermute | solution.py:1081
  96.0 32.1 %collective-permute-start.10 = (bf16[4,384,384]{2,1,0:T(8,128)(2,1)S(1)}, bf16[4,384,384]{2,1,0:T(8,128)(2,1)S(1)}, u32[]{:S(2)}, u32[]{:S(2)}) collective-permute-start(bf16[4,384,384]{2,1,0:T(8,128)(2,1)S(1)} %all-to-all-done.1.refs_3_), channel_id=1, source_target_pairs={{0,4},{4,0},{1,5},{5,1},{2,6},{6,2},{3,7},{7,3},{8,12},{12,8},{9,1... | collective-permute-start | bytes 3538952 | tf_op jit(solution)/shard_map/ppermute | solution.py:1081
  100.4 27.8 %collective-permute-start.11 = (bf16[9,128,128]{2,1,0:T(8,128)(2,1)}, bf16[9,128,128]{2,1,0:T(8,128)(2,1)}, u32[]{:S(2)}, u32[]{:S(2)}) collective-permute-start(bf16[9,128,128]{2,1,0:T(8,128)(2,1)} %get-tuple-element.156), channel_id=1, source_target_pairs={{0,16},{16,0},{1,17},{17,1},{2,18},{18,2},{3,19},{19,3},{4,20},{20... | collective-permute-start | bytes 884744 | tf_op jit(solution)/shard_map/ppermute | solution.py:1077
  187.2 35.2 %all-to-all-start.4 = ((bf16[8,96,768]{2,1,0:T(8,128)(2,1)}), bf16[8,96,768]{2,1,0:T(8,128)(2,1)}, u32[]{:S(2)}, u32[]{:S(2)}) async-start(bf16[8,96,768]{2,1,0:T(8,128)(2,1)} %bitcast.202), calls=%async_computation.4 | async-start | bytes 2359296 | tf_op jit(solution)/shard_map/all_to_all | solution.py:1171
  193.5 27.1 %collective-permute-start.19 = (bf16[18,128,128]{2,1,0:T(8,128)(2,1)}, bf16[18,128,128]{2,1,0:T(8,128)(2,1)}, u32[]{:S(2)}, u32[]{:S(2)}) collective-permute-start(bf16[18,128,128]{2,1,0:T(8,128)(2,1)} %collective-permute-done.16.refs_11_), channel_id=1, source_target_pairs={{0,4},{4,0},{1,5},{5,1},{2,6},{6,2},{3,7},{7,3},{8,12},{12,8},{9,1... | collective-permute-start | bytes 1769480 | tf_op jit(solution)/shard_map/ppermute | solution.py:1081
  222.4 34.3 %all-to-all-start.3 = ((bf16[8,96,768]{2,1,0:T(8,128)(2,1)}), bf16[8,96,768]{2,1,0:T(8,128)(2,1)}, u32[]{:S(2)}, u32[]{:S(2)}) async-start(bf16[8,96,768]{2,1,0:T(8,128)(2,1)} %bitcast.188), calls=%async_computation.3 | async-start | bytes 2359296 | tf_op jit(solution)/shard_map/all_to_all | solution.py:1171
  256.7 36.8 %all-to-all-start.5 = ((bf16[8,96,768]{2,1,0:T(8,128)(2,1)}), bf16[8,96,768]{2,1,0:T(8,128)(2,1)}, u32[]{:S(2)}, u32[]{:S(2)}) async-start(bf16[8,96,768]{2,1,0:T(8,128)(2,1)} %bitcast.201), calls=%async_computation.5 | async-start | bytes 2359296 | tf_op jit(solution)/shard_map/all_to_all | solution.py:1175
  261.0 32.5 %collective-permute-start.20 = (bf16[384,768]{1,0:T(8,128)(2,1)}, bf16[384,768]{1,0:T(8,128)(2,1)}, u32[]{:S(2)}, u32[]{:S(2)}) collective-permute-start(bf16[384,768]{1,0:T(8,128)(2,1)} %collective-permute-done.12), channel_id=1, source_target_pairs={{0,8},{8,0},{1,9},{9,1},{2,10},{10,2},{3,11},{11,3},{4,12},{12,4},... | collective-permute-start | bytes 1769480 | tf_op jit(solution)/shard_map/ppermute | solution.py:1081
  293.5 35.0 %all-to-all-start.6 = ((bf16[8,96,768]{2,1,0:T(8,128)(2,1)}), bf16[8,96,768]{2,1,0:T(8,128)(2,1)}, u32[]{:S(2)}, u32[]{:S(2)}) async-start(bf16[8,96,768]{2,1,0:T(8,128)(2,1)} %bitcast.200), calls=%async_computation.6 | async-start | bytes 2359296 | tf_op jit(solution)/shard_map/all_to_all | solution.py:1175
  299.6 33.4 %collective-permute-start.21 = (bf16[36,128,128]{2,1,0:T(8,128)(2,1)}, bf16[36,128,128]{2,1,0:T(8,128)(2,1)}, u32[]{:S(2)}, u32[]{:S(2)}) collective-permute-start(bf16[36,128,128]{2,1,0:T(8,128)(2,1)} %get-tuple-element.207), channel_id=1, source_target_pairs={{0,4},{4,0},{1,5},{5,1},{2,6},{6,2},{3,7},{7,3},{8,12},{12,8},{9,1... | collective-permute-start | bytes 3538952 | tf_op jit(solution)/shard_map/ppermute | solution.py:1081
  301.2 39.9 %collective-permute-start.22 = (bf16[36,128,128]{2,1,0:T(8,128)(2,1)}, bf16[36,128,128]{2,1,0:T(8,128)(2,1)}, u32[]{:S(2)}, u32[]{:S(2)}) collective-permute-start(bf16[36,128,128]{2,1,0:T(8,128)(2,1)} %get-tuple-element.208), channel_id=1, source_target_pairs={{0,8},{8,0},{1,9},{9,1},{2,10},{10,2},{3,11},{11,3},{4,12},{12,4},... | collective-permute-start | bytes 3538952 | tf_op jit(solution)/shard_map/ppermute | solution.py:1081
  343.1 42.5 %collective-permute-start.25 = (bf16[36,128,128]{2,1,0:T(8,128)(2,1)}, bf16[36,128,128]{2,1,0:T(8,128)(2,1)}, u32[]{:S(2)}, u32[]{:S(2)}) collective-permute-start(bf16[36,128,128]{2,1,0:T(8,128)(2,1)} %get-tuple-element.213), channel_id=1, source_target_pairs={{0,4},{4,0},{1,5},{5,1},{2,6},{6,2},{3,7},{7,3},{8,12},{12,8},{9,1... | collective-permute-start | bytes 3538952 | tf_op jit(solution)/shard_map/ppermute | solution.py:1081
  348.1 37.5 %all-to-all-start.7 = ((bf16[4,192,384]{2,1,0:T(8,128)(2,1)}), bf16[4,192,384]{2,1,0:T(8,128)(2,1)S(1)}, u32[]{:S(2)}, u32[]{:S(2)}) async-start(bf16[4,192,384]{2,1,0:T(8,128)(2,1)} %reshape.357), calls=%async_computation.7 | async-start | bytes 1179648 | tf_op jit(solution)/shard_map/all_to_all | solution.py:1196
  355.6 30.0 %collective-permute-start.24 = (bf16[18,128,128]{2,1,0:T(8,128)(2,1)}, bf16[18,128,128]{2,1,0:T(8,128)(2,1)S(1)}, u32[]{:S(2)}, u32[]{:S(2)}) collective-permute-start(bf16[18,128,128]{2,1,0:T(8,128)(2,1)} %add_convert_fusion.5), channel_id=1, source_target_pairs={{0,4},{4,0},{1,5},{5,1},{2,6},{6,2},{3,7},{7,3},{8,12},{12,8},{9,1... | collective-permute-start | bytes 1769480 | tf_op jit(solution)/shard_map/ppermute | solution.py:1081
  388.0 52.5 %collective-permute-start.33 = (bf16[36,128,128]{2,1,0:T(8,128)(2,1)S(1)}, bf16[36,128,128]{2,1,0:T(8,128)(2,1)S(1)}, u32[]{:S(2)}, u32[]{:S(2)}) collective-permute-start(bf16[36,128,128]{2,1,0:T(8,128)(2,1)S(1)} %pad_maximum_fusion.1), channel_id=1, source_target_pairs={{0,16},{16,0},{1,17},{17,1},{2,18},{18,2},{3,19},{19,3},{4,20},{20... | collective-permute-start | bytes 3538952 | tf_op jit(solution)/shard_map/ppermute | solution.py:1077
  389.1 51.4 %collective-permute-start.32 = (bf16[36,128,128]{2,1,0:T(8,128)(2,1)S(1)}, bf16[36,128,128]{2,1,0:T(8,128)(2,1)S(1)}, u32[]{:S(2)}, u32[]{:S(2)}) collective-permute-start(bf16[36,128,128]{2,1,0:T(8,128)(2,1)S(1)} %copy-done.48), channel_id=1, source_target_pairs={{0,4},{4,0},{1,5},{5,1},{2,6},{6,2},{3,7},{7,3},{8,12},{12,8},{9,1... | collective-permute-start | bytes 3538952 | tf_op jit(solution)/shard_map/ppermute | solution.py:1081
  390.4 37.5 %collective-permute-start.34 = (f32[15,768]{1,0:T(8,128)S(1)}, f32[15,768]{1,0:T(8,128)S(1)}, u32[]{:S(2)}, u32[]{:S(2)}) collective-permute-start(f32[15,768]{1,0:T(8,128)S(1)} %add_add_fusion), channel_id=1, source_target_pairs={{0,4},{4,0},{1,5},{5,1},{2,6},{6,2},{3,7},{7,3},{8,12},{12,8},{9,1... | collective-permute-start | bytes 138248 | tf_op jit(solution)/shard_map/ppermute | solution.py:1081
  443.0 32.8 %all-to-all-start.8 = ((bf16[4,768,192]{1,2,0:T(8,128)(2,1)}), bf16[4,768,192]{1,2,0:T(8,128)(2,1)S(1)}, u32[]{:S(2)}, u32[]{:S(2)}) async-start(bf16[4,768,192]{1,2,0:T(8,128)(2,1)} %convert_bitcast_fusion), calls=%async_computation.8 | async-start | bytes 2359296 | tf_op jit(solution)/shard_map/all_to_all | solution.py:1196
  446.7 28.0 %collective-permute-start.35 = (bf16[4,384,384]{2,1,0:T(8,128)(2,1)S(1)}, bf16[4,384,384]{2,1,0:T(8,128)(2,1)S(1)}, u32[]{:S(2)}, u32[]{:S(2)}) collective-permute-start(bf16[4,384,384]{2,1,0:T(8,128)(2,1)S(1)} %copy-done.49), channel_id=1, source_target_pairs={{0,4},{4,0},{1,5},{5,1},{2,6},{6,2},{3,7},{7,3},{8,12},{12,8},{9,1... | collective-permute-start | bytes 3538952 | tf_op jit(solution)/shard_map/ppermute | solution.py:1077
  482.7 45.3 %all-to-all-start.9 = ((bf16[4,384,576]{1,2,0:T(8,128)(2,1)}), bf16[4,384,576]{1,2,0:T(8,128)(2,1)S(1)}, u32[]{:S(2)}, u32[]{:S(2)}) async-start(bf16[4,384,576]{1,2,0:T(8,128)(2,1)} %copy.66), calls=%async_computation.9 | async-start | bytes 3538944 | tf_op jit(solution)/shard_map/all_to_all | solution.py:1196
  501.1 50.9 %collective-permute-start.50 = (bf16[36,128,128]{2,1,0:T(8,128)(2,1)}, bf16[36,128,128]{2,1,0:T(8,128)(2,1)}, u32[]{:S(2)}, u32[]{:S(2)}) collective-permute-start(bf16[36,128,128]{2,1,0:T(8,128)(2,1)} %add_convert_fusion), channel_id=1, source_target_pairs={{0,8},{8,0},{1,9},{9,1},{2,10},{10,2},{3,11},{11,3},{4,12},{12,4},... | collective-permute-start | bytes 3538952 | tf_op jit(solution)/shard_map/ppermute | solution.py:1081
  536.2 38.5 %collective-permute-start.47 = (bf16[256,576]{1,0:T(8,128)(2,1)S(1)}, bf16[256,576]{1,0:T(8,128)(2,1)S(1)}, u32[]{:S(2)}, u32[]{:S(2)}) collective-permute-start(bf16[256,576]{1,0:T(8,128)(2,1)S(1)} %add_convert_fusion.7.refs_0_), channel_id=1, source_target_pairs={{0,8},{8,0},{16,24},{24,16},{1,9},{9,1},{17,25},{25,17},{2,10},{10... | collective-permute-start | bytes 884744 | tf_op jit(solution)/shard_map/ppermute | solution.py:1081
  536.3 38.4 %collective-permute-start.48 = (bf16[256,576]{1,0:T(8,128)(2,1)S(1)}, bf16[256,576]{1,0:T(8,128)(2,1)S(1)}, u32[]{:S(2)}, u32[]{:S(2)}) collective-permute-start(bf16[256,576]{1,0:T(8,128)(2,1)S(1)} %add_convert_fusion.7.refs_0_), channel_id=1, source_target_pairs={{0,16},{8,24},{16,0},{24,8},{1,17},{9,25},{17,1},{25,9},{2,18},{10... | collective-permute-start | bytes 884744 | tf_op jit(solution)/shard_map/ppermute | solution.py:1081
  538.3 36.4 %collective-permute-start.49 = (bf16[256,576]{1,0:T(8,128)(2,1)S(1)}, bf16[256,576]{1,0:T(8,128)(2,1)S(1)}, u32[]{:S(2)}, u32[]{:S(2)}) collective-permute-start(bf16[256,576]{1,0:T(8,128)(2,1)S(1)} %add_convert_fusion.7.refs_0_), channel_id=1, source_target_pairs={{0,24},{8,16},{16,8},{24,0},{1,25},{9,17},{17,9},{25,1},{2,26},{10... | collective-permute-start | bytes 884744 | tf_op jit(solution)/shard_map/ppermute | solution.py:1081
  (83 other events, 1522.0 us)

commit v2 on v1

--- a/solution.py
+++ b/solution.py
@@ -1416,10 +1416,8 @@
         kept_next = over_c(tie((kept_next, given_c))[0])
         given_c = over_c(given_c)
         early = jnp.concatenate([router_local, second_gain_grad[None], const_grad], axis=0)
-        early = direct_sum(early, "f", f_size)
-        early = direct_sum(early, ("a", "b"), HEAD_GROUPS)
-        attended_grad, given_b, given_c, kept_next, early = tie(
-            (attended_grad, given_b, given_c, kept_next, early)
+        attended_grad, given_b, given_c, kept_next = tie(
+            (attended_grad, given_b, given_c, kept_next)
         )
         kept_b = over_b((kept_far.astype(F32) + kept_next.astype(F32)).astype(LOW))
         taken = jnp.concatenate(
@@ -1431,10 +1429,14 @@
         )
         taken = shifted(taken.astype(LOW), "a", 2, 1)
         kept_near = over_c(tie((kept_near, attended_grad))[0])
-        early = direct_sum(early, "c", c_size)
+        early = direct_sum(tie((early, attended_grad))[0], "f", f_size)
     back_outs = attend_back(kpb, ends, queries, pairs, attended_grad, raw, lse)
     if by_panels:
-        *back_outs, kept_near, taken, early = tie((*back_outs, kept_near, taken, early))
+        sent_outs = back_outs
+        *back_outs, kept_near, taken, kept_b, early = tie(
+            (*back_outs, kept_near, taken, kept_b, early)
+        )
+        early = direct_sum(early, ("a", "b"), HEAD_GROUPS)
         middle_late = tie((middle_low, back_outs[0]))[0]
         output_panels = jnp.einsum(
             "hrj,rd->hdj", by_heads, middle_late, preferred_element_type=F32
@@ -1450,17 +1452,39 @@
         first_all = first_all.reshape(-1, D)
     query_grad, pair_grad = back_outs[:2]
     for step in range(1, c_size):
-        pair_grad = pair_grad + shifted(back_outs[1 + step], "c", c_size, -step).astype(F32)
+        sent = sent_outs if by_panels else back_outs
+        pair_grad = pair_grad + shifted(sent[1 + step], "c", c_size, -step).astype(F32)
     group_grad = jnp.concatenate([query_grad, pair_grad.astype(LOW)], axis=2)
     if by_panels:
         group_grad, output_panels, first_all, early, *expert_outs = tie(
             (group_grad, output_panels, first_all, early, *expert_outs)
         )
+    sent_grad = group_grad
     if by_panels:
         panels = dot(first_all, group_grad.reshape(-1, 3 * GROUP_WIDTH), 0, 0).astype(LOW)
-        group_grad, panels = tie((group_grad, panels))
+        panels = panels.reshape(3, D // 3, 3 * GROUP_WIDTH)
+        output_panels = jnp.sum(output_panels.astype(F32), axis=0).astype(LOW)
+        output_panels = (
+            output_panels.reshape(3, D // 3, GROUP_WIDTH)
+            .transpose(1, 0, 2)
+            .reshape(1, D // 3, 3 * GROUP_WIDTH)
+        )
+        panels = jnp.concatenate([panels, output_panels], axis=0)
+        own_panels = [
+            lax.dynamic_index_in_dim(panels, f_place ^ step, 0, False) for step in range(f_size)
+        ]
+        sent_grad, *own_panels = tie((sent_grad, *own_panels))
+        summed = own_panels[0].astype(F32)
+        for step in range(1, f_size):
+            summed = summed + crossed(own_panels[step], "f", f_size, step).astype(F32)
+        summed = summed.astype(LOW)
+        summed = (summed.astype(F32) + crossed(summed, "c", 2, 1).astype(F32)).astype(LOW)
+        early = direct_sum(early, "c", c_size)
+    project_grad = over_groups(sent_grad)
+    if by_panels:
+        project_grad = tie((project_grad, summed))[0]
     project_grad = (
-        over_groups(group_grad)
+        project_grad
         .reshape(HEAD_GROUPS, rows, 3, GROUP_WIDTH)
         .transpose(1, 2, 0, 3)
         .reshape(rows, 3 * D)
@@ -1479,29 +1503,13 @@
 
     attn_stats = (attn_weights, attn_left, attn_right, attn_left_root, attn_right_root)
     if by_panels:
-        panels = panels.reshape(3, D // 3, 3 * GROUP_WIDTH)
-        output_panels = jnp.sum(output_panels.astype(F32), axis=0).astype(LOW)
-        output_panels = (
-            output_panels.reshape(3, D // 3, GROUP_WIDTH)
-            .transpose(1, 0, 2)
-            .reshape(1, D // 3, 3 * GROUP_WIDTH)
-        )
-        panels = jnp.concatenate([panels, output_panels], axis=0)
-        own_panels = [
-            lax.dynamic_index_in_dim(panels, f_place ^ step, 0, False) for step in range(f_size)
-        ]
-        summed = own_panels[0].astype(F32)
-        for step in range(1, f_size):
-            summed = summed + crossed(own_panels[step], "f", f_size, step).astype(F32)
-        summed = summed.astype(LOW)
         kept = [kept, kept_near, kept_b]
-        summed = (summed.astype(F32) + crossed(summed, "c", 2, 1).astype(F32)).astype(LOW)
         group_panels = [
             crossed(summed, ("a", "b"), HEAD_GROUPS, step) for step in range(1, HEAD_GROUPS)
         ]
         kept[0] = tie((kept[0], summed))[0]
         expert_outs = shampoo_half(half, kept, expert_stats, expert_outs)
-        late, early, *joined = tie((late, early, *group_panels, *expert_outs))
+        late, *joined = tie((late, *group_panels, *expert_outs))
         group_panels, expert_outs = joined[: HEAD_GROUPS - 1], joined[HEAD_GROUPS - 1 :]
         turn = (f_place == 3).astype(jnp.int32).reshape(1)
         attn_outs = shampoo_panel(

time: 605 us -> 611 us (level)
  local copies, waits for them, and re-layouts: 35.5 us -> 47.7 us
  waiting for transfers between devices: 214 us -> 205 us
    ppermute x5, waiting for transfers between devices: 31.1 us -> 18.5 us  [shifted(): lax.ppermute(values, axis, [(i, (i + distance) % size) for i in range(siz...]
  transfers between devices with their start and end apart: 61 -> 61, of which waited for: 27 -> 26; matrix products, arithmetic and copies ran while one was open for 11% -> 12% of each run, Pallas kernels for 26% -> 26%
where the time goes in v2:
time: 611 us; the launch traced here: 601 us
  waiting for transfers between devices  205 us (34%)
  Pallas kernels  172 us (28%)
  starting transfers between devices  104 us (17%)
  local copies, waits for them, and re-layouts  47.7 us (8%)
  matrix products  34.8 us (6%)
  other arithmetic  31.9 us (5%)
    ppermute x46, waiting for transfers between devices, crossed(): return lax.ppermute(values, axes, [(i, i ^ distance) for i in range(size)])  131 us
    ppermute x46, starting transfers between devices, crossed(): return lax.ppermute(values, axes, [(i, i ^ distance) for i in range(size)])  50.1 us
    all_to_all x6, waiting for transfers between devices, over_groups(): lax.all_to_all(values, ('a', 'b'), split_axis=0, concat_axis=0, tiled=True)  40.2 us
    pallas_call x1, Pallas kernels, attend_back(): pl.pallas_call(functools.partial(attend_back_kernel, len(pairs), block_ro...  37.7 us
    pallas_call x2, Pallas kernels, shampoo_half(): pl.pallas_call(kernel, grid_spec=pltpu.PrefetchScalarGridSpec(num_scalar_...  26.7 us
    pallas_call x2, Pallas kernels, expert_half_grads(): pl.pallas_call(kernel, grid=(hidden_blocks // 2,), in_specs=[smem_spec(),...  24.3 us
    all_to_all x6, starting transfers between devices, over_groups(): lax.all_to_all(values, ('a', 'b'), split_axis=0, concat_axis=0, tiled=True)  24.1 us
    dot_general x9, matrix products, dot(): lax.dot_general(left, right, (((left_dim,), (right_dim,)), ((), ())), pre...  20.5 us
  transfers between devices with their start and end apart: 61, of which 26 were waited for; matrix products, arithmetic and copies ran while one was open for 12% of the time, Pallas kernels for 26%

profile of v2, /device:TPU:0, one launch (start us, length us, event | category | flops | bytes accessed | tf_op | source)
XLA Modules:
  0.0 600.9 jit_solution(3516449709820302833)
XLA Ops:
  22.9 13.6 %collective-permute-done.3.refs_2_ = bf16[18,128,128]{2,1,0:T(8,128)(2,1)} collective-permute-done((bf16[18,128,128]{2,1,0:T(8,128)(2,1)}, bf16[18,128,128]{2,1,0:T(8,128)(2,1)}, u32[]{:S(2)}, u32[]{:S(2)}) %collective-permute-start.3) | collective-permute-done | bytes 589856 | tf_op jit(solution)/shard_map/ppermute | solution.py:1081
  42.8 8.9 %project.1 = (bf16[384,768]{1,0:T(8,128)(2,1)}, f32[384,1]{1,0:T(8,128)}, bf16[4,192,384]{2,1,0:T(8,128)(2,1)}, bf16[4,384,384]{2,1,0:T(8,128)(2,1)}, bf16[3,256,2304]{2,1,0:T(8,128)(2,1)}) custom-call(s32[4]{0:T(128)} %pad_add_fusion.2.places_ref, f32[384,768]{1,0:T(8,128)} %rows_ref.1, f32[1,768]{1,0:T(1,128)} %get-tuple-element.319.gain_ref, ...), custom_call_target="tpu_custom_call" | custom-call | flops 589824 | bytes 1000000 | tf_op jit(solution)/shard_map/project/pallas_call | solution.py:143
  51.7 4.4 collective-permute-done.6
  64.5 30.4 %collective-permute-done.7.refs_3_ = bf16[18,128,128]{2,1,0:T(8,128)(2,1)S(1)} collective-permute-done((bf16[18,128,128]{2,1,0:T(8,128)(2,1)S(1)}, bf16[18,128,128]{2,1,0:T(8,128)(2,1)S(1)}, u32[]{:S(2)}, u32[]{:S(2)}) %collective-permute-start.7) | collective-permute-done | bytes 589856 | tf_op jit(solution)/shard_map/ppermute | solution.py:1081
  105.0 17.8 %all-to-all-done.refs_2_ = bf16[4,192,384]{2,1,0:T(8,128)(2,1)S(1)} async-done(((bf16[4,192,384]{2,1,0:T(8,128)(2,1)}), bf16[4,192,384]{2,1,0:T(8,128)(2,1)S(1)}, u32[]{:S(2)}, u32[]{:S(2)}) %all-to-all-start) | async-done | bytes 589856 | tf_op jit(solution)/shard_map/all_to_all | solution.py:1196
  122.8 5.4 collective-permute-done.11
  134.2 20.1 %attend_forward.1 = (f32[4,384,192]{2,1,0:T(8,128)}, bf16[4,192,384]{2,1,0:T(8,128)(2,1)}, f32[16,288,1]{2,1,0:T(8,128)}) custom-call(s32[2,16]{1,0:T(2,128)} %pad_add_fusion.refs_0_, s32[4]{0:T(128)} %bitcast.204, bf16[4,192,384]{2,1,0:T(8,128)(2,1)} %copy-done.8, bf16[4,384,384]{2,1,0:T(8,128)(2,1)} %copy-done.5, bf16[4,384,384]{2,1,0:T(8,128)(2,1)} %copy-done.14), custom_call_target="tpu_custom_call" | custom-call | flops 98304 | bytes 1000000 | tf_op jit(solution)/shard_map/attend_forward/pallas_call | solution.py:382
  166.6 8.7 %all-to-all-done.2 = bf16[4,192,384]{2,1,0:T(8,128)(2,1)S(1)} async-done(((bf16[4,192,384]{2,1,0:T(8,128)(2,1)}), bf16[4,192,384]{2,1,0:T(8,128)(2,1)S(1)}, u32[]{:S(2)}, u32[]{:S(2)}) %all-to-all-start.2) | async-done | bytes 589856 | tf_op jit(solution)/shard_map/all_to_all | solution.py:1196
  187.2 4.6 all-to-all-start.4
  197.1 21.2 %collective-permute-done.17 = bf16[384,768]{1,0:T(8,128)(2,1)} collective-permute-done((bf16[384,768]{1,0:T(8,128)(2,1)}, bf16[384,768]{1,0:T(8,128)(2,1)}, u32[]{:S(2)}, u32[]{:S(2)}) %collective-permute-start.17) | collective-permute-done | bytes 589856 | tf_op jit(solution)/shard_map/ppermute | solution.py:1081
  222.7 4.8 all-to-all-start.3
  227.5 19.1 %expert_forward.1 = (bf16[768,768]{1,0:T(8,128)(2,1)}, f32[768,2048]{1,0:T(8,128)}, f32[768,2048]{1,0:T(8,128)}, bf16[768,2048]{1,0:T(8,128)(2,1)}) custom-call(s32[14]{0:T(128)} %stack.103.places_ref, bf16[768,768]{1,0:T(8,128)(2,1)} %bitcast.34.rows_ref, bf16[36,128,128]{2,1,0:T(8,128)(2,1)} %bitcast.181, ...), custom_call_target="tpu_custom_call" | custom-call | flops 7247757312 | bytes 11796480 | tf_op jit(solution)/shard_map/expert_forward/pallas_call | solution.py:649
  246.7 10.4 %all-to-all-done.3 = bf16[8,96,768]{2,1,0:T(8,128)(2,1)} async-done(((bf16[8,96,768]{2,1,0:T(8,128)(2,1)}), bf16[8,96,768]{2,1,0:T(8,128)(2,1)}, u32[]{:S(2)}, u32[]{:S(2)}) %all-to-all-start.3) | async-done | bytes 1179680 | tf_op jit(solution)/shard_map/all_to_all | solution.py:1171
  257.0 4.3 all-to-all-start.5
  261.4 20.2 %expert_row_grads.1 = (bf16[768,768]{1,0:T(8,128)(2,1)}, bf16[768,2048]{1,0:T(8,128)(2,1)}, bf16[768,2048]{1,0:T(8,128)(2,1)}) custom-call(s32[14]{0:T(128)} %stack.103.places_ref, bf16[768,768]{1,0:T(8,128)(2,1)} %bitcast.32.grads_ref, f32[768,2048]{1,0:T(8,128)} %get-tuple-element.190.gate_i, f32[768,2048]{1,0:T(8,128)} %get-tuple-element.191.up_i, ...), custom_call_target="tpu_custom_call" | custom-call | flops 7247757312 | bytes 22413312 | tf_op jit(solution)/shard_map/expert_row_grads/pallas_call | solution.py:720
  281.6 12.2 %expert_half_grads.2 = (bf16[36,128,128]{2,1,0:T(8,128)(2,1)}, bf16[36,128,128]{2,1,0:T(8,128)(2,1)}, bf16[36,128,128]{2,1,0:T(8,128)(2,1)}, bf16[18,128,128]{2,1,0:T(8,128)(2,1)}, bf16[18,128,128]{2,1,0:T(8,128)(2,1)}) custom-call(s32[1]{0:T(128)S(6)} %sub.58.which_ref.half_ref, s32[7]{0:T(128)} %stack.111.places_ref, bf16[768,768]{1,0:T(8,128)(2,1)} %bitcast.34.rows_ref, ...), custom_call_target="tpu_custom_call" | custom-call | flops 3623878656 | bytes 12976128 | tf_op jit(solution)/shard_map/expert_half_grads/pallas_call | solution.py:875
  293.8 5.2 all-to-all-start.6
  309.9 12.1 %expert_half_grads.3 = (bf16[36,128,128]{2,1,0:T(8,128)(2,1)}, bf16[36,128,128]{2,1,0:T(8,128)(2,1)}, bf16[36,128,128]{2,1,0:T(8,128)(2,1)}, bf16[36,128,128]{2,1,0:T(8,128)(2,1)}) custom-call(s32[1]{0:T(128)} %bitcast.36.which_ref.half_ref, s32[4]{0:T(128)} %get-tuple-element.203.places_ref, bf16[768,768]{1,0:T(8,128)(2,1)} %bitcast.34.rows_ref, ...), custom_call_target="tpu_custom_call" | custom-call | flops 3623878656 | bytes 12976128 | tf_op jit(solution)/shard_map/expert_half_grads/pallas_call | solution.py:875
  323.7 4.9 all-to-all-done.6
  333.7 7.5 %collective-permute-done.22 = bf16[36,128,128]{2,1,0:T(8,128)(2,1)} collective-permute-done((bf16[36,128,128]{2,1,0:T(8,128)(2,1)}, bf16[36,128,128]{2,1,0:T(8,128)(2,1)}, u32[]{:S(2)}, u32[]{:S(2)}) %collective-permute-start.22) | collective-permute-done | bytes 1179680 | tf_op jit(solution)/shard_map/ppermute | solution.py:1081
  350.9 5.4 all-to-all-start.7
  361.4 22.6 %collective-permute-done.24 = bf16[18,128,128]{2,1,0:T(8,128)(2,1)S(1)} collective-permute-done((bf16[18,128,128]{2,1,0:T(8,128)(2,1)}, bf16[18,128,128]{2,1,0:T(8,128)(2,1)S(1)}, u32[]{:S(2)}, u32[]{:S(2)}) %collective-permute-start.24) | collective-permute-done | bytes 589856 | tf_op jit(solution)/shard_map/ppermute | solution.py:1081
  398.6 37.7 %attend_backward.1 = (bf16[4,384,192]{2,1,0:T(8,128)(2,1)}, f32[4,384,384]{2,1,0:T(8,128)}, bf16[4,384,384]{2,1,0:T(8,128)(2,1)}) custom-call(s32[2,16]{1,0:T(2,128)} %pad_add_fusion.refs_0_, s32[4]{0:T(128)} %bitcast.205, bf16[4,192,384]{2,1,0:T(8,128)(2,1)} %copy-done.8, bf16[4,384,384]{2,1,0:T(8,128)(2,1)} %copy-done.5, bf16[4,384,384]{2,1,0:T(8,128)(2,1)} %copy-done.14, ...), custom_call_target="tpu_custom_call" | custom-call | flops 98304 | bytes 1000000 | tf_op jit(solution)/shard_map/attend_backward/pallas_call | solution.py:543
  437.6 6.6 %collective-permute-done.27.refs_0_ = bf16[36,128,128]{2,1,0:T(8,128)(2,1)} collective-permute-done((bf16[36,128,128]{2,1,0:T(8,128)(2,1)}, bf16[36,128,128]{2,1,0:T(8,128)(2,1)}, u32[]{:S(2)}, u32[]{:S(2)}) %collective-permute-start.27) | collective-permute-done | bytes 1179680 | tf_op jit(solution)/shard_map/ppermute | solution.py:1077
  454.3 13.2 %shampoo_half.2 = (f32[72,128,128]{2,1,0:T(8,128)}, f32[72,128,128]{2,1,0:T(8,128)}, f32[72,128,128]{2,1,0:T(8,128)}, f32[72,128,128]{2,1,0:T(8,128)}) custom-call(s32[1]{0:T(128)S(6)} %sub.58.which_ref.half_ref, bf16[36,128,128]{2,1,0:T(8,128)(2,1)} %collective-permute-done.27.refs_0_, bf16[72,128,128]{2,1,0:T(8,128)(2,1)} %bitcast.163, ...), custom_call_target="tpu_custom_call" | custom-call | flops 1811939328 | bytes 21233664 | tf_op jit(solution)/shard_map/shampoo_half/pallas_call | solution.py:936
  511.1 4.5 collective-permute-done.37
  515.6 6.5 %collective-permute-done.38 = bf16[256,576]{1,0:T(8,128)(2,1)} collective-permute-done((bf16[256,576]{1,0:T(8,128)(2,1)S(1)}, bf16[256,576]{1,0:T(8,128)(2,1)}, u32[]{:S(2)}, u32[]{:S(2)}) %collective-permute-start.38) | collective-permute-done | bytes 294944 | tf_op jit(solution)/shard_map/ppermute | solution.py:1081
  526.9 6.5 %collective-permute-done.39 = bf16[256,576]{1,0:T(8,128)(2,1)S(1)} collective-permute-done((bf16[256,576]{1,0:T(8,128)(2,1)S(1)}, bf16[256,576]{1,0:T(8,128)(2,1)S(1)}, u32[]{:S(2)}, u32[]{:S(2)}) %collective-permute-start.39) | collective-permute-done | bytes 294944 | tf_op jit(solution)/shard_map/ppermute | solution.py:1081
  533.5 9.7 %all-to-all-done.9 = bf16[4,384,576]{1,2,0:T(8,128)(2,1)S(1)} async-done(((bf16[4,384,576]{1,2,0:T(8,128)(2,1)}), bf16[4,384,576]{1,2,0:T(8,128)(2,1)S(1)}, u32[]{:S(2)}, u32[]{:S(2)}) %all-to-all-start.9) | async-done | bytes 1769504 | tf_op jit(solution)/shard_map/all_to_all | solution.py:1196
  557.7 13.6 %shampoo_half.3 = (f32[72,128,128]{2,1,0:T(8,128)}, f32[72,128,128]{2,1,0:T(8,128)}, f32[72,128,128]{2,1,0:T(8,128)}, f32[72,128,128]{2,1,0:T(8,128)}) custom-call(s32[1]{0:T(128)} %bitcast.36.which_ref.half_ref, bf16[36,128,128]{2,1,0:T(8,128)(2,1)} %get-tuple-element.257.refs_0_, ...), custom_call_target="tpu_custom_call", output_to_operand_aliasing={{0}: (9, {}), {1}: (10, {}), {2}: (11, {}), {3}: (12, {})} | custom-call | flops 1811939328 | bytes 23592960 | tf_op jit(solution)/shard_map/shampoo_half/pallas_call | solution.py:936
  577.9 6.8 %collective-permute-done.45 = f32[1,768]{1,0:T(1,128)S(1)} collective-permute-done((f32[1,768]{1,0:T(1,128)S(1)}, f32[1,768]{1,0:T(1,128)S(1)}, u32[]{:S(2)}, u32[]{:S(2)}) %collective-permute-start.45) | collective-permute-done | bytes 3104 | tf_op jit(solution)/shard_map/ppermute | solution.py:1081
  585.7 14.9 %shampoo_panel.1 = (f32[36,128,128]{2,1,0:T(8,128)}, f32[36,128,128]{2,1,0:T(8,128)}, f32[36,128,128]{2,1,0:T(8,128)}, f32[36,128,128]{2,1,0:T(8,128)}) custom-call(s32[1]{0:T(128)} %bitcast.72.turn_ref, s32[4]{0:T(128)} %get-tuple-element.270.places_ref, bf16[256,576]{1,0:T(8,128)(2,1)} %copy-done.23, bf16[256,576]{1,0:T(8,128)(2,1)} %copy-done.32, ...), custom_call_target="tpu_custom_call" | custom-call | flops 1811939328 | bytes 22413312 | tf_op jit(solution)/shard_map/shampoo_panel/pallas_call | solution.py:1041
  (328 shorter events, 211.7 us)
Async XLA Ops:
  0.7 38.1 %collective-permute-start = (bf16[36,128,128]{2,1,0:T(8,128)(2,1)}, bf16[36,128,128]{2,1,0:T(8,128)(2,1)}, u32[]{:S(2)}, u32[]{:S(2)}) collective-permute-start(bf16[36,128,128]{2,1,0:T(8,128)(2,1)} %refs_4_.1), channel_id=1, source_target_pairs={{0,2},{1,3},{2,0},{3,1},{4,6},{5,7},{6,4},{7,5},{8,10},{9,11},{10,... | collective-permute-start | bytes 3538952 | tf_op jit(solution)/shard_map/ppermute | solution.py:1081
  3.7 37.4 %collective-permute-start.4 = (bf16[36,128,128]{2,1,0:T(8,128)(2,1)}, bf16[36,128,128]{2,1,0:T(8,128)(2,1)}, u32[]{:S(2)}, u32[]{:S(2)}) collective-permute-start(bf16[36,128,128]{2,1,0:T(8,128)(2,1)} %refs_4_.1), channel_id=1, source_target_pairs={{0,1},{1,0},{2,3},{3,2},{4,5},{5,4},{6,7},{7,6},{8,9},{9,8},{10,11... | collective-permute-start | bytes 3538952 | tf_op jit(solution)/shard_map/ppermute | solution.py:1081
  5.5 33.3 %collective-permute-start.1 = (bf16[36,128,128]{2,1,0:T(8,128)(2,1)S(1)}, bf16[36,128,128]{2,1,0:T(8,128)(2,1)}, u32[]{:S(2)}, u32[]{:S(2)}) collective-permute-start(bf16[36,128,128]{2,1,0:T(8,128)(2,1)S(1)} %bitcast.180), channel_id=1, source_target_pairs={{0,4},{4,0},{1,5},{5,1},{2,6},{6,2},{3,7},{7,3},{8,12},{12,8},{9,1... | collective-permute-start | bytes 3538952 | tf_op jit(solution)/shard_map/ppermute | solution.py:1081
  8.1 28.4 %collective-permute-start.3 = (bf16[18,128,128]{2,1,0:T(8,128)(2,1)}, bf16[18,128,128]{2,1,0:T(8,128)(2,1)}, u32[]{:S(2)}, u32[]{:S(2)}) collective-permute-start(bf16[18,128,128]{2,1,0:T(8,128)(2,1)} %get-tuple-element.318), channel_id=1, source_target_pairs={{0,8},{8,0},{1,9},{9,1},{2,10},{10,2},{3,11},{11,3},{4,12},{12,4},... | collective-permute-start | bytes 1769480 | tf_op jit(solution)/shard_map/ppermute | solution.py:1081
  9.8 28.9 %collective-permute-start.2 = (bf16[18,128,128]{2,1,0:T(8,128)(2,1)S(1)}, bf16[18,128,128]{2,1,0:T(8,128)(2,1)}, u32[]{:S(2)}, u32[]{:S(2)}) collective-permute-start(bf16[18,128,128]{2,1,0:T(8,128)(2,1)S(1)} %slice_bitcast_fusion.2), channel_id=1, source_target_pairs={{0,16},{16,0},{1,17},{17,1},{2,18},{18,2},{3,19},{19,3},{4,20},{20... | collective-permute-start | bytes 1769480 | tf_op jit(solution)/shard_map/ppermute | solution.py:1077
  56.8 39.2 %all-to-all-start.1 = ((bf16[4,384,384]{2,1,0:T(8,128)(2,1)}), bf16[4,384,384]{2,1,0:T(8,128)(2,1)S(1)}, u32[]{:S(2)}, u32[]{:S(2)}) async-start(bf16[4,384,384]{2,1,0:T(8,128)(2,1)} %get-tuple-element.155), calls=%async_computation.1 | async-start | bytes 2359296 | tf_op jit(solution)/shard_map/all_to_all | solution.py:1196
  60.5 34.4 %collective-permute-start.7 = (bf16[18,128,128]{2,1,0:T(8,128)(2,1)S(1)}, bf16[18,128,128]{2,1,0:T(8,128)(2,1)S(1)}, u32[]{:S(2)}, u32[]{:S(2)}) collective-permute-start(bf16[18,128,128]{2,1,0:T(8,128)(2,1)S(1)} %copy-done.30), channel_id=1, source_target_pairs={{0,8},{8,0},{1,9},{9,1},{2,10},{10,2},{3,11},{11,3},{4,12},{12,4},... | collective-permute-start | bytes 1769480 | tf_op jit(solution)/shard_map/ppermute | solution.py:1081
  62.5 32.5 %collective-permute-start.8 = (bf16[18,128,128]{2,1,0:T(8,128)(2,1)}, bf16[18,128,128]{2,1,0:T(8,128)(2,1)S(1)}, u32[]{:S(2)}, u32[]{:S(2)}) collective-permute-start(bf16[18,128,128]{2,1,0:T(8,128)(2,1)} %collective-permute-done.3.refs_2_), channel_id=1, source_target_pairs={{0,4},{4,0},{1,5},{5,1},{2,6},{6,2},{3,7},{7,3},{8,12},{12,8},{9,1... | collective-permute-start | bytes 1769480 | tf_op jit(solution)/shard_map/ppermute | solution.py:1081
  63.0 31.9 %collective-permute-start.9 = (bf16[18,128,128]{2,1,0:T(8,128)(2,1)}, bf16[18,128,128]{2,1,0:T(8,128)(2,1)}, u32[]{:S(2)}, u32[]{:S(2)}) collective-permute-start(bf16[18,128,128]{2,1,0:T(8,128)(2,1)} %collective-permute-done.2.refs_6_), channel_id=1, source_target_pairs={{0,4},{4,0},{1,5},{5,1},{2,6},{6,2},{3,7},{7,3},{8,12},{12,8},{9,1... | collective-permute-start | bytes 1769480 | tf_op jit(solution)/shard_map/ppermute | solution.py:1081
  96.0 32.1 %collective-permute-start.10 = (bf16[4,384,384]{2,1,0:T(8,128)(2,1)S(1)}, bf16[4,384,384]{2,1,0:T(8,128)(2,1)S(1)}, u32[]{:S(2)}, u32[]{:S(2)}) collective-permute-start(bf16[4,384,384]{2,1,0:T(8,128)(2,1)S(1)} %all-to-all-done.1.refs_3_), channel_id=1, source_target_pairs={{0,4},{4,0},{1,5},{5,1},{2,6},{6,2},{3,7},{7,3},{8,12},{12,8},{9,1... | collective-permute-start | bytes 3538952 | tf_op jit(solution)/shard_map/ppermute | solution.py:1081
  187.2 35.6 %all-to-all-start.4 = ((bf16[8,96,768]{2,1,0:T(8,128)(2,1)}), bf16[8,96,768]{2,1,0:T(8,128)(2,1)}, u32[]{:S(2)}, u32[]{:S(2)}) async-start(bf16[8,96,768]{2,1,0:T(8,128)(2,1)} %bitcast.198), calls=%async_computation.4 | async-start | bytes 2359296 | tf_op jit(solution)/shard_map/all_to_all | solution.py:1171
  222.7 34.3 %all-to-all-start.3 = ((bf16[8,96,768]{2,1,0:T(8,128)(2,1)}), bf16[8,96,768]{2,1,0:T(8,128)(2,1)}, u32[]{:S(2)}, u32[]{:S(2)}) async-start(bf16[8,96,768]{2,1,0:T(8,128)(2,1)} %bitcast.183), calls=%async_computation.3 | async-start | bytes 2359296 | tf_op jit(solution)/shard_map/all_to_all | solution.py:1171
  257.0 36.8 %all-to-all-start.5 = ((bf16[8,96,768]{2,1,0:T(8,128)(2,1)}), bf16[8,96,768]{2,1,0:T(8,128)(2,1)}, u32[]{:S(2)}, u32[]{:S(2)}) async-start(bf16[8,96,768]{2,1,0:T(8,128)(2,1)} %bitcast.197), calls=%async_computation.5 | async-start | bytes 2359296 | tf_op jit(solution)/shard_map/all_to_all | solution.py:1175
  261.3 32.5 %collective-permute-start.20 = (bf16[384,768]{1,0:T(8,128)(2,1)}, bf16[384,768]{1,0:T(8,128)(2,1)}, u32[]{:S(2)}, u32[]{:S(2)}) collective-permute-start(bf16[384,768]{1,0:T(8,128)(2,1)} %collective-permute-done.12), channel_id=1, source_target_pairs={{0,8},{8,0},{1,9},{9,1},{2,10},{10,2},{3,11},{11,3},{4,12},{12,4},... | collective-permute-start | bytes 1769480 | tf_op jit(solution)/shard_map/ppermute | solution.py:1081
  293.8 34.8 %all-to-all-start.6 = ((bf16[8,96,768]{2,1,0:T(8,128)(2,1)}), bf16[8,96,768]{2,1,0:T(8,128)(2,1)}, u32[]{:S(2)}, u32[]{:S(2)}) async-start(bf16[8,96,768]{2,1,0:T(8,128)(2,1)} %bitcast.196), calls=%async_computation.6 | async-start | bytes 2359296 | tf_op jit(solution)/shard_map/all_to_all | solution.py:1175
  299.1 34.6 %collective-permute-start.21 = (bf16[36,128,128]{2,1,0:T(8,128)(2,1)}, bf16[36,128,128]{2,1,0:T(8,128)(2,1)}, u32[]{:S(2)}, u32[]{:S(2)}) collective-permute-start(bf16[36,128,128]{2,1,0:T(8,128)(2,1)} %get-tuple-element.210), channel_id=1, source_target_pairs={{0,4},{4,0},{1,5},{5,1},{2,6},{6,2},{3,7},{7,3},{8,12},{12,8},{9,1... | collective-permute-start | bytes 3538952 | tf_op jit(solution)/shard_map/ppermute | solution.py:1081
  300.6 40.5 %collective-permute-start.22 = (bf16[36,128,128]{2,1,0:T(8,128)(2,1)}, bf16[36,128,128]{2,1,0:T(8,128)(2,1)}, u32[]{:S(2)}, u32[]{:S(2)}) collective-permute-start(bf16[36,128,128]{2,1,0:T(8,128)(2,1)} %get-tuple-element.211), channel_id=1, source_target_pairs={{0,8},{8,0},{1,9},{9,1},{2,10},{10,2},{3,11},{11,3},{4,12},{12,4},... | collective-permute-start | bytes 3538952 | tf_op jit(solution)/shard_map/ppermute | solution.py:1081
  343.2 40.8 %collective-permute-start.25 = (bf16[36,128,128]{2,1,0:T(8,128)(2,1)}, bf16[36,128,128]{2,1,0:T(8,128)(2,1)}, u32[]{:S(2)}, u32[]{:S(2)}) collective-permute-start(bf16[36,128,128]{2,1,0:T(8,128)(2,1)} %get-tuple-element.216), channel_id=1, source_target_pairs={{0,4},{4,0},{1,5},{5,1},{2,6},{6,2},{3,7},{7,3},{8,12},{12,8},{9,1... | collective-permute-start | bytes 3538952 | tf_op jit(solution)/shard_map/ppermute | solution.py:1081
  350.9 33.1 %all-to-all-start.7 = ((bf16[4,192,384]{2,1,0:T(8,128)(2,1)}), bf16[4,192,384]{2,1,0:T(8,128)(2,1)S(1)}, u32[]{:S(2)}, u32[]{:S(2)}) async-start(bf16[4,192,384]{2,1,0:T(8,128)(2,1)} %reshape.355), calls=%async_computation.7 | async-start | bytes 1179648 | tf_op jit(solution)/shard_map/all_to_all | solution.py:1196
  387.4 50.2 %collective-permute-start.28 = (bf16[36,128,128]{2,1,0:T(8,128)(2,1)}, bf16[36,128,128]{2,1,0:T(8,128)(2,1)}, u32[]{:S(2)}, u32[]{:S(2)}) collective-permute-start(bf16[36,128,128]{2,1,0:T(8,128)(2,1)} %add_convert_fusion.1), channel_id=1, source_target_pairs={{0,8},{8,0},{1,9},{9,1},{2,10},{10,2},{3,11},{11,3},{4,12},{12,4},... | collective-permute-start | bytes 3538952 | tf_op jit(solution)/shard_map/ppermute | solution.py:1081
  390.5 53.6 %collective-permute-start.27 = (bf16[36,128,128]{2,1,0:T(8,128)(2,1)}, bf16[36,128,128]{2,1,0:T(8,128)(2,1)}, u32[]{:S(2)}, u32[]{:S(2)}) collective-permute-start(bf16[36,128,128]{2,1,0:T(8,128)(2,1)} %pad_maximum_fusion.1), channel_id=1, source_target_pairs={{0,16},{16,0},{1,17},{17,1},{2,18},{18,2},{3,19},{19,3},{4,20},{20... | collective-permute-start | bytes 3538952 | tf_op jit(solution)/shard_map/ppermute | solution.py:1077
  394.5 49.6 %collective-permute-start.26 = (bf16[36,128,128]{2,1,0:T(8,128)(2,1)}, bf16[36,128,128]{2,1,0:T(8,128)(2,1)S(1)}, u32[]{:S(2)}, u32[]{:S(2)}) collective-permute-start(bf16[36,128,128]{2,1,0:T(8,128)(2,1)} %get-tuple-element.224), channel_id=1, source_target_pairs={{0,4},{4,0},{1,5},{5,1},{2,6},{6,2},{3,7},{7,3},{8,12},{12,8},{9,1... | collective-permute-start | bytes 3538952 | tf_op jit(solution)/shard_map/ppermute | solution.py:1081
  396.2 40.2 %collective-permute-start.30 = (f32[15,768]{1,0:T(8,128)S(1)}, f32[15,768]{1,0:T(8,128)S(1)}, u32[]{:S(2)}, u32[]{:S(2)}) collective-permute-start(f32[15,768]{1,0:T(8,128)S(1)} %pad_maximum_fusion.2), channel_id=1, source_target_pairs={{0,2},{1,3},{2,0},{3,1},{4,6},{5,7},{6,4},{7,5},{8,10},{9,11},{10,... | collective-permute-start | bytes 138248 | tf_op jit(solution)/shard_map/ppermute | solution.py:1081
  397.7 39.3 %collective-permute-start.31 = (f32[15,768]{1,0:T(8,128)S(1)}, f32[15,768]{1,0:T(8,128)S(1)}, u32[]{:S(2)}, u32[]{:S(2)}) collective-permute-start(f32[15,768]{1,0:T(8,128)S(1)} %pad_maximum_fusion.2), channel_id=1, source_target_pairs={{0,3},{1,2},{2,1},{3,0},{4,7},{5,6},{6,5},{7,4},{8,11},{9,10},{10,... | collective-permute-start | bytes 138248 | tf_op jit(solution)/shard_map/ppermute | solution.py:1081
  436.3 37.2 %collective-permute-start.32 = (bf16[4,384,384]{2,1,0:T(8,128)(2,1)}, bf16[4,384,384]{2,1,0:T(8,128)(2,1)S(1)}, u32[]{:S(2)}, u32[]{:S(2)}) collective-permute-start(bf16[4,384,384]{2,1,0:T(8,128)(2,1)} %get-tuple-element.222), channel_id=1, source_target_pairs={{0,4},{4,0},{1,5},{5,1},{2,6},{6,2},{3,7},{7,3},{8,12},{12,8},{9,1... | collective-permute-start | bytes 3538952 | tf_op jit(solution)/shard_map/ppermute | solution.py:1077
  444.2 31.3 %collective-permute-start.33 = (f32[15,768]{1,0:T(8,128)}, f32[15,768]{1,0:T(8,128)}, u32[]{:S(2)}, u32[]{:S(2)}) collective-permute-start(f32[15,768]{1,0:T(8,128)} %add_add_fusion.1), channel_id=1, source_target_pairs={{0,8},{8,0},{16,24},{24,16},{1,9},{9,1},{17,25},{25,17},{2,10},{10... | collective-permute-start | bytes 138248 | tf_op jit(solution)/shard_map/ppermute | solution.py:1081
  444.2 31.3 %collective-permute-start.34 = (f32[15,768]{1,0:T(8,128)}, f32[15,768]{1,0:T(8,128)}, u32[]{:S(2)}, u32[]{:S(2)}) collective-permute-start(f32[15,768]{1,0:T(8,128)} %add_add_fusion.1), channel_id=1, source_target_pairs={{0,16},{8,24},{16,0},{24,8},{1,17},{9,25},{17,1},{25,9},{2,18},{10... | collective-permute-start | bytes 138248 | tf_op jit(solution)/shard_map/ppermute | solution.py:1081
  450.5 30.5 %all-to-all-start.8 = ((bf16[4,768,192]{1,2,0:T(8,128)(2,1)}), bf16[4,768,192]{1,2,0:T(8,128)(2,1)S(1)}, u32[]{:S(2)}, u32[]{:S(2)}) async-start(bf16[4,768,192]{1,2,0:T(8,128)(2,1)} %convert_bitcast_fusion), calls=%async_computation.8 | async-start | bytes 2359296 | tf_op jit(solution)/shard_map/all_to_all | solution.py:1196
  498.6 44.6 %all-to-all-start.9 = ((bf16[4,384,576]{1,2,0:T(8,128)(2,1)}), bf16[4,384,576]{1,2,0:T(8,128)(2,1)S(1)}, u32[]{:S(2)}, u32[]{:S(2)}) async-start(bf16[4,384,576]{1,2,0:T(8,128)(2,1)} %copy.69), calls=%async_computation.9 | async-start | bytes 3538944 | tf_op jit(solution)/shard_map/all_to_all | solution.py:1196
  552.5 32.2 %collective-permute-start.47 = (bf16[256,576]{1,0:T(8,128)(2,1)S(1)}, bf16[256,576]{1,0:T(8,128)(2,1)S(1)}, u32[]{:S(2)}, u32[]{:S(2)}) collective-permute-start(bf16[256,576]{1,0:T(8,128)(2,1)S(1)} %add_convert_fusion.7.refs_0_), channel_id=1, source_target_pairs={{0,8},{8,0},{16,24},{24,16},{1,9},{9,1},{17,25},{25,17},{2,10},{10... | collective-permute-start | bytes 884744 | tf_op jit(solution)/shard_map/ppermute | solution.py:1081
  552.5 32.3 %collective-permute-start.48 = (bf16[256,576]{1,0:T(8,128)(2,1)S(1)}, bf16[256,576]{1,0:T(8,128)(2,1)S(1)}, u32[]{:S(2)}, u32[]{:S(2)}) collective-permute-start(bf16[256,576]{1,0:T(8,128)(2,1)S(1)} %add_convert_fusion.7.refs_0_), channel_id=1, source_target_pairs={{0,16},{8,24},{16,0},{24,8},{1,17},{9,25},{17,1},{25,9},{2,18},{10... | collective-permute-start | bytes 884744 | tf_op jit(solution)/shard_map/ppermute | solution.py:1081
  554.5 30.3 %collective-permute-start.49 = (bf16[256,576]{1,0:T(8,128)(2,1)S(1)}, bf16[256,576]{1,0:T(8,128)(2,1)S(1)}, u32[]{:S(2)}, u32[]{:S(2)}) collective-permute-start(bf16[256,576]{1,0:T(8,128)(2,1)S(1)} %add_convert_fusion.7.refs_0_), channel_id=1, source_target_pairs={{0,24},{8,16},{16,8},{24,0},{1,25},{9,17},{17,9},{25,1},{2,26},{10... | collective-permute-start | bytes 884744 | tf_op jit(solution)/shard_map/ppermute | solution.py:1081
  (84 other events, 1496.8 us)

commit v3 on v2

--- a/solution.py
+++ b/solution.py
@@ -1416,8 +1416,10 @@
         kept_next = over_c(tie((kept_next, given_c))[0])
         given_c = over_c(given_c)
         early = jnp.concatenate([router_local, second_gain_grad[None], const_grad], axis=0)
-        attended_grad, given_b, given_c, kept_next = tie(
-            (attended_grad, given_b, given_c, kept_next)
+        early = direct_sum(early, "f", f_size)
+        early = direct_sum(early, ("a", "b"), HEAD_GROUPS)
+        attended_grad, given_b, given_c, kept_next, early = tie(
+            (attended_grad, given_b, given_c, kept_next, early)
         )
         kept_b = over_b((kept_far.astype(F32) + kept_next.astype(F32)).astype(LOW))
         taken = jnp.concatenate(
@@ -1429,14 +1431,10 @@
         )
         taken = shifted(taken.astype(LOW), "a", 2, 1)
         kept_near = over_c(tie((kept_near, attended_grad))[0])
-        early = direct_sum(tie((early, attended_grad))[0], "f", f_size)
     back_outs = attend_back(kpb, ends, queries, pairs, attended_grad, raw, lse)
     if by_panels:
         sent_outs = back_outs
-        *back_outs, kept_near, taken, kept_b, early = tie(
-            (*back_outs, kept_near, taken, kept_b, early)
-        )
-        early = direct_sum(early, ("a", "b"), HEAD_GROUPS)
+        *back_outs, kept_near, taken, kept_b = tie((*back_outs, kept_near, taken, kept_b))
         middle_late = tie((middle_low, back_outs[0]))[0]
         output_panels = jnp.einsum(
             "hrj,rd->hdj", by_heads, middle_late, preferred_element_type=F32
@@ -1456,12 +1454,14 @@
         pair_grad = pair_grad + shifted(sent[1 + step], "c", c_size, -step).astype(F32)
     group_grad = jnp.concatenate([query_grad, pair_grad.astype(LOW)], axis=2)
     if by_panels:
-        group_grad, output_panels, first_all, early, *expert_outs = tie(
-            (group_grad, output_panels, first_all, early, *expert_outs)
-        )
-    sent_grad = group_grad
+        group_grad, output_panels, first_all, *expert_outs = tie(
+            (group_grad, output_panels, first_all, *expert_outs)
+        )
     if by_panels:
         panels = dot(first_all, group_grad.reshape(-1, 3 * GROUP_WIDTH), 0, 0).astype(LOW)
+        group_grad, panels = tie((group_grad, panels))
+    project_grad = over_groups(group_grad)
+    if by_panels:
         panels = panels.reshape(3, D // 3, 3 * GROUP_WIDTH)
         output_panels = jnp.sum(output_panels.astype(F32), axis=0).astype(LOW)
         output_panels = (
@@ -1473,19 +1473,18 @@
         own_panels = [
             lax.dynamic_index_in_dim(panels, f_place ^ step, 0, False) for step in range(f_size)
         ]
-        sent_grad, *own_panels = tie((sent_grad, *own_panels))
         summed = own_panels[0].astype(F32)
         for step in range(1, f_size):
             summed = summed + crossed(own_panels[step], "f", f_size, step).astype(F32)
         summed = summed.astype(LOW)
         summed = (summed.astype(F32) + crossed(summed, "c", 2, 1).astype(F32)).astype(LOW)
-        early = direct_sum(early, "c", c_size)
-    project_grad = over_groups(sent_grad)
-    if by_panels:
-        project_grad = tie((project_grad, summed))[0]
+        group_panels = [
+            crossed(summed, ("a", "b"), HEAD_GROUPS, step) for step in range(1, HEAD_GROUPS)
+        ]
+        early = direct_sum(tie((early, summed))[0], "c", c_size)
+        project_grad, *group_panels = tie((project_grad, *group_panels))
     project_grad = (
-        project_grad
-        .reshape(HEAD_GROUPS, rows, 3, GROUP_WIDTH)
+        project_grad.reshape(HEAD_GROUPS, rows, 3, GROUP_WIDTH)
         .transpose(1, 2, 0, 3)
         .reshape(rows, 3 * D)
     )
@@ -1499,18 +1498,11 @@
         early = everywhere_sum(early, sizes)
     late = direct_sum(first_gain_grad[None], "f", f_size)
     late = direct_sum(late, "c", c_size)
-    late = direct_sum(late, ("a", "b"), a_size * b_size)
 
     attn_stats = (attn_weights, attn_left, attn_right, attn_left_root, attn_right_root)
     if by_panels:
-        kept = [kept, kept_near, kept_b]
-        group_panels = [
-            crossed(summed, ("a", "b"), HEAD_GROUPS, step) for step in range(1, HEAD_GROUPS)
-        ]
-        kept[0] = tie((kept[0], summed))[0]
+        kept = [tie((kept, summed))[0], kept_near, kept_b]
         expert_outs = shampoo_half(half, kept, expert_stats, expert_outs)
-        late, *joined = tie((late, *group_panels, *expert_outs))
-        group_panels, expert_outs = joined[: HEAD_GROUPS - 1], joined[HEAD_GROUPS - 1 :]
         turn = (f_place == 3).astype(jnp.int32).reshape(1)
         attn_outs = shampoo_panel(
             turn, group_places, [summed, *group_panels], attn_stats
@@ -1539,6 +1531,8 @@
     expert_grads, expert_left_new, expert_right_new, expert_new = [
         item.reshape(expert_weights.shape) for item in expert_outs
     ]
+    late, *attn_outs = tie((late, *attn_outs))
+    late = direct_sum(late, ("a", "b"), a_size * b_size)
     attn_grads, attn_left_new, attn_right_new, attn_new = attn_outs
     router_grads = early[:route_count].T
     vector_grads = jnp.concatenate([late, early[route_count:]], axis=0)

time: 611 us -> 611 us (level)
  local copies, waits for them, and re-layouts: 47.7 us -> 36.4 us
  starting transfers between devices: 104 us -> 112 us
    all_to_all x6, waiting for transfers between devices: 40.2 us -> 26.5 us  [over_groups(): lax.all_to_all(values, ('a', 'b'), split_axis=0, concat_axis=0, tiled=True)]
    ppermute x46, waiting for transfers between devices: 131 us -> 141 us  [crossed(): return lax.ppermute(values, axes, [(i, i ^ distance) for i in range(size)])]
    ppermute x5, waiting for transfers between devices: 18.5 us -> 26.2 us  [shifted(): lax.ppermute(values, axis, [(i, (i + distance) % size) for i in range(siz...]
    ppermute x46, starting transfers between devices: 50.1 us -> 57.1 us  [crossed(): return lax.ppermute(values, axes, [(i, i ^ distance) for i in range(size)])]
  transfers between devices with their start and end apart: 61 -> 61, of which waited for: 26 -> 31; matrix products, arithmetic and copies ran while one was open for 12% -> 13% of each run, Pallas kernels for 26% -> 29%
where the time goes in v3:
time: 611 us; the launch traced here: 600 us
  waiting for transfers between devices  207 us (34%)
  Pallas kernels  173 us (28%)
  starting transfers between devices  112 us (18%)
  local copies, waits for them, and re-layouts  36.4 us (6%)
  matrix products  33.8 us (6%)
  other arithmetic  31.8 us (5%)
    ppermute x46, waiting for transfers between devices, crossed(): return lax.ppermute(values, axes, [(i, i ^ distance) for i in range(size)])  141 us
    ppermute x46, starting transfers between devices, crossed(): return lax.ppermute(values, axes, [(i, i ^ distance) for i in range(size)])  57.1 us
    pallas_call x1, Pallas kernels, attend_back(): pl.pallas_call(functools.partial(attend_back_kernel, len(pairs), block_ro...  38.4 us
    pallas_call x2, Pallas kernels, shampoo_half(): pl.pallas_call(kernel, grid_spec=pltpu.PrefetchScalarGridSpec(num_scalar_...  26.7 us
    all_to_all x6, waiting for transfers between devices, over_groups(): lax.all_to_all(values, ('a', 'b'), split_axis=0, concat_axis=0, tiled=True)  26.5 us
    ppermute x5, waiting for transfers between devices, shifted(): lax.ppermute(values, axis, [(i, (i + distance) % size) for i in range(siz...  26.2 us
    pallas_call x2, Pallas kernels, expert_half_grads(): pl.pallas_call(kernel, grid=(hidden_blocks // 2,), in_specs=[smem_spec(),...  24.4 us
    all_to_all x6, starting transfers between devices, over_groups(): lax.all_to_all(values, ('a', 'b'), split_axis=0, concat_axis=0, tiled=True)  23.9 us
  transfers between devices with their start and end apart: 61, of which 31 were waited for; matrix products, arithmetic and copies ran while one was open for 13% of the time, Pallas kernels for 29%

profile of v3, /device:TPU:0, one launch (start us, length us, event | category | flops | bytes accessed | tf_op | source)
XLA Modules:
  0.0 600.5 jit_solution(12301600906806269640)
XLA Ops:
  22.9 13.6 %collective-permute-done.3.refs_2_ = bf16[18,128,128]{2,1,0:T(8,128)(2,1)} collective-permute-done((bf16[18,128,128]{2,1,0:T(8,128)(2,1)}, bf16[18,128,128]{2,1,0:T(8,128)(2,1)}, u32[]{:S(2)}, u32[]{:S(2)}) %collective-permute-start.3) | collective-permute-done | bytes 589856 | tf_op jit(solution)/shard_map/ppermute | solution.py:1081
  42.8 8.9 %project.1 = (bf16[384,768]{1,0:T(8,128)(2,1)}, f32[384,1]{1,0:T(8,128)}, bf16[4,192,384]{2,1,0:T(8,128)(2,1)}, bf16[4,384,384]{2,1,0:T(8,128)(2,1)}, bf16[3,256,2304]{2,1,0:T(8,128)(2,1)}) custom-call(s32[4]{0:T(128)} %pad_add_fusion.2.places_ref, f32[384,768]{1,0:T(8,128)} %rows_ref.1, f32[1,768]{1,0:T(1,128)} %get-tuple-element.310.gain_ref, ...), custom_call_target="tpu_custom_call" | custom-call | flops 589824 | bytes 1000000 | tf_op jit(solution)/shard_map/project/pallas_call | solution.py:143
  51.7 4.4 collective-permute-done.6
  64.5 30.4 %collective-permute-done.7.refs_3_ = bf16[18,128,128]{2,1,0:T(8,128)(2,1)S(1)} collective-permute-done((bf16[18,128,128]{2,1,0:T(8,128)(2,1)S(1)}, bf16[18,128,128]{2,1,0:T(8,128)(2,1)S(1)}, u32[]{:S(2)}, u32[]{:S(2)}) %collective-permute-start.7) | collective-permute-done | bytes 589856 | tf_op jit(solution)/shard_map/ppermute | solution.py:1081
  105.0 17.8 %all-to-all-done.refs_2_ = bf16[4,192,384]{2,1,0:T(8,128)(2,1)S(1)} async-done(((bf16[4,192,384]{2,1,0:T(8,128)(2,1)}), bf16[4,192,384]{2,1,0:T(8,128)(2,1)S(1)}, u32[]{:S(2)}, u32[]{:S(2)}) %all-to-all-start) | async-done | bytes 589856 | tf_op jit(solution)/shard_map/all_to_all | solution.py:1196
  122.8 5.4 collective-permute-done.11
  134.1 20.5 %attend_forward.1 = (f32[4,384,192]{2,1,0:T(8,128)}, bf16[4,192,384]{2,1,0:T(8,128)(2,1)}, f32[16,288,1]{2,1,0:T(8,128)}) custom-call(s32[2,16]{1,0:T(2,128)} %pad_add_fusion.refs_0_, s32[4]{0:T(128)} %bitcast.207, bf16[4,192,384]{2,1,0:T(8,128)(2,1)} %copy-done.8, bf16[4,384,384]{2,1,0:T(8,128)(2,1)} %copy-done.5, bf16[4,384,384]{2,1,0:T(8,128)(2,1)} %copy-done.15), custom_call_target="tpu_custom_call" | custom-call | flops 98304 | bytes 1000000 | tf_op jit(solution)/shard_map/attend_forward/pallas_call | solution.py:382
  166.6 8.7 %all-to-all-done.2 = bf16[4,192,384]{2,1,0:T(8,128)(2,1)S(1)} async-done(((bf16[4,192,384]{2,1,0:T(8,128)(2,1)}), bf16[4,192,384]{2,1,0:T(8,128)(2,1)S(1)}, u32[]{:S(2)}, u32[]{:S(2)}) %all-to-all-start.2) | async-done | bytes 589856 | tf_op jit(solution)/shard_map/all_to_all | solution.py:1196
  180.4 4.9 collective-permute-done.16.refs_11_
  187.2 4.6 all-to-all-start.4
  196.4 21.8 %collective-permute-done.17 = bf16[384,768]{1,0:T(8,128)(2,1)} collective-permute-done((bf16[384,768]{1,0:T(8,128)(2,1)}, bf16[384,768]{1,0:T(8,128)(2,1)}, u32[]{:S(2)}, u32[]{:S(2)}) %collective-permute-start.17) | collective-permute-done | bytes 589856 | tf_op jit(solution)/shard_map/ppermute | solution.py:1081
  222.3 4.8 all-to-all-start.3
  227.1 19.1 %expert_forward.1 = (bf16[768,768]{1,0:T(8,128)(2,1)}, f32[768,2048]{1,0:T(8,128)}, f32[768,2048]{1,0:T(8,128)}, bf16[768,2048]{1,0:T(8,128)(2,1)}) custom-call(s32[14]{0:T(128)} %stack.103.places_ref, bf16[768,768]{1,0:T(8,128)(2,1)} %bitcast.34.rows_ref, bf16[36,128,128]{2,1,0:T(8,128)(2,1)} %bitcast.186, ...), custom_call_target="tpu_custom_call" | custom-call | flops 7247757312 | bytes 11796480 | tf_op jit(solution)/shard_map/expert_forward/pallas_call | solution.py:649
  246.2 10.4 %all-to-all-done.3 = bf16[8,96,768]{2,1,0:T(8,128)(2,1)} async-done(((bf16[8,96,768]{2,1,0:T(8,128)(2,1)}), bf16[8,96,768]{2,1,0:T(8,128)(2,1)}, u32[]{:S(2)}, u32[]{:S(2)}) %all-to-all-start.3) | async-done | bytes 1179680 | tf_op jit(solution)/shard_map/all_to_all | solution.py:1171
  261.0 20.2 %expert_row_grads.1 = (bf16[768,768]{1,0:T(8,128)(2,1)}, bf16[768,2048]{1,0:T(8,128)(2,1)}, bf16[768,2048]{1,0:T(8,128)(2,1)}) custom-call(s32[14]{0:T(128)} %stack.103.places_ref, bf16[768,768]{1,0:T(8,128)(2,1)} %bitcast.32.grads_ref, f32[768,2048]{1,0:T(8,128)} %get-tuple-element.186.gate_i, f32[768,2048]{1,0:T(8,128)} %get-tuple-element.187.up_i, ...), custom_call_target="tpu_custom_call" | custom-call | flops 7247757312 | bytes 22413312 | tf_op jit(solution)/shard_map/expert_row_grads/pallas_call | solution.py:720
  281.3 12.2 %expert_half_grads.2 = (bf16[36,128,128]{2,1,0:T(8,128)(2,1)}, bf16[36,128,128]{2,1,0:T(8,128)(2,1)}, bf16[36,128,128]{2,1,0:T(8,128)(2,1)}, bf16[18,128,128]{2,1,0:T(8,128)(2,1)}, bf16[18,128,128]{2,1,0:T(8,128)(2,1)}) custom-call(s32[1]{0:T(128)S(6)} %sub.58.which_ref.half_ref, s32[7]{0:T(128)} %stack.111.places_ref, bf16[768,768]{1,0:T(8,128)(2,1)} %bitcast.34.rows_ref, ...), custom_call_target="tpu_custom_call" | custom-call | flops 3623878656 | bytes 12976128 | tf_op jit(solution)/shard_map/expert_half_grads/pallas_call | solution.py:875
  293.5 5.4 all-to-all-start.6
  312.0 12.2 %expert_half_grads.3 = (bf16[36,128,128]{2,1,0:T(8,128)(2,1)}, bf16[36,128,128]{2,1,0:T(8,128)(2,1)}, bf16[36,128,128]{2,1,0:T(8,128)(2,1)}, bf16[36,128,128]{2,1,0:T(8,128)(2,1)}) custom-call(s32[1]{0:T(128)} %bitcast.36.which_ref.half_ref, s32[4]{0:T(128)} %get-tuple-element.199.places_ref, bf16[768,768]{1,0:T(8,128)(2,1)} %bitcast.34.rows_ref, ...), custom_call_target="tpu_custom_call" | custom-call | flops 3623878656 | bytes 12976128 | tf_op jit(solution)/shard_map/expert_half_grads/pallas_call | solution.py:875
  333.0 8.0 %collective-permute-done.22 = bf16[36,128,128]{2,1,0:T(8,128)(2,1)} collective-permute-done((bf16[36,128,128]{2,1,0:T(8,128)(2,1)}, bf16[36,128,128]{2,1,0:T(8,128)(2,1)}, u32[]{:S(2)}, u32[]{:S(2)}) %collective-permute-start.22) | collective-permute-done | bytes 1179680 | tf_op jit(solution)/shard_map/ppermute | solution.py:1081
  348.1 5.5 all-to-all-start.7
  363.7 16.0 %collective-permute-done.29 = f32[15,768]{1,0:T(8,128)S(1)} collective-permute-done((f32[15,768]{1,0:T(8,128)S(1)}, f32[15,768]{1,0:T(8,128)S(1)}, u32[]{:S(2)}, u32[]{:S(2)}) %collective-permute-start.29) | collective-permute-done | bytes 46112 | tf_op jit(solution)/shard_map/ppermute | solution.py:1081
  395.8 38.4 %attend_backward.1 = (bf16[4,384,192]{2,1,0:T(8,128)(2,1)}, f32[4,384,384]{2,1,0:T(8,128)}, bf16[4,384,384]{2,1,0:T(8,128)(2,1)}) custom-call(s32[2,16]{1,0:T(2,128)} %pad_add_fusion.refs_0_, s32[4]{0:T(128)} %bitcast.208, bf16[4,192,384]{2,1,0:T(8,128)(2,1)} %copy-done.8, bf16[4,384,384]{2,1,0:T(8,128)(2,1)} %copy-done.5, bf16[4,384,384]{2,1,0:T(8,128)(2,1)} %copy-done.15, ...), custom_call_target="tpu_custom_call" | custom-call | flops 98304 | bytes 1000000 | tf_op jit(solution)/shard_map/attend_backward/pallas_call | solution.py:543
  439.0 5.1 collective-permute-done.33.refs_0_
  450.3 9.2 %collective-permute-done.35 = bf16[4,384,384]{2,1,0:T(8,128)(2,1)} collective-permute-done((bf16[4,384,384]{2,1,0:T(8,128)(2,1)}, bf16[4,384,384]{2,1,0:T(8,128)(2,1)}, u32[]{:S(2)}, u32[]{:S(2)}) %collective-permute-start.35) | collective-permute-done | bytes 1179680 | tf_op jit(solution)/shard_map/ppermute | solution.py:1077
  462.5 13.2 %shampoo_half.2 = (f32[72,128,128]{2,1,0:T(8,128)}, f32[72,128,128]{2,1,0:T(8,128)}, f32[72,128,128]{2,1,0:T(8,128)}, f32[72,128,128]{2,1,0:T(8,128)}) custom-call(s32[1]{0:T(128)S(6)} %sub.58.which_ref.half_ref, bf16[36,128,128]{2,1,0:T(8,128)(2,1)} %copy-done.24, bf16[72,128,128]{2,1,0:T(8,128)(2,1)} %bitcast.166, f32[72,128,128]{2,1,0:T(8,128)} %bitcast.168, ...), custom_call_target="tpu_custom_call" | custom-call | flops 1811939328 | bytes 21233664 | tf_op jit(solution)/shard_map/shampoo_half/pallas_call | solution.py:936
  483.9 4.6 convolution_convert_fusion.1
  504.6 8.9 %collective-permute-done.37 = bf16[256,576]{1,0:T(8,128)(2,1)} collective-permute-done((bf16[256,576]{1,0:T(8,128)(2,1)}, bf16[256,576]{1,0:T(8,128)(2,1)}, u32[]{:S(2)}, u32[]{:S(2)}) %collective-permute-start.37) | collective-permute-done | bytes 294944 | tf_op jit(solution)/shard_map/ppermute | solution.py:1081
  513.4 6.2 %collective-permute-done.38 = bf16[256,576]{1,0:T(8,128)(2,1)} collective-permute-done((bf16[256,576]{1,0:T(8,128)(2,1)}, bf16[256,576]{1,0:T(8,128)(2,1)}, u32[]{:S(2)}, u32[]{:S(2)}) %collective-permute-start.38) | collective-permute-done | bytes 294944 | tf_op jit(solution)/shard_map/ppermute | solution.py:1081
  524.3 7.8 %collective-permute-done.39 = bf16[256,576]{1,0:T(8,128)(2,1)S(1)} collective-permute-done((bf16[256,576]{1,0:T(8,128)(2,1)}, bf16[256,576]{1,0:T(8,128)(2,1)S(1)}, u32[]{:S(2)}, u32[]{:S(2)}) %collective-permute-start.39) | collective-permute-done | bytes 294944 | tf_op jit(solution)/shard_map/ppermute | solution.py:1081
  539.0 13.6 %shampoo_half.3 = (f32[72,128,128]{2,1,0:T(8,128)}, f32[72,128,128]{2,1,0:T(8,128)}, f32[72,128,128]{2,1,0:T(8,128)}, f32[72,128,128]{2,1,0:T(8,128)}) custom-call(s32[1]{0:T(128)} %bitcast.36.which_ref.half_ref, bf16[36,128,128]{2,1,0:T(8,128)(2,1)} %get-tuple-element.263.refs_0_, ...), custom_call_target="tpu_custom_call", output_to_operand_aliasing={{0}: (9, {}), {1}: (10, {}), {2}: (11, {}), {3}: (12, {})} | custom-call | flops 1811939328 | bytes 23592960 | tf_op jit(solution)/shard_map/shampoo_half/pallas_call | solution.py:936
  572.1 15.1 %shampoo_panel.1 = (f32[36,128,128]{2,1,0:T(8,128)}, f32[36,128,128]{2,1,0:T(8,128)}, f32[36,128,128]{2,1,0:T(8,128)}, f32[36,128,128]{2,1,0:T(8,128)}) custom-call(s32[1]{0:T(128)} %bitcast.72.turn_ref, s32[4]{0:T(128)} %get-tuple-element.247.places_ref, bf16[256,576]{1,0:T(8,128)(2,1)} %copy-done.21, bf16[256,576]{1,0:T(8,128)(2,1)} %copy-done.32, ...), custom_call_target="tpu_custom_call" | custom-call | flops 1811939328 | bytes 22413312 | tf_op jit(solution)/shard_map/shampoo_panel/pallas_call | solution.py:1041
  587.2 6.0 %collective-permute-start.47 = (f32[1,768]{1,0:T(1,128)S(1)}, f32[1,768]{1,0:T(1,128)S(1)}, u32[]{:S(2)}, u32[]{:S(2)}) collective-permute-start(f32[1,768]{1,0:T(1,128)S(1)} %add.314), channel_id=1, source_target_pairs={{0,8},{8,0},{16,24},{24,16},{1,9},{9,1},{17,25},{25,17},{2,10},{10... | collective-permute-start | bytes 9224 | tf_op jit(solution)/shard_map/ppermute | solution.py:1081
  (312 shorter events, 211.8 us)
Async XLA Ops:
  0.7 38.1 %collective-permute-start = (bf16[36,128,128]{2,1,0:T(8,128)(2,1)}, bf16[36,128,128]{2,1,0:T(8,128)(2,1)}, u32[]{:S(2)}, u32[]{:S(2)}) collective-permute-start(bf16[36,128,128]{2,1,0:T(8,128)(2,1)} %refs_4_.1), channel_id=1, source_target_pairs={{0,2},{1,3},{2,0},{3,1},{4,6},{5,7},{6,4},{7,5},{8,10},{9,11},{10,... | collective-permute-start | bytes 3538952 | tf_op jit(solution)/shard_map/ppermute | solution.py:1081
  3.7 36.8 %collective-permute-start.4 = (bf16[36,128,128]{2,1,0:T(8,128)(2,1)}, bf16[36,128,128]{2,1,0:T(8,128)(2,1)}, u32[]{:S(2)}, u32[]{:S(2)}) collective-permute-start(bf16[36,128,128]{2,1,0:T(8,128)(2,1)} %refs_4_.1), channel_id=1, source_target_pairs={{0,1},{1,0},{2,3},{3,2},{4,5},{5,4},{6,7},{7,6},{8,9},{9,8},{10,11... | collective-permute-start | bytes 3538952 | tf_op jit(solution)/shard_map/ppermute | solution.py:1081
  5.5 33.3 %collective-permute-start.1 = (bf16[36,128,128]{2,1,0:T(8,128)(2,1)S(1)}, bf16[36,128,128]{2,1,0:T(8,128)(2,1)}, u32[]{:S(2)}, u32[]{:S(2)}) collective-permute-start(bf16[36,128,128]{2,1,0:T(8,128)(2,1)S(1)} %bitcast.185), channel_id=1, source_target_pairs={{0,4},{4,0},{1,5},{5,1},{2,6},{6,2},{3,7},{7,3},{8,12},{12,8},{9,1... | collective-permute-start | bytes 3538952 | tf_op jit(solution)/shard_map/ppermute | solution.py:1081
  8.1 28.4 %collective-permute-start.3 = (bf16[18,128,128]{2,1,0:T(8,128)(2,1)}, bf16[18,128,128]{2,1,0:T(8,128)(2,1)}, u32[]{:S(2)}, u32[]{:S(2)}) collective-permute-start(bf16[18,128,128]{2,1,0:T(8,128)(2,1)} %get-tuple-element.309), channel_id=1, source_target_pairs={{0,8},{8,0},{1,9},{9,1},{2,10},{10,2},{3,11},{11,3},{4,12},{12,4},... | collective-permute-start | bytes 1769480 | tf_op jit(solution)/shard_map/ppermute | solution.py:1081
  9.8 28.9 %collective-permute-start.2 = (bf16[18,128,128]{2,1,0:T(8,128)(2,1)S(1)}, bf16[18,128,128]{2,1,0:T(8,128)(2,1)}, u32[]{:S(2)}, u32[]{:S(2)}) collective-permute-start(bf16[18,128,128]{2,1,0:T(8,128)(2,1)S(1)} %slice_bitcast_fusion.2), channel_id=1, source_target_pairs={{0,16},{16,0},{1,17},{17,1},{2,18},{18,2},{3,19},{19,3},{4,20},{20... | collective-permute-start | bytes 1769480 | tf_op jit(solution)/shard_map/ppermute | solution.py:1077
  56.8 39.2 %all-to-all-start.1 = ((bf16[4,384,384]{2,1,0:T(8,128)(2,1)}), bf16[4,384,384]{2,1,0:T(8,128)(2,1)S(1)}, u32[]{:S(2)}, u32[]{:S(2)}) async-start(bf16[4,384,384]{2,1,0:T(8,128)(2,1)} %get-tuple-element.151), calls=%async_computation.1 | async-start | bytes 2359296 | tf_op jit(solution)/shard_map/all_to_all | solution.py:1196
  60.5 34.4 %collective-permute-start.7 = (bf16[18,128,128]{2,1,0:T(8,128)(2,1)S(1)}, bf16[18,128,128]{2,1,0:T(8,128)(2,1)S(1)}, u32[]{:S(2)}, u32[]{:S(2)}) collective-permute-start(bf16[18,128,128]{2,1,0:T(8,128)(2,1)S(1)} %copy-done.30), channel_id=1, source_target_pairs={{0,8},{8,0},{1,9},{9,1},{2,10},{10,2},{3,11},{11,3},{4,12},{12,4},... | collective-permute-start | bytes 1769480 | tf_op jit(solution)/shard_map/ppermute | solution.py:1081
  62.5 32.5 %collective-permute-start.8 = (bf16[18,128,128]{2,1,0:T(8,128)(2,1)}, bf16[18,128,128]{2,1,0:T(8,128)(2,1)S(1)}, u32[]{:S(2)}, u32[]{:S(2)}) collective-permute-start(bf16[18,128,128]{2,1,0:T(8,128)(2,1)} %collective-permute-done.3.refs_2_), channel_id=1, source_target_pairs={{0,4},{4,0},{1,5},{5,1},{2,6},{6,2},{3,7},{7,3},{8,12},{12,8},{9,1... | collective-permute-start | bytes 1769480 | tf_op jit(solution)/shard_map/ppermute | solution.py:1081
  63.0 31.9 %collective-permute-start.9 = (bf16[18,128,128]{2,1,0:T(8,128)(2,1)}, bf16[18,128,128]{2,1,0:T(8,128)(2,1)}, u32[]{:S(2)}, u32[]{:S(2)}) collective-permute-start(bf16[18,128,128]{2,1,0:T(8,128)(2,1)} %collective-permute-done.2.refs_6_), channel_id=1, source_target_pairs={{0,4},{4,0},{1,5},{5,1},{2,6},{6,2},{3,7},{7,3},{8,12},{12,8},{9,1... | collective-permute-start | bytes 1769480 | tf_op jit(solution)/shard_map/ppermute | solution.py:1081
  96.0 32.1 %collective-permute-start.10 = (bf16[4,384,384]{2,1,0:T(8,128)(2,1)S(1)}, bf16[4,384,384]{2,1,0:T(8,128)(2,1)S(1)}, u32[]{:S(2)}, u32[]{:S(2)}) collective-permute-start(bf16[4,384,384]{2,1,0:T(8,128)(2,1)S(1)} %all-to-all-done.1.refs_3_), channel_id=1, source_target_pairs={{0,4},{4,0},{1,5},{5,1},{2,6},{6,2},{3,7},{7,3},{8,12},{12,8},{9,1... | collective-permute-start | bytes 3538952 | tf_op jit(solution)/shard_map/ppermute | solution.py:1081
  100.4 27.8 %collective-permute-start.11 = (bf16[9,128,128]{2,1,0:T(8,128)(2,1)}, bf16[9,128,128]{2,1,0:T(8,128)(2,1)}, u32[]{:S(2)}, u32[]{:S(2)}) collective-permute-start(bf16[9,128,128]{2,1,0:T(8,128)(2,1)} %get-tuple-element.155), channel_id=1, source_target_pairs={{0,16},{16,0},{1,17},{17,1},{2,18},{18,2},{3,19},{19,3},{4,20},{20... | collective-permute-start | bytes 884744 | tf_op jit(solution)/shard_map/ppermute | solution.py:1077
  130.0 26.5 %collective-permute-start.12 = (bf16[384,768]{1,0:T(8,128)(2,1)}, bf16[384,768]{1,0:T(8,128)(2,1)}, u32[]{:S(2)}, u32[]{:S(2)}) collective-permute-start(bf16[384,768]{1,0:T(8,128)(2,1)} %get-tuple-element.231), channel_id=1, source_target_pairs={{0,16},{8,24},{16,0},{24,8},{1,17},{9,25},{17,1},{25,9},{2,18},{10... | collective-permute-start | bytes 1769480 | tf_op jit(solution)/shard_map/ppermute | solution.py:1081
  130.0 26.5 %collective-permute-start.13 = (bf16[18,128,128]{2,1,0:T(8,128)(2,1)}, bf16[18,128,128]{2,1,0:T(8,128)(2,1)}, u32[]{:S(2)}, u32[]{:S(2)}) collective-permute-start(bf16[18,128,128]{2,1,0:T(8,128)(2,1)} %copy-done.43), channel_id=1, source_target_pairs={{0,4},{4,0},{1,5},{5,1},{2,6},{6,2},{3,7},{7,3},{8,12},{12,8},{9,1... | collective-permute-start | bytes 1769480 | tf_op jit(solution)/shard_map/ppermute | solution.py:1081
  132.0 26.6 %collective-permute-start.15 = (bf16[18,128,128]{2,1,0:T(8,128)(2,1)}, bf16[18,128,128]{2,1,0:T(8,128)(2,1)}, u32[]{:S(2)}, u32[]{:S(2)}) collective-permute-start(bf16[18,128,128]{2,1,0:T(8,128)(2,1)} %collective-permute-done.2.refs_6_), channel_id=1, source_target_pairs={{0,8},{8,0},{1,9},{9,1},{2,10},{10,2},{3,11},{11,3},{4,12},{12,4},... | collective-permute-start | bytes 1769480 | tf_op jit(solution)/shard_map/ppermute | solution.py:1081
  187.2 35.2 %all-to-all-start.4 = ((bf16[8,96,768]{2,1,0:T(8,128)(2,1)}), bf16[8,96,768]{2,1,0:T(8,128)(2,1)}, u32[]{:S(2)}, u32[]{:S(2)}) async-start(bf16[8,96,768]{2,1,0:T(8,128)(2,1)} %bitcast.201), calls=%async_computation.4 | async-start | bytes 2359296 | tf_op jit(solution)/shard_map/all_to_all | solution.py:1171
  191.8 26.5 %collective-permute-start.17 = (bf16[384,768]{1,0:T(8,128)(2,1)}, bf16[384,768]{1,0:T(8,128)(2,1)}, u32[]{:S(2)}, u32[]{:S(2)}) collective-permute-start(bf16[384,768]{1,0:T(8,128)(2,1)} %get-tuple-element.231), channel_id=1, source_target_pairs={{0,8},{8,0},{16,24},{24,16},{1,9},{9,1},{17,25},{25,17},{2,10},{10... | collective-permute-start | bytes 1769480 | tf_op jit(solution)/shard_map/ppermute | solution.py:1081
  193.4 27.1 %collective-permute-start.19 = (bf16[18,128,128]{2,1,0:T(8,128)(2,1)}, bf16[18,128,128]{2,1,0:T(8,128)(2,1)}, u32[]{:S(2)}, u32[]{:S(2)}) collective-permute-start(bf16[18,128,128]{2,1,0:T(8,128)(2,1)} %collective-permute-done.16.refs_11_), channel_id=1, source_target_pairs={{0,4},{4,0},{1,5},{5,1},{2,6},{6,2},{3,7},{7,3},{8,12},{12,8},{9,1... | collective-permute-start | bytes 1769480 | tf_op jit(solution)/shard_map/ppermute | solution.py:1081
  222.3 34.3 %all-to-all-start.3 = ((bf16[8,96,768]{2,1,0:T(8,128)(2,1)}), bf16[8,96,768]{2,1,0:T(8,128)(2,1)}, u32[]{:S(2)}, u32[]{:S(2)}) async-start(bf16[8,96,768]{2,1,0:T(8,128)(2,1)} %bitcast.188), calls=%async_computation.3 | async-start | bytes 2359296 | tf_op jit(solution)/shard_map/all_to_all | solution.py:1171
  256.6 36.9 %all-to-all-start.5 = ((bf16[8,96,768]{2,1,0:T(8,128)(2,1)}), bf16[8,96,768]{2,1,0:T(8,128)(2,1)}, u32[]{:S(2)}, u32[]{:S(2)}) async-start(bf16[8,96,768]{2,1,0:T(8,128)(2,1)} %bitcast.200), calls=%async_computation.5 | async-start | bytes 2359296 | tf_op jit(solution)/shard_map/all_to_all | solution.py:1175
  261.0 32.5 %collective-permute-start.20 = (bf16[384,768]{1,0:T(8,128)(2,1)}, bf16[384,768]{1,0:T(8,128)(2,1)}, u32[]{:S(2)}, u32[]{:S(2)}) collective-permute-start(bf16[384,768]{1,0:T(8,128)(2,1)} %collective-permute-done.12), channel_id=1, source_target_pairs={{0,8},{8,0},{1,9},{9,1},{2,10},{10,2},{3,11},{11,3},{4,12},{12,4},... | collective-permute-start | bytes 1769480 | tf_op jit(solution)/shard_map/ppermute | solution.py:1081
  293.5 35.0 %all-to-all-start.6 = ((bf16[8,96,768]{2,1,0:T(8,128)(2,1)}), bf16[8,96,768]{2,1,0:T(8,128)(2,1)}, u32[]{:S(2)}, u32[]{:S(2)}) async-start(bf16[8,96,768]{2,1,0:T(8,128)(2,1)} %bitcast.199), calls=%async_computation.6 | async-start | bytes 2359296 | tf_op jit(solution)/shard_map/all_to_all | solution.py:1175
  299.6 33.4 %collective-permute-start.21 = (bf16[36,128,128]{2,1,0:T(8,128)(2,1)}, bf16[36,128,128]{2,1,0:T(8,128)(2,1)}, u32[]{:S(2)}, u32[]{:S(2)}) collective-permute-start(bf16[36,128,128]{2,1,0:T(8,128)(2,1)} %get-tuple-element.206), channel_id=1, source_target_pairs={{0,4},{4,0},{1,5},{5,1},{2,6},{6,2},{3,7},{7,3},{8,12},{12,8},{9,1... | collective-permute-start | bytes 3538952 | tf_op jit(solution)/shard_map/ppermute | solution.py:1081
  301.2 39.9 %collective-permute-start.22 = (bf16[36,128,128]{2,1,0:T(8,128)(2,1)}, bf16[36,128,128]{2,1,0:T(8,128)(2,1)}, u32[]{:S(2)}, u32[]{:S(2)}) collective-permute-start(bf16[36,128,128]{2,1,0:T(8,128)(2,1)} %get-tuple-element.207), channel_id=1, source_target_pairs={{0,8},{8,0},{1,9},{9,1},{2,10},{10,2},{3,11},{11,3},{4,12},{12,4},... | collective-permute-start | bytes 3538952 | tf_op jit(solution)/shard_map/ppermute | solution.py:1081
  343.1 43.1 %collective-permute-start.25 = (bf16[36,128,128]{2,1,0:T(8,128)(2,1)}, bf16[36,128,128]{2,1,0:T(8,128)(2,1)}, u32[]{:S(2)}, u32[]{:S(2)}) collective-permute-start(bf16[36,128,128]{2,1,0:T(8,128)(2,1)} %get-tuple-element.212), channel_id=1, source_target_pairs={{0,4},{4,0},{1,5},{5,1},{2,6},{6,2},{3,7},{7,3},{8,12},{12,8},{9,1... | collective-permute-start | bytes 3538952 | tf_op jit(solution)/shard_map/ppermute | solution.py:1081
  348.1 38.1 %all-to-all-start.7 = ((bf16[4,192,384]{2,1,0:T(8,128)(2,1)}), bf16[4,192,384]{2,1,0:T(8,128)(2,1)S(1)}, u32[]{:S(2)}, u32[]{:S(2)}) async-start(bf16[4,192,384]{2,1,0:T(8,128)(2,1)} %reshape.357), calls=%async_computation.7 | async-start | bytes 1179648 | tf_op jit(solution)/shard_map/all_to_all | solution.py:1196
  355.6 30.6 %collective-permute-start.24 = (bf16[18,128,128]{2,1,0:T(8,128)(2,1)}, bf16[18,128,128]{2,1,0:T(8,128)(2,1)S(1)}, u32[]{:S(2)}, u32[]{:S(2)}) collective-permute-start(bf16[18,128,128]{2,1,0:T(8,128)(2,1)} %add_convert_fusion.5), channel_id=1, source_target_pairs={{0,4},{4,0},{1,5},{5,1},{2,6},{6,2},{3,7},{7,3},{8,12},{12,8},{9,1... | collective-permute-start | bytes 1769480 | tf_op jit(solution)/shard_map/ppermute | solution.py:1081
  358.5 27.7 %collective-permute-start.23 = (bf16[18,128,128]{2,1,0:T(8,128)(2,1)S(1)}, bf16[18,128,128]{2,1,0:T(8,128)(2,1)}, u32[]{:S(2)}, u32[]{:S(2)}) collective-permute-start(bf16[18,128,128]{2,1,0:T(8,128)(2,1)S(1)} %add_convert_fusion.6), channel_id=1, source_target_pairs={{0,8},{8,0},{1,9},{9,1},{2,10},{10,2},{3,11},{11,3},{4,12},{12,4},... | collective-permute-start | bytes 1769480 | tf_op jit(solution)/shard_map/ppermute | solution.py:1081
  389.2 49.8 %collective-permute-start.34 = (bf16[36,128,128]{2,1,0:T(8,128)(2,1)}, bf16[36,128,128]{2,1,0:T(8,128)(2,1)S(1)}, u32[]{:S(2)}, u32[]{:S(2)}) collective-permute-start(bf16[36,128,128]{2,1,0:T(8,128)(2,1)} %add_convert_fusion.1), channel_id=1, source_target_pairs={{0,8},{8,0},{1,9},{9,1},{2,10},{10,2},{3,11},{11,3},{4,12},{12,4},... | collective-permute-start | bytes 3538952 | tf_op jit(solution)/shard_map/ppermute | solution.py:1081
  391.3 52.9 %collective-permute-start.33 = (bf16[36,128,128]{2,1,0:T(8,128)(2,1)S(1)}, bf16[36,128,128]{2,1,0:T(8,128)(2,1)S(1)}, u32[]{:S(2)}, u32[]{:S(2)}) collective-permute-start(bf16[36,128,128]{2,1,0:T(8,128)(2,1)S(1)} %pad_maximum_fusion.1), channel_id=1, source_target_pairs={{0,16},{16,0},{1,17},{17,1},{2,18},{18,2},{3,19},{19,3},{4,20},{20... | collective-permute-start | bytes 3538952 | tf_op jit(solution)/shard_map/ppermute | solution.py:1077
  394.6 49.6 %collective-permute-start.32 = (bf16[36,128,128]{2,1,0:T(8,128)(2,1)S(1)}, bf16[36,128,128]{2,1,0:T(8,128)(2,1)S(1)}, u32[]{:S(2)}, u32[]{:S(2)}) collective-permute-start(bf16[36,128,128]{2,1,0:T(8,128)(2,1)S(1)} %copy-done.42), channel_id=1, source_target_pairs={{0,4},{4,0},{1,5},{5,1},{2,6},{6,2},{3,7},{7,3},{8,12},{12,8},{9,1... | collective-permute-start | bytes 3538952 | tf_op jit(solution)/shard_map/ppermute | solution.py:1081
  446.7 37.2 %all-to-all-start.8 = ((bf16[4,768,192]{1,2,0:T(8,128)(2,1)}), bf16[4,768,192]{1,2,0:T(8,128)(2,1)S(1)}, u32[]{:S(2)}, u32[]{:S(2)}) async-start(bf16[4,768,192]{1,2,0:T(8,128)(2,1)} %convert_bitcast_fusion), calls=%async_computation.8 | async-start | bytes 2359296 | tf_op jit(solution)/shard_map/all_to_all | solution.py:1196
  490.7 70.2 %all-to-all-start.9 = ((bf16[4,384,576]{1,2,0:T(8,128)(2,1)}), bf16[4,384,576]{1,2,0:T(8,128)(2,1)S(1)}, u32[]{:S(2)}, u32[]{:S(2)}) async-start(bf16[4,384,576]{1,2,0:T(8,128)(2,1)} %copy.66), calls=%async_computation.9 | async-start | bytes 3538944 | tf_op jit(solution)/shard_map/all_to_all | solution.py:1196
  (76 other events, 1453.0 us)

commit v4 on v3

--- a/solution.py
+++ b/solution.py
@@ -1421,7 +1421,7 @@
         attended_grad, given_b, given_c, kept_next, early = tie(
             (attended_grad, given_b, given_c, kept_next, early)
         )
-        kept_b = over_b((kept_far.astype(F32) + kept_next.astype(F32)).astype(LOW))
+        kept_sum = (kept_far.astype(F32) + kept_next.astype(F32)).astype(LOW)
         taken = jnp.concatenate(
             [
                 given[:part].astype(F32) + hop_c[:part].astype(F32) + given_b.astype(F32),
@@ -1431,10 +1431,10 @@
         )
         taken = shifted(taken.astype(LOW), "a", 2, 1)
         kept_near = over_c(tie((kept_near, attended_grad))[0])
+        early = direct_sum(early, "c", c_size)
     back_outs = attend_back(kpb, ends, queries, pairs, attended_grad, raw, lse)
     if by_panels:
-        sent_outs = back_outs
-        *back_outs, kept_near, taken, kept_b = tie((*back_outs, kept_near, taken, kept_b))
+        *back_outs, kept_near, taken, early = tie((*back_outs, kept_near, taken, early))
         middle_late = tie((middle_low, back_outs[0]))[0]
         output_panels = jnp.einsum(
             "hrj,rd->hdj", by_heads, middle_late, preferred_element_type=F32
@@ -1450,12 +1450,11 @@
         first_all = first_all.reshape(-1, D)
     query_grad, pair_grad = back_outs[:2]
     for step in range(1, c_size):
-        sent = sent_outs if by_panels else back_outs
-        pair_grad = pair_grad + shifted(sent[1 + step], "c", c_size, -step).astype(F32)
+        pair_grad = pair_grad + shifted(back_outs[1 + step], "c", c_size, -step).astype(F32)
     group_grad = jnp.concatenate([query_grad, pair_grad.astype(LOW)], axis=2)
     if by_panels:
-        group_grad, output_panels, first_all, *expert_outs = tie(
-            (group_grad, output_panels, first_all, *expert_outs)
+        group_grad, output_panels, first_all, early, *expert_outs = tie(
+            (group_grad, output_panels, first_all, early, *expert_outs)
         )
     if by_panels:
         panels = dot(first_all, group_grad.reshape(-1, 3 * GROUP_WIDTH), 0, 0).astype(LOW)
@@ -1481,8 +1480,8 @@
         group_panels = [
             crossed(summed, ("a", "b"), HEAD_GROUPS, step) for step in range(1, HEAD_GROUPS)
         ]
-        early = direct_sum(tie((early, summed))[0], "c", c_size)
         project_grad, *group_panels = tie((project_grad, *group_panels))
+        kept_b = over_b(tie((kept_sum, summed))[0])
     project_grad = (
         project_grad.reshape(HEAD_GROUPS, rows, 3, GROUP_WIDTH)
         .transpose(1, 2, 0, 3)
@@ -1497,16 +1496,16 @@
         early = jnp.concatenate([router_local, second_gain_grad[None], const_grad], axis=0)
         early = everywhere_sum(early, sizes)
     late = direct_sum(first_gain_grad[None], "f", f_size)
-    late = direct_sum(late, "c", c_size)
 
     attn_stats = (attn_weights, attn_left, attn_right, attn_left_root, attn_right_root)
     if by_panels:
-        kept = [tie((kept, summed))[0], kept_near, kept_b]
-        expert_outs = shampoo_half(half, kept, expert_stats, expert_outs)
         turn = (f_place == 3).astype(jnp.int32).reshape(1)
         attn_outs = shampoo_panel(
             turn, group_places, [summed, *group_panels], attn_stats
         )
+        late, kept, *attn_outs = tie((late, kept, *attn_outs))
+        late, kept = tie((direct_sum(late, "c", c_size), kept))
+        expert_outs = shampoo_half(half, [kept, kept_near, kept_b], expert_stats, expert_outs)
     else:
         output_weight_grad = dot(attended, middle_low, 0, 0)
         project_weight_grad = dot(first_low, project_grad, 0, 0)
@@ -1531,7 +1530,8 @@
     expert_grads, expert_left_new, expert_right_new, expert_new = [
         item.reshape(expert_weights.shape) for item in expert_outs
     ]
-    late, *attn_outs = tie((late, *attn_outs))
+    if not by_panels:
+        late = direct_sum(late, "c", c_size)
     late = direct_sum(late, ("a", "b"), a_size * b_size)
     attn_grads, attn_left_new, attn_right_new, attn_new = attn_outs
     router_grads = early[:route_count].T

time: 611 us -> 611 us (level)
    ppermute x5, waiting for transfers between devices: 26.2 us -> 41.2 us  [shifted(): lax.ppermute(values, axis, [(i, (i + distance) % size) for i in range(siz...]
    ppermute x46, waiting for transfers between devices: 141 us -> 128 us  [crossed(): return lax.ppermute(values, axes, [(i, i ^ distance) for i in range(size)])]
  transfers between devices with their start and end apart: 61 -> 61, of which waited for: 31 -> 28; matrix products, arithmetic and copies ran while one was open for 13% -> 13% of each run, Pallas kernels for 29% -> 29%
where the time goes in v4:
time: 611 us; the launch traced here: 600 us
  waiting for transfers between devices  210 us (34%)
  Pallas kernels  173 us (28%)
  starting transfers between devices  113 us (18%)
  local copies, waits for them, and re-layouts  37.2 us (6%)
  matrix products  33.8 us (6%)
  other arithmetic  27.5 us (5%)
    ppermute x46, waiting for transfers between devices, crossed(): return lax.ppermute(values, axes, [(i, i ^ distance) for i in range(size)])  128 us
    ppermute x46, starting transfers between devices, crossed(): return lax.ppermute(values, axes, [(i, i ^ distance) for i in range(size)])  59.3 us
    ppermute x5, waiting for transfers between devices, shifted(): lax.ppermute(values, axis, [(i, (i + distance) % size) for i in range(siz...  41.2 us
    pallas_call x1, Pallas kernels, attend_back(): pl.pallas_call(functools.partial(attend_back_kernel, len(pairs), block_ro...  38.4 us
    pallas_call x2, Pallas kernels, shampoo_half(): pl.pallas_call(kernel, grid_spec=pltpu.PrefetchScalarGridSpec(num_scalar_...  26.7 us
    all_to_all x6, waiting for transfers between devices, over_groups(): lax.all_to_all(values, ('a', 'b'), split_axis=0, concat_axis=0, tiled=True)  26.5 us
    all_to_all x6, starting transfers between devices, over_groups(): lax.all_to_all(values, ('a', 'b'), split_axis=0, concat_axis=0, tiled=True)  25.6 us
    pallas_call x2, Pallas kernels, expert_half_grads(): pl.pallas_call(kernel, grid=(hidden_blocks // 2,), in_specs=[smem_spec(),...  24.4 us
  transfers between devices with their start and end apart: 61, of which 28 were waited for; matrix products, arithmetic and copies ran while one was open for 13% of the time, Pallas kernels for 29%

profile of v4, /device:TPU:0, one launch (start us, length us, event | category | flops | bytes accessed | tf_op | source)
XLA Modules:
  0.0 600.4 jit_solution(14370302353433695427)
XLA Ops:
  22.8 13.6 %collective-permute-done.2.refs_6_ = bf16[18,128,128]{2,1,0:T(8,128)(2,1)} collective-permute-done((bf16[18,128,128]{2,1,0:T(8,128)(2,1)S(1)}, bf16[18,128,128]{2,1,0:T(8,128)(2,1)}, u32[]{:S(2)}, u32[]{:S(2)}) %collective-permute-start.2) | collective-permute-done | bytes 589856 | tf_op jit(solution)/shard_map/ppermute | solution.py:1077
  42.0 8.9 %project.1 = (bf16[384,768]{1,0:T(8,128)(2,1)}, f32[384,1]{1,0:T(8,128)}, bf16[4,192,384]{2,1,0:T(8,128)(2,1)}, bf16[4,384,384]{2,1,0:T(8,128)(2,1)}, bf16[3,256,2304]{2,1,0:T(8,128)(2,1)}) custom-call(s32[4]{0:T(128)} %pad_add_fusion.2.places_ref, f32[384,768]{1,0:T(8,128)} %rows_ref.1, f32[1,768]{1,0:T(1,128)} %get-tuple-element.318.gain_ref, ...), custom_call_target="tpu_custom_call" | custom-call | flops 589824 | bytes 1000000 | tf_op jit(solution)/shard_map/project/pallas_call | solution.py:143
  63.5 30.4 %collective-permute-done.7.refs_3_ = bf16[18,128,128]{2,1,0:T(8,128)(2,1)S(1)} collective-permute-done((bf16[18,128,128]{2,1,0:T(8,128)(2,1)S(1)}, bf16[18,128,128]{2,1,0:T(8,128)(2,1)S(1)}, u32[]{:S(2)}, u32[]{:S(2)}) %collective-permute-start.7) | collective-permute-done | bytes 589856 | tf_op jit(solution)/shard_map/ppermute | solution.py:1081
  104.0 17.8 %all-to-all-done.refs_2_ = bf16[4,192,384]{2,1,0:T(8,128)(2,1)S(1)} async-done(((bf16[4,192,384]{2,1,0:T(8,128)(2,1)}), bf16[4,192,384]{2,1,0:T(8,128)(2,1)S(1)}, u32[]{:S(2)}, u32[]{:S(2)}) %all-to-all-start) | async-done | bytes 589856 | tf_op jit(solution)/shard_map/all_to_all | solution.py:1196
  121.8 5.4 collective-permute-done.11
  133.2 20.5 %attend_forward.1 = (f32[4,384,192]{2,1,0:T(8,128)}, bf16[4,192,384]{2,1,0:T(8,128)(2,1)}, f32[16,288,1]{2,1,0:T(8,128)}) custom-call(s32[2,16]{1,0:T(2,128)} %pad_add_fusion.refs_0_, s32[4]{0:T(128)} %bitcast.208, bf16[4,192,384]{2,1,0:T(8,128)(2,1)} %copy-done.8, bf16[4,384,384]{2,1,0:T(8,128)(2,1)} %copy-done.5, bf16[4,384,384]{2,1,0:T(8,128)(2,1)} %copy-done.15), custom_call_target="tpu_custom_call" | custom-call | flops 98304 | bytes 1000000 | tf_op jit(solution)/shard_map/attend_forward/pallas_call | solution.py:382
  165.6 8.7 %all-to-all-done.2 = bf16[4,192,384]{2,1,0:T(8,128)(2,1)S(1)} async-done(((bf16[4,192,384]{2,1,0:T(8,128)(2,1)}), bf16[4,192,384]{2,1,0:T(8,128)(2,1)S(1)}, u32[]{:S(2)}, u32[]{:S(2)}) %all-to-all-start.2) | async-done | bytes 589856 | tf_op jit(solution)/shard_map/all_to_all | solution.py:1196
  179.4 4.9 collective-permute-done.16.refs_11_
  195.4 21.8 %collective-permute-done.17 = bf16[384,768]{1,0:T(8,128)(2,1)} collective-permute-done((bf16[384,768]{1,0:T(8,128)(2,1)}, bf16[384,768]{1,0:T(8,128)(2,1)}, u32[]{:S(2)}, u32[]{:S(2)}) %collective-permute-start.17) | collective-permute-done | bytes 589856 | tf_op jit(solution)/shard_map/ppermute | solution.py:1081
  221.4 4.8 all-to-all-start.3
  226.1 19.1 %expert_forward.1 = (bf16[768,768]{1,0:T(8,128)(2,1)}, f32[768,2048]{1,0:T(8,128)}, f32[768,2048]{1,0:T(8,128)}, bf16[768,2048]{1,0:T(8,128)(2,1)}) custom-call(s32[14]{0:T(128)} %stack.103.places_ref, bf16[768,768]{1,0:T(8,128)(2,1)} %bitcast.34.rows_ref, bf16[36,128,128]{2,1,0:T(8,128)(2,1)} %bitcast.186, ...), custom_call_target="tpu_custom_call" | custom-call | flops 7247757312 | bytes 11796480 | tf_op jit(solution)/shard_map/expert_forward/pallas_call | solution.py:649
  245.3 10.4 %all-to-all-done.3 = bf16[8,96,768]{2,1,0:T(8,128)(2,1)} async-done(((bf16[8,96,768]{2,1,0:T(8,128)(2,1)}), bf16[8,96,768]{2,1,0:T(8,128)(2,1)}, u32[]{:S(2)}, u32[]{:S(2)}) %all-to-all-start.3) | async-done | bytes 1179680 | tf_op jit(solution)/shard_map/all_to_all | solution.py:1171
  260.0 20.2 %expert_row_grads.1 = (bf16[768,768]{1,0:T(8,128)(2,1)}, bf16[768,2048]{1,0:T(8,128)(2,1)}, bf16[768,2048]{1,0:T(8,128)(2,1)}) custom-call(s32[14]{0:T(128)} %stack.103.places_ref, bf16[768,768]{1,0:T(8,128)(2,1)} %bitcast.32.grads_ref, f32[768,2048]{1,0:T(8,128)} %get-tuple-element.190.gate_i, f32[768,2048]{1,0:T(8,128)} %get-tuple-element.191.up_i, ...), custom_call_target="tpu_custom_call" | custom-call | flops 7247757312 | bytes 22413312 | tf_op jit(solution)/shard_map/expert_row_grads/pallas_call | solution.py:720
  280.3 12.2 %expert_half_grads.2 = (bf16[36,128,128]{2,1,0:T(8,128)(2,1)}, bf16[36,128,128]{2,1,0:T(8,128)(2,1)}, bf16[36,128,128]{2,1,0:T(8,128)(2,1)}, bf16[18,128,128]{2,1,0:T(8,128)(2,1)}, bf16[18,128,128]{2,1,0:T(8,128)(2,1)}) custom-call(s32[1]{0:T(128)S(6)} %sub.58.which_ref.half_ref, s32[7]{0:T(128)} %stack.111.places_ref, bf16[768,768]{1,0:T(8,128)(2,1)} %bitcast.34.rows_ref, ...), custom_call_target="tpu_custom_call" | custom-call | flops 3623878656 | bytes 12976128 | tf_op jit(solution)/shard_map/expert_half_grads/pallas_call | solution.py:875
  292.5 5.4 all-to-all-start.6
  311.0 12.2 %expert_half_grads.3 = (bf16[36,128,128]{2,1,0:T(8,128)(2,1)}, bf16[36,128,128]{2,1,0:T(8,128)(2,1)}, bf16[36,128,128]{2,1,0:T(8,128)(2,1)}, bf16[36,128,128]{2,1,0:T(8,128)(2,1)}) custom-call(s32[1]{0:T(128)} %bitcast.36.which_ref.half_ref, s32[4]{0:T(128)} %get-tuple-element.203.places_ref, bf16[768,768]{1,0:T(8,128)(2,1)} %bitcast.34.rows_ref, ...), custom_call_target="tpu_custom_call" | custom-call | flops 3623878656 | bytes 12976128 | tf_op jit(solution)/shard_map/expert_half_grads/pallas_call | solution.py:875
  332.0 8.0 %collective-permute-done.22 = bf16[36,128,128]{2,1,0:T(8,128)(2,1)} collective-permute-done((bf16[36,128,128]{2,1,0:T(8,128)(2,1)}, bf16[36,128,128]{2,1,0:T(8,128)(2,1)}, u32[]{:S(2)}, u32[]{:S(2)}) %collective-permute-start.22) | collective-permute-done | bytes 1179680 | tf_op jit(solution)/shard_map/ppermute | solution.py:1081
  347.1 5.5 all-to-all-start.7
  362.8 12.5 %collective-permute-done.30 = f32[15,768]{1,0:T(8,128)S(1)} collective-permute-done((f32[15,768]{1,0:T(8,128)S(1)}, f32[15,768]{1,0:T(8,128)S(1)}, u32[]{:S(2)}, u32[]{:S(2)}) %collective-permute-start.30) | collective-permute-done | bytes 46112 | tf_op jit(solution)/shard_map/ppermute | solution.py:1081
  375.3 5.2 collective-permute-start.29
  389.4 38.4 %attend_backward.1 = (bf16[4,384,192]{2,1,0:T(8,128)(2,1)}, f32[4,384,384]{2,1,0:T(8,128)}, bf16[4,384,384]{2,1,0:T(8,128)(2,1)}) custom-call(s32[2,16]{1,0:T(2,128)} %pad_add_fusion.refs_0_, s32[4]{0:T(128)} %bitcast.209, bf16[4,192,384]{2,1,0:T(8,128)(2,1)} %copy-done.8, bf16[4,384,384]{2,1,0:T(8,128)(2,1)} %copy-done.5, bf16[4,384,384]{2,1,0:T(8,128)(2,1)} %copy-done.15, ...), custom_call_target="tpu_custom_call" | custom-call | flops 98304 | bytes 1000000 | tf_op jit(solution)/shard_map/attend_backward/pallas_call | solution.py:543
  428.4 10.5 %collective-permute-done.33.refs_0_ = bf16[36,128,128]{2,1,0:T(8,128)(2,1)S(1)} collective-permute-done((bf16[36,128,128]{2,1,0:T(8,128)(2,1)S(1)}, bf16[36,128,128]{2,1,0:T(8,128)(2,1)S(1)}, u32[]{:S(2)}, u32[]{:S(2)}) %collective-permute-start.33) | collective-permute-done | bytes 1179680 | tf_op jit(solution)/shard_map/ppermute | solution.py:1077
  446.1 13.1 %shampoo_half.2 = (f32[72,128,128]{2,1,0:T(8,128)}, f32[72,128,128]{2,1,0:T(8,128)}, f32[72,128,128]{2,1,0:T(8,128)}, f32[72,128,128]{2,1,0:T(8,128)}) custom-call(s32[1]{0:T(128)S(6)} %sub.58.which_ref.half_ref, bf16[36,128,128]{2,1,0:T(8,128)(2,1)} %copy-done.25, bf16[72,128,128]{2,1,0:T(8,128)(2,1)} %bitcast.166, f32[72,128,128]{2,1,0:T(8,128)} %bitcast.168, ...), custom_call_target="tpu_custom_call" | custom-call | flops 1811939328 | bytes 21233664 | tf_op jit(solution)/shard_map/shampoo_half/pallas_call | solution.py:936
  465.2 7.5 %collective-permute-done.35 = bf16[4,384,384]{2,1,0:T(8,128)(2,1)S(1)} collective-permute-done((bf16[4,384,384]{2,1,0:T(8,128)(2,1)S(1)}, bf16[4,384,384]{2,1,0:T(8,128)(2,1)S(1)}, u32[]{:S(2)}, u32[]{:S(2)}) %collective-permute-start.35) | collective-permute-done | bytes 1179680 | tf_op jit(solution)/shard_map/ppermute | solution.py:1077
  480.8 5.1 all-to-all-start.9
  505.7 7.0 %collective-permute-done.37 = bf16[256,576]{1,0:T(8,128)(2,1)} collective-permute-done((bf16[256,576]{1,0:T(8,128)(2,1)}, bf16[256,576]{1,0:T(8,128)(2,1)}, u32[]{:S(2)}, u32[]{:S(2)}) %collective-permute-start.37) | collective-permute-done | bytes 294944 | tf_op jit(solution)/shard_map/ppermute | solution.py:1081
  515.9 8.1 %collective-permute-done.39 = bf16[256,576]{1,0:T(8,128)(2,1)S(1)} collective-permute-done((bf16[256,576]{1,0:T(8,128)(2,1)S(1)}, bf16[256,576]{1,0:T(8,128)(2,1)S(1)}, u32[]{:S(2)}, u32[]{:S(2)}) %collective-permute-start.39) | collective-permute-done | bytes 294944 | tf_op jit(solution)/shard_map/ppermute | solution.py:1081
  533.4 7.2 %collective-permute-done.40.refs_1_ = bf16[256,576]{1,0:T(8,128)(2,1)S(1)} collective-permute-done((bf16[256,576]{1,0:T(8,128)(2,1)S(1)}, bf16[256,576]{1,0:T(8,128)(2,1)S(1)}, u32[]{:S(2)}, u32[]{:S(2)}) %collective-permute-start.40) | collective-permute-done | bytes 294944 | tf_op jit(solution)/shard_map/ppermute | solution.py:1081
  540.6 11.1 %collective-permute-done.41.refs_2_ = bf16[256,576]{1,0:T(8,128)(2,1)S(1)} collective-permute-done((bf16[256,576]{1,0:T(8,128)(2,1)S(1)}, bf16[256,576]{1,0:T(8,128)(2,1)S(1)}, u32[]{:S(2)}, u32[]{:S(2)}) %collective-permute-start.41) | collective-permute-done | bytes 294944 | tf_op jit(solution)/shard_map/ppermute | solution.py:1081
  559.8 15.1 %shampoo_panel.1 = (f32[36,128,128]{2,1,0:T(8,128)}, f32[36,128,128]{2,1,0:T(8,128)}, f32[36,128,128]{2,1,0:T(8,128)}, f32[36,128,128]{2,1,0:T(8,128)}) custom-call(s32[1]{0:T(128)} %bitcast.72.turn_ref, s32[4]{0:T(128)} %get-tuple-element.253.places_ref, bf16[256,576]{1,0:T(8,128)(2,1)} %copy-done.23, bf16[256,576]{1,0:T(8,128)(2,1)} %copy-done.35, ...), custom_call_target="tpu_custom_call" | custom-call | flops 1811939328 | bytes 22413312 | tf_op jit(solution)/shard_map/shampoo_panel/pallas_call | solution.py:1041
  578.6 5.9 collective-permute-start.48
  586.0 13.6 %shampoo_half.3 = (f32[72,128,128]{2,1,0:T(8,128)}, f32[72,128,128]{2,1,0:T(8,128)}, f32[72,128,128]{2,1,0:T(8,128)}, f32[72,128,128]{2,1,0:T(8,128)}) custom-call(s32[1]{0:T(128)} %bitcast.36.which_ref.half_ref, bf16[36,128,128]{2,1,0:T(8,128)(2,1)} %get-tuple-element.269.refs_0_, ...), custom_call_target="tpu_custom_call", output_to_operand_aliasing={{0}: (9, {}), {1}: (10, {}), {2}: (11, {}), {3}: (12, {})} | custom-call | flops 1811939328 | bytes 23592960 | tf_op jit(solution)/shard_map/shampoo_half/pallas_call | solution.py:936
  (324 shorter events, 204.5 us)
Async XLA Ops:
  0.7 37.2 %collective-permute-start = (bf16[36,128,128]{2,1,0:T(8,128)(2,1)}, bf16[36,128,128]{2,1,0:T(8,128)(2,1)}, u32[]{:S(2)}, u32[]{:S(2)}) collective-permute-start(bf16[36,128,128]{2,1,0:T(8,128)(2,1)} %refs_4_.1), channel_id=1, source_target_pairs={{0,2},{1,3},{2,0},{3,1},{4,6},{5,7},{6,4},{7,5},{8,10},{9,11},{10,... | collective-permute-start | bytes 3538952 | tf_op jit(solution)/shard_map/ppermute | solution.py:1081
  3.7 36.1 %collective-permute-start.4 = (bf16[36,128,128]{2,1,0:T(8,128)(2,1)}, bf16[36,128,128]{2,1,0:T(8,128)(2,1)}, u32[]{:S(2)}, u32[]{:S(2)}) collective-permute-start(bf16[36,128,128]{2,1,0:T(8,128)(2,1)} %refs_4_.1), channel_id=1, source_target_pairs={{0,1},{1,0},{2,3},{3,2},{4,5},{5,4},{6,7},{7,6},{8,9},{9,8},{10,11... | collective-permute-start | bytes 3538952 | tf_op jit(solution)/shard_map/ppermute | solution.py:1081
  5.5 32.4 %collective-permute-start.1 = (bf16[36,128,128]{2,1,0:T(8,128)(2,1)S(1)}, bf16[36,128,128]{2,1,0:T(8,128)(2,1)}, u32[]{:S(2)}, u32[]{:S(2)}) collective-permute-start(bf16[36,128,128]{2,1,0:T(8,128)(2,1)S(1)} %bitcast.185), channel_id=1, source_target_pairs={{0,4},{4,0},{1,5},{5,1},{2,6},{6,2},{3,7},{7,3},{8,12},{12,8},{9,1... | collective-permute-start | bytes 3538952 | tf_op jit(solution)/shard_map/ppermute | solution.py:1081
  7.1 29.3 %collective-permute-start.2 = (bf16[18,128,128]{2,1,0:T(8,128)(2,1)S(1)}, bf16[18,128,128]{2,1,0:T(8,128)(2,1)}, u32[]{:S(2)}, u32[]{:S(2)}) collective-permute-start(bf16[18,128,128]{2,1,0:T(8,128)(2,1)S(1)} %slice_bitcast_fusion.2), channel_id=1, source_target_pairs={{0,16},{16,0},{1,17},{17,1},{2,18},{18,2},{3,19},{19,3},{4,20},{20... | collective-permute-start | bytes 1769480 | tf_op jit(solution)/shard_map/ppermute | solution.py:1077
  10.9 27.0 %collective-permute-start.3 = (bf16[18,128,128]{2,1,0:T(8,128)(2,1)}, bf16[18,128,128]{2,1,0:T(8,128)(2,1)}, u32[]{:S(2)}, u32[]{:S(2)}) collective-permute-start(bf16[18,128,128]{2,1,0:T(8,128)(2,1)} %get-tuple-element.317), channel_id=1, source_target_pairs={{0,8},{8,0},{1,9},{9,1},{2,10},{10,2},{3,11},{11,3},{4,12},{12,4},... | collective-permute-start | bytes 1769480 | tf_op jit(solution)/shard_map/ppermute | solution.py:1081
  55.8 39.2 %all-to-all-start.1 = ((bf16[4,384,384]{2,1,0:T(8,128)(2,1)}), bf16[4,384,384]{2,1,0:T(8,128)(2,1)S(1)}, u32[]{:S(2)}, u32[]{:S(2)}) async-start(bf16[4,384,384]{2,1,0:T(8,128)(2,1)} %get-tuple-element.155), calls=%async_computation.1 | async-start | bytes 2359296 | tf_op jit(solution)/shard_map/all_to_all | solution.py:1196
  59.5 34.4 %collective-permute-start.7 = (bf16[18,128,128]{2,1,0:T(8,128)(2,1)S(1)}, bf16[18,128,128]{2,1,0:T(8,128)(2,1)S(1)}, u32[]{:S(2)}, u32[]{:S(2)}) collective-permute-start(bf16[18,128,128]{2,1,0:T(8,128)(2,1)S(1)} %copy-done.33), channel_id=1, source_target_pairs={{0,8},{8,0},{1,9},{9,1},{2,10},{10,2},{3,11},{11,3},{4,12},{12,4},... | collective-permute-start | bytes 1769480 | tf_op jit(solution)/shard_map/ppermute | solution.py:1081
  61.5 32.5 %collective-permute-start.8 = (bf16[18,128,128]{2,1,0:T(8,128)(2,1)}, bf16[18,128,128]{2,1,0:T(8,128)(2,1)S(1)}, u32[]{:S(2)}, u32[]{:S(2)}) collective-permute-start(bf16[18,128,128]{2,1,0:T(8,128)(2,1)} %collective-permute-done.3.refs_2_), channel_id=1, source_target_pairs={{0,4},{4,0},{1,5},{5,1},{2,6},{6,2},{3,7},{7,3},{8,12},{12,8},{9,1... | collective-permute-start | bytes 1769480 | tf_op jit(solution)/shard_map/ppermute | solution.py:1081
  62.0 31.9 %collective-permute-start.9 = (bf16[18,128,128]{2,1,0:T(8,128)(2,1)}, bf16[18,128,128]{2,1,0:T(8,128)(2,1)}, u32[]{:S(2)}, u32[]{:S(2)}) collective-permute-start(bf16[18,128,128]{2,1,0:T(8,128)(2,1)} %collective-permute-done.2.refs_6_), channel_id=1, source_target_pairs={{0,4},{4,0},{1,5},{5,1},{2,6},{6,2},{3,7},{7,3},{8,12},{12,8},{9,1... | collective-permute-start | bytes 1769480 | tf_op jit(solution)/shard_map/ppermute | solution.py:1081
  95.0 32.1 %collective-permute-start.10 = (bf16[4,384,384]{2,1,0:T(8,128)(2,1)S(1)}, bf16[4,384,384]{2,1,0:T(8,128)(2,1)S(1)}, u32[]{:S(2)}, u32[]{:S(2)}) collective-permute-start(bf16[4,384,384]{2,1,0:T(8,128)(2,1)S(1)} %all-to-all-done.1.refs_3_), channel_id=1, source_target_pairs={{0,4},{4,0},{1,5},{5,1},{2,6},{6,2},{3,7},{7,3},{8,12},{12,8},{9,1... | collective-permute-start | bytes 3538952 | tf_op jit(solution)/shard_map/ppermute | solution.py:1081
  99.4 27.8 %collective-permute-start.11 = (bf16[9,128,128]{2,1,0:T(8,128)(2,1)}, bf16[9,128,128]{2,1,0:T(8,128)(2,1)}, u32[]{:S(2)}, u32[]{:S(2)}) collective-permute-start(bf16[9,128,128]{2,1,0:T(8,128)(2,1)} %get-tuple-element.159), channel_id=1, source_target_pairs={{0,16},{16,0},{1,17},{17,1},{2,18},{18,2},{3,19},{19,3},{4,20},{20... | collective-permute-start | bytes 884744 | tf_op jit(solution)/shard_map/ppermute | solution.py:1077
  129.0 26.5 %collective-permute-start.12 = (bf16[384,768]{1,0:T(8,128)(2,1)}, bf16[384,768]{1,0:T(8,128)(2,1)}, u32[]{:S(2)}, u32[]{:S(2)}) collective-permute-start(bf16[384,768]{1,0:T(8,128)(2,1)} %get-tuple-element.235), channel_id=1, source_target_pairs={{0,16},{8,24},{16,0},{24,8},{1,17},{9,25},{17,1},{25,9},{2,18},{10... | collective-permute-start | bytes 1769480 | tf_op jit(solution)/shard_map/ppermute | solution.py:1081
  129.0 26.5 %collective-permute-start.13 = (bf16[18,128,128]{2,1,0:T(8,128)(2,1)}, bf16[18,128,128]{2,1,0:T(8,128)(2,1)}, u32[]{:S(2)}, u32[]{:S(2)}) collective-permute-start(bf16[18,128,128]{2,1,0:T(8,128)(2,1)} %copy-done.49), channel_id=1, source_target_pairs={{0,4},{4,0},{1,5},{5,1},{2,6},{6,2},{3,7},{7,3},{8,12},{12,8},{9,1... | collective-permute-start | bytes 1769480 | tf_op jit(solution)/shard_map/ppermute | solution.py:1081
  131.1 26.6 %collective-permute-start.15 = (bf16[18,128,128]{2,1,0:T(8,128)(2,1)}, bf16[18,128,128]{2,1,0:T(8,128)(2,1)}, u32[]{:S(2)}, u32[]{:S(2)}) collective-permute-start(bf16[18,128,128]{2,1,0:T(8,128)(2,1)} %collective-permute-done.2.refs_6_), channel_id=1, source_target_pairs={{0,8},{8,0},{1,9},{9,1},{2,10},{10,2},{3,11},{11,3},{4,12},{12,4},... | collective-permute-start | bytes 1769480 | tf_op jit(solution)/shard_map/ppermute | solution.py:1081
  186.2 35.2 %all-to-all-start.4 = ((bf16[8,96,768]{2,1,0:T(8,128)(2,1)}), bf16[8,96,768]{2,1,0:T(8,128)(2,1)}, u32[]{:S(2)}, u32[]{:S(2)}) async-start(bf16[8,96,768]{2,1,0:T(8,128)(2,1)} %bitcast.202), calls=%async_computation.4 | async-start | bytes 2359296 | tf_op jit(solution)/shard_map/all_to_all | solution.py:1171
  192.4 27.1 %collective-permute-start.19 = (bf16[18,128,128]{2,1,0:T(8,128)(2,1)}, bf16[18,128,128]{2,1,0:T(8,128)(2,1)}, u32[]{:S(2)}, u32[]{:S(2)}) collective-permute-start(bf16[18,128,128]{2,1,0:T(8,128)(2,1)} %collective-permute-done.16.refs_11_), channel_id=1, source_target_pairs={{0,4},{4,0},{1,5},{5,1},{2,6},{6,2},{3,7},{7,3},{8,12},{12,8},{9,1... | collective-permute-start | bytes 1769480 | tf_op jit(solution)/shard_map/ppermute | solution.py:1081
  221.4 34.3 %all-to-all-start.3 = ((bf16[8,96,768]{2,1,0:T(8,128)(2,1)}), bf16[8,96,768]{2,1,0:T(8,128)(2,1)}, u32[]{:S(2)}, u32[]{:S(2)}) async-start(bf16[8,96,768]{2,1,0:T(8,128)(2,1)} %bitcast.188), calls=%async_computation.3 | async-start | bytes 2359296 | tf_op jit(solution)/shard_map/all_to_all | solution.py:1171
  255.6 36.8 %all-to-all-start.5 = ((bf16[8,96,768]{2,1,0:T(8,128)(2,1)}), bf16[8,96,768]{2,1,0:T(8,128)(2,1)}, u32[]{:S(2)}, u32[]{:S(2)}) async-start(bf16[8,96,768]{2,1,0:T(8,128)(2,1)} %bitcast.201), calls=%async_computation.5 | async-start | bytes 2359296 | tf_op jit(solution)/shard_map/all_to_all | solution.py:1175
  260.0 32.5 %collective-permute-start.20 = (bf16[384,768]{1,0:T(8,128)(2,1)}, bf16[384,768]{1,0:T(8,128)(2,1)}, u32[]{:S(2)}, u32[]{:S(2)}) collective-permute-start(bf16[384,768]{1,0:T(8,128)(2,1)} %collective-permute-done.12), channel_id=1, source_target_pairs={{0,8},{8,0},{1,9},{9,1},{2,10},{10,2},{3,11},{11,3},{4,12},{12,4},... | collective-permute-start | bytes 1769480 | tf_op jit(solution)/shard_map/ppermute | solution.py:1081
  292.5 35.0 %all-to-all-start.6 = ((bf16[8,96,768]{2,1,0:T(8,128)(2,1)}), bf16[8,96,768]{2,1,0:T(8,128)(2,1)}, u32[]{:S(2)}, u32[]{:S(2)}) async-start(bf16[8,96,768]{2,1,0:T(8,128)(2,1)} %bitcast.200), calls=%async_computation.6 | async-start | bytes 2359296 | tf_op jit(solution)/shard_map/all_to_all | solution.py:1175
  298.6 33.4 %collective-permute-start.21 = (bf16[36,128,128]{2,1,0:T(8,128)(2,1)}, bf16[36,128,128]{2,1,0:T(8,128)(2,1)}, u32[]{:S(2)}, u32[]{:S(2)}) collective-permute-start(bf16[36,128,128]{2,1,0:T(8,128)(2,1)} %get-tuple-element.210), channel_id=1, source_target_pairs={{0,4},{4,0},{1,5},{5,1},{2,6},{6,2},{3,7},{7,3},{8,12},{12,8},{9,1... | collective-permute-start | bytes 3538952 | tf_op jit(solution)/shard_map/ppermute | solution.py:1081
  300.1 39.9 %collective-permute-start.22 = (bf16[36,128,128]{2,1,0:T(8,128)(2,1)}, bf16[36,128,128]{2,1,0:T(8,128)(2,1)}, u32[]{:S(2)}, u32[]{:S(2)}) collective-permute-start(bf16[36,128,128]{2,1,0:T(8,128)(2,1)} %get-tuple-element.211), channel_id=1, source_target_pairs={{0,8},{8,0},{1,9},{9,1},{2,10},{10,2},{3,11},{11,3},{4,12},{12,4},... | collective-permute-start | bytes 3538952 | tf_op jit(solution)/shard_map/ppermute | solution.py:1081
  342.1 40.7 %collective-permute-start.25 = (bf16[36,128,128]{2,1,0:T(8,128)(2,1)}, bf16[36,128,128]{2,1,0:T(8,128)(2,1)}, u32[]{:S(2)}, u32[]{:S(2)}) collective-permute-start(bf16[36,128,128]{2,1,0:T(8,128)(2,1)} %get-tuple-element.216), channel_id=1, source_target_pairs={{0,4},{4,0},{1,5},{5,1},{2,6},{6,2},{3,7},{7,3},{8,12},{12,8},{9,1... | collective-permute-start | bytes 3538952 | tf_op jit(solution)/shard_map/ppermute | solution.py:1081
  347.1 35.6 %all-to-all-start.7 = ((bf16[4,192,384]{2,1,0:T(8,128)(2,1)}), bf16[4,192,384]{2,1,0:T(8,128)(2,1)S(1)}, u32[]{:S(2)}, u32[]{:S(2)}) async-start(bf16[4,192,384]{2,1,0:T(8,128)(2,1)} %reshape.357), calls=%async_computation.7 | async-start | bytes 1179648 | tf_op jit(solution)/shard_map/all_to_all | solution.py:1196
  356.1 26.5 %collective-permute-start.23 = (bf16[18,128,128]{2,1,0:T(8,128)(2,1)S(1)}, bf16[18,128,128]{2,1,0:T(8,128)(2,1)S(1)}, u32[]{:S(2)}, u32[]{:S(2)}) collective-permute-start(bf16[18,128,128]{2,1,0:T(8,128)(2,1)S(1)} %add_convert_fusion.6), channel_id=1, source_target_pairs={{0,8},{8,0},{1,9},{9,1},{2,10},{10,2},{3,11},{11,3},{4,12},{12,4},... | collective-permute-start | bytes 1769480 | tf_op jit(solution)/shard_map/ppermute | solution.py:1081
  382.7 45.7 %collective-permute-start.32 = (bf16[36,128,128]{2,1,0:T(8,128)(2,1)}, bf16[36,128,128]{2,1,0:T(8,128)(2,1)S(1)}, u32[]{:S(2)}, u32[]{:S(2)}) collective-permute-start(bf16[36,128,128]{2,1,0:T(8,128)(2,1)} %get-tuple-element.224), channel_id=1, source_target_pairs={{0,4},{4,0},{1,5},{5,1},{2,6},{6,2},{3,7},{7,3},{8,12},{12,8},{9,1... | collective-permute-start | bytes 3538952 | tf_op jit(solution)/shard_map/ppermute | solution.py:1081
  386.7 52.3 %collective-permute-start.33 = (bf16[36,128,128]{2,1,0:T(8,128)(2,1)S(1)}, bf16[36,128,128]{2,1,0:T(8,128)(2,1)S(1)}, u32[]{:S(2)}, u32[]{:S(2)}) collective-permute-start(bf16[36,128,128]{2,1,0:T(8,128)(2,1)S(1)} %pad_maximum_fusion.1), channel_id=1, source_target_pairs={{0,16},{16,0},{1,17},{17,1},{2,18},{18,2},{3,19},{19,3},{4,20},{20... | collective-permute-start | bytes 3538952 | tf_op jit(solution)/shard_map/ppermute | solution.py:1077
  388.3 39.5 %collective-permute-start.34 = (f32[15,768]{1,0:T(8,128)S(1)}, f32[15,768]{1,0:T(8,128)S(1)}, u32[]{:S(2)}, u32[]{:S(2)}) collective-permute-start(f32[15,768]{1,0:T(8,128)S(1)} %add_add_fusion), channel_id=1, source_target_pairs={{0,4},{4,0},{1,5},{5,1},{2,6},{6,2},{3,7},{7,3},{8,12},{12,8},{9,1... | collective-permute-start | bytes 138248 | tf_op jit(solution)/shard_map/ppermute | solution.py:1081
  441.1 32.8 %all-to-all-start.8 = ((bf16[4,768,192]{1,2,0:T(8,128)(2,1)}), bf16[4,768,192]{1,2,0:T(8,128)(2,1)S(1)}, u32[]{:S(2)}, u32[]{:S(2)}) async-start(bf16[4,768,192]{1,2,0:T(8,128)(2,1)} %convert_bitcast_fusion), calls=%async_computation.8 | async-start | bytes 2359296 | tf_op jit(solution)/shard_map/all_to_all | solution.py:1196
  445.1 27.6 %collective-permute-start.35 = (bf16[4,384,384]{2,1,0:T(8,128)(2,1)S(1)}, bf16[4,384,384]{2,1,0:T(8,128)(2,1)S(1)}, u32[]{:S(2)}, u32[]{:S(2)}) collective-permute-start(bf16[4,384,384]{2,1,0:T(8,128)(2,1)S(1)} %copy-done.48), channel_id=1, source_target_pairs={{0,4},{4,0},{1,5},{5,1},{2,6},{6,2},{3,7},{7,3},{8,12},{12,8},{9,1... | collective-permute-start | bytes 3538952 | tf_op jit(solution)/shard_map/ppermute | solution.py:1077
  480.8 71.7 %all-to-all-start.9 = ((bf16[4,384,576]{1,2,0:T(8,128)(2,1)}), bf16[4,384,576]{1,2,0:T(8,128)(2,1)S(1)}, u32[]{:S(2)}, u32[]{:S(2)}) async-start(bf16[4,384,576]{1,2,0:T(8,128)(2,1)} %copy.66), calls=%async_computation.9 | async-start | bytes 3538944 | tf_op jit(solution)/shard_map/all_to_all | solution.py:1196
  532.3 53.6 %collective-permute-start.50 = (bf16[36,128,128]{2,1,0:T(8,128)(2,1)}, bf16[36,128,128]{2,1,0:T(8,128)(2,1)}, u32[]{:S(2)}, u32[]{:S(2)}) collective-permute-start(bf16[36,128,128]{2,1,0:T(8,128)(2,1)} %add_convert_fusion), channel_id=1, source_target_pairs={{0,8},{8,0},{1,9},{9,1},{2,10},{10,2},{3,11},{11,3},{4,12},{12,4},... | collective-permute-start | bytes 3538952 | tf_op jit(solution)/shard_map/ppermute | solution.py:1081
  (82 other events, 1514.3 us)

commit v5 on v1

--- a/solution.py
+++ b/solution.py
@@ -1501,7 +1501,7 @@
         ]
         kept[0] = tie((kept[0], summed))[0]
         expert_outs = shampoo_half(half, kept, expert_stats, expert_outs)
-        late, early, *joined = tie((late, early, *group_panels, *expert_outs))
+        late, *joined = tie((late, *group_panels, *expert_outs))
         group_panels, expert_outs = joined[: HEAD_GROUPS - 1], joined[HEAD_GROUPS - 1 :]
         turn = (f_place == 3).astype(jnp.int32).reshape(1)
         attn_outs = shampoo_panel(

time: 605 us -> 601 us (level)
  waiting for transfers between devices: 214 us -> 193 us
  Pallas kernels: 171 us -> 178 us
    ppermute x46, waiting for transfers between devices: 130 us -> 122 us  [crossed(): return lax.ppermute(values, axes, [(i, i ^ distance) for i in range(size)])]
    all_to_all x6, waiting for transfers between devices: 38.8 us -> 30.8 us  [over_groups(): lax.all_to_all(values, ('a', 'b'), split_axis=0, concat_axis=0, tiled=True)]
  transfers between devices with their start and end apart: 61 -> 61, of which waited for: 27 -> 27; matrix products, arithmetic and copies ran while one was open for 11% -> 13% of each run, Pallas kernels for 26% -> 28%
where the time goes in v5:
time: 601 us; the launch traced here: 591 us
  waiting for transfers between devices  193 us (32%)
  Pallas kernels  178 us (30%)
  starting transfers between devices  109 us (18%)
  local copies, waits for them, and re-layouts  37.9 us (6%)
  matrix products  36.3 us (6%)
  other arithmetic  30.6 us (5%)
    ppermute x46, waiting for transfers between devices, crossed(): return lax.ppermute(values, axes, [(i, i ^ distance) for i in range(size)])  122 us
    ppermute x46, starting transfers between devices, crossed(): return lax.ppermute(values, axes, [(i, i ^ distance) for i in range(size)])  56.9 us
    pallas_call x1, Pallas kernels, attend_back(): pl.pallas_call(functools.partial(attend_back_kernel, len(pairs), block_ro...  41.8 us
    all_to_all x6, waiting for transfers between devices, over_groups(): lax.all_to_all(values, ('a', 'b'), split_axis=0, concat_axis=0, tiled=True)  30.8 us
    pallas_call x2, Pallas kernels, shampoo_half(): pl.pallas_call(kernel, grid_spec=pltpu.PrefetchScalarGridSpec(num_scalar_...  26.7 us
    ppermute x5, waiting for transfers between devices, shifted(): lax.ppermute(values, axis, [(i, (i + distance) % size) for i in range(siz...  26 us
    all_to_all x6, starting transfers between devices, over_groups(): lax.all_to_all(values, ('a', 'b'), split_axis=0, concat_axis=0, tiled=True)  25.2 us
    pallas_call x2, Pallas kernels, expert_half_grads(): pl.pallas_call(kernel, grid=(hidden_blocks // 2,), in_specs=[smem_spec(),...  24.3 us
  transfers between devices with their start and end apart: 61, of which 27 were waited for; matrix products, arithmetic and copies ran while one was open for 13% of the time, Pallas kernels for 28%

profile of v5, /device:TPU:0, one launch (start us, length us, event | category | flops | bytes accessed | tf_op | source)
XLA Modules:
  0.0 590.8 jit_solution(13304448270172743326)
XLA Ops:
  22.9 13.6 %collective-permute-done.3.refs_2_ = bf16[18,128,128]{2,1,0:T(8,128)(2,1)} collective-permute-done((bf16[18,128,128]{2,1,0:T(8,128)(2,1)}, bf16[18,128,128]{2,1,0:T(8,128)(2,1)}, u32[]{:S(2)}, u32[]{:S(2)}) %collective-permute-start.3) | collective-permute-done | bytes 589856 | tf_op jit(solution)/shard_map/ppermute | solution.py:1081
  42.8 8.9 %project.1 = (bf16[384,768]{1,0:T(8,128)(2,1)}, f32[384,1]{1,0:T(8,128)}, bf16[4,192,384]{2,1,0:T(8,128)(2,1)}, bf16[4,384,384]{2,1,0:T(8,128)(2,1)}, bf16[3,256,2304]{2,1,0:T(8,128)(2,1)}) custom-call(s32[4]{0:T(128)} %pad_add_fusion.2.places_ref, f32[384,768]{1,0:T(8,128)} %rows_ref.1, f32[1,768]{1,0:T(1,128)} %get-tuple-element.310.gain_ref, ...), custom_call_target="tpu_custom_call" | custom-call | flops 589824 | bytes 1000000 | tf_op jit(solution)/shard_map/project/pallas_call | solution.py:143
  51.7 4.4 collective-permute-done.6
  64.5 30.4 %collective-permute-done.7.refs_3_ = bf16[18,128,128]{2,1,0:T(8,128)(2,1)S(1)} collective-permute-done((bf16[18,128,128]{2,1,0:T(8,128)(2,1)S(1)}, bf16[18,128,128]{2,1,0:T(8,128)(2,1)S(1)}, u32[]{:S(2)}, u32[]{:S(2)}) %collective-permute-start.7) | collective-permute-done | bytes 589856 | tf_op jit(solution)/shard_map/ppermute | solution.py:1081
  105.0 17.8 %all-to-all-done.refs_2_ = bf16[4,192,384]{2,1,0:T(8,128)(2,1)S(1)} async-done(((bf16[4,192,384]{2,1,0:T(8,128)(2,1)}), bf16[4,192,384]{2,1,0:T(8,128)(2,1)S(1)}, u32[]{:S(2)}, u32[]{:S(2)}) %all-to-all-start) | async-done | bytes 589856 | tf_op jit(solution)/shard_map/all_to_all | solution.py:1196
  122.8 5.4 collective-permute-done.11
  134.2 22.1 %attend_forward.1 = (f32[4,384,192]{2,1,0:T(8,128)}, bf16[4,192,384]{2,1,0:T(8,128)(2,1)}, f32[16,288,1]{2,1,0:T(8,128)}) custom-call(s32[2,16]{1,0:T(2,128)} %pad_add_fusion.refs_0_, s32[4]{0:T(128)} %bitcast.208, bf16[4,192,384]{2,1,0:T(8,128)(2,1)} %copy-done.8, bf16[4,384,384]{2,1,0:T(8,128)(2,1)} %copy-done.5, bf16[4,384,384]{2,1,0:T(8,128)(2,1)} %copy-done.15), custom_call_target="tpu_custom_call" | custom-call | flops 98304 | bytes 1000000 | tf_op jit(solution)/shard_map/attend_forward/pallas_call | solution.py:382
  166.6 8.7 %all-to-all-done.2 = bf16[4,192,384]{2,1,0:T(8,128)(2,1)S(1)} async-done(((bf16[4,192,384]{2,1,0:T(8,128)(2,1)}), bf16[4,192,384]{2,1,0:T(8,128)(2,1)S(1)}, u32[]{:S(2)}, u32[]{:S(2)}) %all-to-all-start.2) | async-done | bytes 589856 | tf_op jit(solution)/shard_map/all_to_all | solution.py:1196
  180.5 4.9 collective-permute-done.16.refs_11_
  187.2 4.6 all-to-all-start.4
  196.4 21.8 %collective-permute-done.17 = bf16[384,768]{1,0:T(8,128)(2,1)} collective-permute-done((bf16[384,768]{1,0:T(8,128)(2,1)}, bf16[384,768]{1,0:T(8,128)(2,1)}, u32[]{:S(2)}, u32[]{:S(2)}) %collective-permute-start.17) | collective-permute-done | bytes 589856 | tf_op jit(solution)/shard_map/ppermute | solution.py:1081
  222.4 4.8 all-to-all-start.3
  227.1 19.1 %expert_forward.1 = (bf16[768,768]{1,0:T(8,128)(2,1)}, f32[768,2048]{1,0:T(8,128)}, f32[768,2048]{1,0:T(8,128)}, bf16[768,2048]{1,0:T(8,128)(2,1)}) custom-call(s32[14]{0:T(128)} %stack.103.places_ref, bf16[768,768]{1,0:T(8,128)(2,1)} %bitcast.34.rows_ref, bf16[36,128,128]{2,1,0:T(8,128)(2,1)} %bitcast.186, ...), custom_call_target="tpu_custom_call" | custom-call | flops 7247757312 | bytes 11796480 | tf_op jit(solution)/shard_map/expert_forward/pallas_call | solution.py:649
  246.3 10.4 %all-to-all-done.3 = bf16[8,96,768]{2,1,0:T(8,128)(2,1)} async-done(((bf16[8,96,768]{2,1,0:T(8,128)(2,1)}), bf16[8,96,768]{2,1,0:T(8,128)(2,1)}, u32[]{:S(2)}, u32[]{:S(2)}) %all-to-all-start.3) | async-done | bytes 1179680 | tf_op jit(solution)/shard_map/all_to_all | solution.py:1171
  261.0 20.2 %expert_row_grads.1 = (bf16[768,768]{1,0:T(8,128)(2,1)}, bf16[768,2048]{1,0:T(8,128)(2,1)}, bf16[768,2048]{1,0:T(8,128)(2,1)}) custom-call(s32[14]{0:T(128)} %stack.103.places_ref, bf16[768,768]{1,0:T(8,128)(2,1)} %bitcast.32.grads_ref, f32[768,2048]{1,0:T(8,128)} %get-tuple-element.186.gate_i, f32[768,2048]{1,0:T(8,128)} %get-tuple-element.187.up_i, ...), custom_call_target="tpu_custom_call" | custom-call | flops 7247757312 | bytes 22413312 | tf_op jit(solution)/shard_map/expert_row_grads/pallas_call | solution.py:720
  281.3 12.2 %expert_half_grads.2 = (bf16[36,128,128]{2,1,0:T(8,128)(2,1)}, bf16[36,128,128]{2,1,0:T(8,128)(2,1)}, bf16[36,128,128]{2,1,0:T(8,128)(2,1)}, bf16[18,128,128]{2,1,0:T(8,128)(2,1)}, bf16[18,128,128]{2,1,0:T(8,128)(2,1)}) custom-call(s32[1]{0:T(128)S(6)} %sub.58.which_ref.half_ref, s32[7]{0:T(128)} %stack.111.places_ref, bf16[768,768]{1,0:T(8,128)(2,1)} %bitcast.34.rows_ref, ...), custom_call_target="tpu_custom_call" | custom-call | flops 3623878656 | bytes 12976128 | tf_op jit(solution)/shard_map/expert_half_grads/pallas_call | solution.py:875
  293.4 5.4 all-to-all-start.6
  312.0 12.2 %expert_half_grads.3 = (bf16[36,128,128]{2,1,0:T(8,128)(2,1)}, bf16[36,128,128]{2,1,0:T(8,128)(2,1)}, bf16[36,128,128]{2,1,0:T(8,128)(2,1)}, bf16[36,128,128]{2,1,0:T(8,128)(2,1)}) custom-call(s32[1]{0:T(128)} %bitcast.36.which_ref.half_ref, s32[4]{0:T(128)} %get-tuple-element.199.places_ref, bf16[768,768]{1,0:T(8,128)(2,1)} %bitcast.34.rows_ref, ...), custom_call_target="tpu_custom_call" | custom-call | flops 3623878656 | bytes 12976128 | tf_op jit(solution)/shard_map/expert_half_grads/pallas_call | solution.py:875
  333.0 8.0 %collective-permute-done.22 = bf16[36,128,128]{2,1,0:T(8,128)(2,1)} collective-permute-done((bf16[36,128,128]{2,1,0:T(8,128)(2,1)}, bf16[36,128,128]{2,1,0:T(8,128)(2,1)}, u32[]{:S(2)}, u32[]{:S(2)}) %collective-permute-start.22) | collective-permute-done | bytes 1179680 | tf_op jit(solution)/shard_map/ppermute | solution.py:1081
  348.1 5.5 all-to-all-start.7
  363.6 16.0 %collective-permute-done.29 = f32[15,768]{1,0:T(8,128)S(1)} collective-permute-done((f32[15,768]{1,0:T(8,128)S(1)}, f32[15,768]{1,0:T(8,128)S(1)}, u32[]{:S(2)}, u32[]{:S(2)}) %collective-permute-start.29) | collective-permute-done | bytes 46112 | tf_op jit(solution)/shard_map/ppermute | solution.py:1081
  391.1 41.8 %attend_backward.1 = (bf16[4,384,192]{2,1,0:T(8,128)(2,1)}, f32[4,384,384]{2,1,0:T(8,128)}, bf16[4,384,384]{2,1,0:T(8,128)(2,1)}) custom-call(s32[2,16]{1,0:T(2,128)} %pad_add_fusion.refs_0_, s32[4]{0:T(128)} %bitcast.209, bf16[4,192,384]{2,1,0:T(8,128)(2,1)} %copy-done.8, bf16[4,384,384]{2,1,0:T(8,128)(2,1)} %copy-done.5, bf16[4,384,384]{2,1,0:T(8,128)(2,1)} %copy-done.15, ...), custom_call_target="tpu_custom_call" | custom-call | flops 98304 | bytes 1000000 | tf_op jit(solution)/shard_map/attend_backward/pallas_call | solution.py:543
  433.5 6.9 %collective-permute-done.33.refs_0_ = bf16[36,128,128]{2,1,0:T(8,128)(2,1)S(1)} collective-permute-done((bf16[36,128,128]{2,1,0:T(8,128)(2,1)S(1)}, bf16[36,128,128]{2,1,0:T(8,128)(2,1)S(1)}, u32[]{:S(2)}, u32[]{:S(2)}) %collective-permute-start.33) | collective-permute-done | bytes 1179680 | tf_op jit(solution)/shard_map/ppermute | solution.py:1077
  448.3 13.1 %shampoo_half.2 = (f32[72,128,128]{2,1,0:T(8,128)}, f32[72,128,128]{2,1,0:T(8,128)}, f32[72,128,128]{2,1,0:T(8,128)}, f32[72,128,128]{2,1,0:T(8,128)}) custom-call(s32[1]{0:T(128)S(6)} %sub.58.which_ref.half_ref, bf16[36,128,128]{2,1,0:T(8,128)(2,1)} %copy-done.25, bf16[72,128,128]{2,1,0:T(8,128)(2,1)} %bitcast.166, f32[72,128,128]{2,1,0:T(8,128)} %bitcast.168, ...), custom_call_target="tpu_custom_call" | custom-call | flops 1811939328 | bytes 21233664 | tf_op jit(solution)/shard_map/shampoo_half/pallas_call | solution.py:936
  467.4 7.2 %collective-permute-done.35 = bf16[4,384,384]{2,1,0:T(8,128)(2,1)S(1)} collective-permute-done((bf16[4,384,384]{2,1,0:T(8,128)(2,1)S(1)}, bf16[4,384,384]{2,1,0:T(8,128)(2,1)S(1)}, u32[]{:S(2)}, u32[]{:S(2)}) %collective-permute-start.35) | collective-permute-done | bytes 1179680 | tf_op jit(solution)/shard_map/ppermute | solution.py:1077
  475.8 4.6 convolution_convert_fusion.1
  482.7 5.0 all-to-all-start.9
  513.7 6.2 %collective-permute-done.45 = bf16[256,576]{1,0:T(8,128)(2,1)} collective-permute-done((bf16[256,576]{1,0:T(8,128)(2,1)}, bf16[256,576]{1,0:T(8,128)(2,1)}, u32[]{:S(2)}, u32[]{:S(2)}) %collective-permute-start.45) | collective-permute-done | bytes 294944 | tf_op jit(solution)/shard_map/ppermute | solution.py:1081
  523.7 4.3 all-to-all-done.9
  542.3 9.7 %collective-permute-done.50.refs_2_ = bf16[36,128,128]{2,1,0:T(8,128)(2,1)} collective-permute-done((bf16[36,128,128]{2,1,0:T(8,128)(2,1)}, bf16[36,128,128]{2,1,0:T(8,128)(2,1)}, u32[]{:S(2)}, u32[]{:S(2)}) %collective-permute-start.50) | collective-permute-done | bytes 1179680 | tf_op jit(solution)/shard_map/ppermute | solution.py:1081
  551.9 13.6 %shampoo_half.3 = (f32[72,128,128]{2,1,0:T(8,128)}, f32[72,128,128]{2,1,0:T(8,128)}, f32[72,128,128]{2,1,0:T(8,128)}, f32[72,128,128]{2,1,0:T(8,128)}) custom-call(s32[1]{0:T(128)} %bitcast.36.which_ref.half_ref, bf16[36,128,128]{2,1,0:T(8,128)(2,1)} %get-tuple-element.248.refs_0_, ...), custom_call_target="tpu_custom_call", output_to_operand_aliasing={{0}: (9, {}), {1}: (10, {}), {2}: (11, {}), {3}: (12, {})} | custom-call | flops 1811939328 | bytes 23592960 | tf_op jit(solution)/shard_map/shampoo_half/pallas_call | solution.py:936
  575.6 14.9 %shampoo_panel.1 = (f32[36,128,128]{2,1,0:T(8,128)}, f32[36,128,128]{2,1,0:T(8,128)}, f32[36,128,128]{2,1,0:T(8,128)}, f32[36,128,128]{2,1,0:T(8,128)}) custom-call(s32[1]{0:T(128)} %bitcast.72.turn_ref, s32[4]{0:T(128)} %get-tuple-element.262.places_ref, bf16[256,576]{1,0:T(8,128)(2,1)} %copy-done.23, bf16[256,576]{1,0:T(8,128)(2,1)} %copy-done.33, ...), custom_call_target="tpu_custom_call" | custom-call | flops 1811939328 | bytes 22413312 | tf_op jit(solution)/shard_map/shampoo_panel/pallas_call | solution.py:1041
  (316 shorter events, 201.3 us)
Async XLA Ops:
  0.7 38.1 %collective-permute-start = (bf16[36,128,128]{2,1,0:T(8,128)(2,1)}, bf16[36,128,128]{2,1,0:T(8,128)(2,1)}, u32[]{:S(2)}, u32[]{:S(2)}) collective-permute-start(bf16[36,128,128]{2,1,0:T(8,128)(2,1)} %refs_4_.1), channel_id=1, source_target_pairs={{0,2},{1,3},{2,0},{3,1},{4,6},{5,7},{6,4},{7,5},{8,10},{9,11},{10,... | collective-permute-start | bytes 3538952 | tf_op jit(solution)/shard_map/ppermute | solution.py:1081
  3.7 36.8 %collective-permute-start.4 = (bf16[36,128,128]{2,1,0:T(8,128)(2,1)}, bf16[36,128,128]{2,1,0:T(8,128)(2,1)}, u32[]{:S(2)}, u32[]{:S(2)}) collective-permute-start(bf16[36,128,128]{2,1,0:T(8,128)(2,1)} %refs_4_.1), channel_id=1, source_target_pairs={{0,1},{1,0},{2,3},{3,2},{4,5},{5,4},{6,7},{7,6},{8,9},{9,8},{10,11... | collective-permute-start | bytes 3538952 | tf_op jit(solution)/shard_map/ppermute | solution.py:1081
  5.5 33.3 %collective-permute-start.1 = (bf16[36,128,128]{2,1,0:T(8,128)(2,1)S(1)}, bf16[36,128,128]{2,1,0:T(8,128)(2,1)}, u32[]{:S(2)}, u32[]{:S(2)}) collective-permute-start(bf16[36,128,128]{2,1,0:T(8,128)(2,1)S(1)} %bitcast.185), channel_id=1, source_target_pairs={{0,4},{4,0},{1,5},{5,1},{2,6},{6,2},{3,7},{7,3},{8,12},{12,8},{9,1... | collective-permute-start | bytes 3538952 | tf_op jit(solution)/shard_map/ppermute | solution.py:1081
  8.1 28.4 %collective-permute-start.3 = (bf16[18,128,128]{2,1,0:T(8,128)(2,1)}, bf16[18,128,128]{2,1,0:T(8,128)(2,1)}, u32[]{:S(2)}, u32[]{:S(2)}) collective-permute-start(bf16[18,128,128]{2,1,0:T(8,128)(2,1)} %get-tuple-element.309), channel_id=1, source_target_pairs={{0,8},{8,0},{1,9},{9,1},{2,10},{10,2},{3,11},{11,3},{4,12},{12,4},... | collective-permute-start | bytes 1769480 | tf_op jit(solution)/shard_map/ppermute | solution.py:1081
  9.8 28.9 %collective-permute-start.2 = (bf16[18,128,128]{2,1,0:T(8,128)(2,1)S(1)}, bf16[18,128,128]{2,1,0:T(8,128)(2,1)}, u32[]{:S(2)}, u32[]{:S(2)}) collective-permute-start(bf16[18,128,128]{2,1,0:T(8,128)(2,1)S(1)} %slice_bitcast_fusion.2), channel_id=1, source_target_pairs={{0,16},{16,0},{1,17},{17,1},{2,18},{18,2},{3,19},{19,3},{4,20},{20... | collective-permute-start | bytes 1769480 | tf_op jit(solution)/shard_map/ppermute | solution.py:1077
  56.8 39.2 %all-to-all-start.1 = ((bf16[4,384,384]{2,1,0:T(8,128)(2,1)}), bf16[4,384,384]{2,1,0:T(8,128)(2,1)S(1)}, u32[]{:S(2)}, u32[]{:S(2)}) async-start(bf16[4,384,384]{2,1,0:T(8,128)(2,1)} %get-tuple-element.151), calls=%async_computation.1 | async-start | bytes 2359296 | tf_op jit(solution)/shard_map/all_to_all | solution.py:1196
  60.5 34.4 %collective-permute-start.7 = (bf16[18,128,128]{2,1,0:T(8,128)(2,1)S(1)}, bf16[18,128,128]{2,1,0:T(8,128)(2,1)S(1)}, u32[]{:S(2)}, u32[]{:S(2)}) collective-permute-start(bf16[18,128,128]{2,1,0:T(8,128)(2,1)S(1)} %copy-done.31), channel_id=1, source_target_pairs={{0,8},{8,0},{1,9},{9,1},{2,10},{10,2},{3,11},{11,3},{4,12},{12,4},... | collective-permute-start | bytes 1769480 | tf_op jit(solution)/shard_map/ppermute | solution.py:1081
  62.5 32.5 %collective-permute-start.8 = (bf16[18,128,128]{2,1,0:T(8,128)(2,1)}, bf16[18,128,128]{2,1,0:T(8,128)(2,1)S(1)}, u32[]{:S(2)}, u32[]{:S(2)}) collective-permute-start(bf16[18,128,128]{2,1,0:T(8,128)(2,1)} %collective-permute-done.3.refs_2_), channel_id=1, source_target_pairs={{0,4},{4,0},{1,5},{5,1},{2,6},{6,2},{3,7},{7,3},{8,12},{12,8},{9,1... | collective-permute-start | bytes 1769480 | tf_op jit(solution)/shard_map/ppermute | solution.py:1081
  63.0 31.9 %collective-permute-start.9 = (bf16[18,128,128]{2,1,0:T(8,128)(2,1)}, bf16[18,128,128]{2,1,0:T(8,128)(2,1)}, u32[]{:S(2)}, u32[]{:S(2)}) collective-permute-start(bf16[18,128,128]{2,1,0:T(8,128)(2,1)} %collective-permute-done.2.refs_6_), channel_id=1, source_target_pairs={{0,4},{4,0},{1,5},{5,1},{2,6},{6,2},{3,7},{7,3},{8,12},{12,8},{9,1... | collective-permute-start | bytes 1769480 | tf_op jit(solution)/shard_map/ppermute | solution.py:1081
  96.0 32.1 %collective-permute-start.10 = (bf16[4,384,384]{2,1,0:T(8,128)(2,1)S(1)}, bf16[4,384,384]{2,1,0:T(8,128)(2,1)S(1)}, u32[]{:S(2)}, u32[]{:S(2)}) collective-permute-start(bf16[4,384,384]{2,1,0:T(8,128)(2,1)S(1)} %all-to-all-done.1.refs_3_), channel_id=1, source_target_pairs={{0,4},{4,0},{1,5},{5,1},{2,6},{6,2},{3,7},{7,3},{8,12},{12,8},{9,1... | collective-permute-start | bytes 3538952 | tf_op jit(solution)/shard_map/ppermute | solution.py:1081
  100.4 27.8 %collective-permute-start.11 = (bf16[9,128,128]{2,1,0:T(8,128)(2,1)}, bf16[9,128,128]{2,1,0:T(8,128)(2,1)}, u32[]{:S(2)}, u32[]{:S(2)}) collective-permute-start(bf16[9,128,128]{2,1,0:T(8,128)(2,1)} %get-tuple-element.155), channel_id=1, source_target_pairs={{0,16},{16,0},{1,17},{17,1},{2,18},{18,2},{3,19},{19,3},{4,20},{20... | collective-permute-start | bytes 884744 | tf_op jit(solution)/shard_map/ppermute | solution.py:1077
  187.2 35.2 %all-to-all-start.4 = ((bf16[8,96,768]{2,1,0:T(8,128)(2,1)}), bf16[8,96,768]{2,1,0:T(8,128)(2,1)}, u32[]{:S(2)}, u32[]{:S(2)}) async-start(bf16[8,96,768]{2,1,0:T(8,128)(2,1)} %bitcast.202), calls=%async_computation.4 | async-start | bytes 2359296 | tf_op jit(solution)/shard_map/all_to_all | solution.py:1171
  193.4 27.1 %collective-permute-start.19 = (bf16[18,128,128]{2,1,0:T(8,128)(2,1)}, bf16[18,128,128]{2,1,0:T(8,128)(2,1)}, u32[]{:S(2)}, u32[]{:S(2)}) collective-permute-start(bf16[18,128,128]{2,1,0:T(8,128)(2,1)} %collective-permute-done.16.refs_11_), channel_id=1, source_target_pairs={{0,4},{4,0},{1,5},{5,1},{2,6},{6,2},{3,7},{7,3},{8,12},{12,8},{9,1... | collective-permute-start | bytes 1769480 | tf_op jit(solution)/shard_map/ppermute | solution.py:1081
  222.4 34.3 %all-to-all-start.3 = ((bf16[8,96,768]{2,1,0:T(8,128)(2,1)}), bf16[8,96,768]{2,1,0:T(8,128)(2,1)}, u32[]{:S(2)}, u32[]{:S(2)}) async-start(bf16[8,96,768]{2,1,0:T(8,128)(2,1)} %bitcast.188), calls=%async_computation.3 | async-start | bytes 2359296 | tf_op jit(solution)/shard_map/all_to_all | solution.py:1171
  256.7 36.8 %all-to-all-start.5 = ((bf16[8,96,768]{2,1,0:T(8,128)(2,1)}), bf16[8,96,768]{2,1,0:T(8,128)(2,1)}, u32[]{:S(2)}, u32[]{:S(2)}) async-start(bf16[8,96,768]{2,1,0:T(8,128)(2,1)} %bitcast.201), calls=%async_computation.5 | async-start | bytes 2359296 | tf_op jit(solution)/shard_map/all_to_all | solution.py:1175
  261.0 32.5 %collective-permute-start.20 = (bf16[384,768]{1,0:T(8,128)(2,1)}, bf16[384,768]{1,0:T(8,128)(2,1)}, u32[]{:S(2)}, u32[]{:S(2)}) collective-permute-start(bf16[384,768]{1,0:T(8,128)(2,1)} %collective-permute-done.12), channel_id=1, source_target_pairs={{0,8},{8,0},{1,9},{9,1},{2,10},{10,2},{3,11},{11,3},{4,12},{12,4},... | collective-permute-start | bytes 1769480 | tf_op jit(solution)/shard_map/ppermute | solution.py:1081
  293.4 35.0 %all-to-all-start.6 = ((bf16[8,96,768]{2,1,0:T(8,128)(2,1)}), bf16[8,96,768]{2,1,0:T(8,128)(2,1)}, u32[]{:S(2)}, u32[]{:S(2)}) async-start(bf16[8,96,768]{2,1,0:T(8,128)(2,1)} %bitcast.200), calls=%async_computation.6 | async-start | bytes 2359296 | tf_op jit(solution)/shard_map/all_to_all | solution.py:1175
  299.6 33.4 %collective-permute-start.21 = (bf16[36,128,128]{2,1,0:T(8,128)(2,1)}, bf16[36,128,128]{2,1,0:T(8,128)(2,1)}, u32[]{:S(2)}, u32[]{:S(2)}) collective-permute-start(bf16[36,128,128]{2,1,0:T(8,128)(2,1)} %get-tuple-element.206), channel_id=1, source_target_pairs={{0,4},{4,0},{1,5},{5,1},{2,6},{6,2},{3,7},{7,3},{8,12},{12,8},{9,1... | collective-permute-start | bytes 3538952 | tf_op jit(solution)/shard_map/ppermute | solution.py:1081
  301.1 39.9 %collective-permute-start.22 = (bf16[36,128,128]{2,1,0:T(8,128)(2,1)}, bf16[36,128,128]{2,1,0:T(8,128)(2,1)}, u32[]{:S(2)}, u32[]{:S(2)}) collective-permute-start(bf16[36,128,128]{2,1,0:T(8,128)(2,1)} %get-tuple-element.207), channel_id=1, source_target_pairs={{0,8},{8,0},{1,9},{9,1},{2,10},{10,2},{3,11},{11,3},{4,12},{12,4},... | collective-permute-start | bytes 3538952 | tf_op jit(solution)/shard_map/ppermute | solution.py:1081
  343.0 42.5 %collective-permute-start.25 = (bf16[36,128,128]{2,1,0:T(8,128)(2,1)}, bf16[36,128,128]{2,1,0:T(8,128)(2,1)}, u32[]{:S(2)}, u32[]{:S(2)}) collective-permute-start(bf16[36,128,128]{2,1,0:T(8,128)(2,1)} %get-tuple-element.212), channel_id=1, source_target_pairs={{0,4},{4,0},{1,5},{5,1},{2,6},{6,2},{3,7},{7,3},{8,12},{12,8},{9,1... | collective-permute-start | bytes 3538952 | tf_op jit(solution)/shard_map/ppermute | solution.py:1081
  348.1 37.5 %all-to-all-start.7 = ((bf16[4,192,384]{2,1,0:T(8,128)(2,1)}), bf16[4,192,384]{2,1,0:T(8,128)(2,1)S(1)}, u32[]{:S(2)}, u32[]{:S(2)}) async-start(bf16[4,192,384]{2,1,0:T(8,128)(2,1)} %reshape.357), calls=%async_computation.7 | async-start | bytes 1179648 | tf_op jit(solution)/shard_map/all_to_all | solution.py:1196
  355.5 30.0 %collective-permute-start.24 = (bf16[18,128,128]{2,1,0:T(8,128)(2,1)}, bf16[18,128,128]{2,1,0:T(8,128)(2,1)S(1)}, u32[]{:S(2)}, u32[]{:S(2)}) collective-permute-start(bf16[18,128,128]{2,1,0:T(8,128)(2,1)} %add_convert_fusion.5), channel_id=1, source_target_pairs={{0,4},{4,0},{1,5},{5,1},{2,6},{6,2},{3,7},{7,3},{8,12},{12,8},{9,1... | collective-permute-start | bytes 1769480 | tf_op jit(solution)/shard_map/ppermute | solution.py:1081
  387.9 52.5 %collective-permute-start.33 = (bf16[36,128,128]{2,1,0:T(8,128)(2,1)S(1)}, bf16[36,128,128]{2,1,0:T(8,128)(2,1)S(1)}, u32[]{:S(2)}, u32[]{:S(2)}) collective-permute-start(bf16[36,128,128]{2,1,0:T(8,128)(2,1)S(1)} %pad_maximum_fusion.1), channel_id=1, source_target_pairs={{0,16},{16,0},{1,17},{17,1},{2,18},{18,2},{3,19},{19,3},{4,20},{20... | collective-permute-start | bytes 3538952 | tf_op jit(solution)/shard_map/ppermute | solution.py:1077
  389.0 51.4 %collective-permute-start.32 = (bf16[36,128,128]{2,1,0:T(8,128)(2,1)S(1)}, bf16[36,128,128]{2,1,0:T(8,128)(2,1)S(1)}, u32[]{:S(2)}, u32[]{:S(2)}) collective-permute-start(bf16[36,128,128]{2,1,0:T(8,128)(2,1)S(1)} %copy-done.43), channel_id=1, source_target_pairs={{0,4},{4,0},{1,5},{5,1},{2,6},{6,2},{3,7},{7,3},{8,12},{12,8},{9,1... | collective-permute-start | bytes 3538952 | tf_op jit(solution)/shard_map/ppermute | solution.py:1081
  390.3 42.6 %collective-permute-start.34 = (f32[15,768]{1,0:T(8,128)S(1)}, f32[15,768]{1,0:T(8,128)S(1)}, u32[]{:S(2)}, u32[]{:S(2)}) collective-permute-start(f32[15,768]{1,0:T(8,128)S(1)} %add_add_fusion), channel_id=1, source_target_pairs={{0,4},{4,0},{1,5},{5,1},{2,6},{6,2},{3,7},{7,3},{8,12},{12,8},{9,1... | collective-permute-start | bytes 138248 | tf_op jit(solution)/shard_map/ppermute | solution.py:1081
  442.9 32.8 %all-to-all-start.8 = ((bf16[4,768,192]{1,2,0:T(8,128)(2,1)}), bf16[4,768,192]{1,2,0:T(8,128)(2,1)S(1)}, u32[]{:S(2)}, u32[]{:S(2)}) async-start(bf16[4,768,192]{1,2,0:T(8,128)(2,1)} %convert_bitcast_fusion), calls=%async_computation.8 | async-start | bytes 2359296 | tf_op jit(solution)/shard_map/all_to_all | solution.py:1196
  446.7 28.0 %collective-permute-start.35 = (bf16[4,384,384]{2,1,0:T(8,128)(2,1)S(1)}, bf16[4,384,384]{2,1,0:T(8,128)(2,1)S(1)}, u32[]{:S(2)}, u32[]{:S(2)}) collective-permute-start(bf16[4,384,384]{2,1,0:T(8,128)(2,1)S(1)} %copy-done.44), channel_id=1, source_target_pairs={{0,4},{4,0},{1,5},{5,1},{2,6},{6,2},{3,7},{7,3},{8,12},{12,8},{9,1... | collective-permute-start | bytes 3538952 | tf_op jit(solution)/shard_map/ppermute | solution.py:1077
  482.7 45.3 %all-to-all-start.9 = ((bf16[4,384,576]{1,2,0:T(8,128)(2,1)}), bf16[4,384,576]{1,2,0:T(8,128)(2,1)S(1)}, u32[]{:S(2)}, u32[]{:S(2)}) async-start(bf16[4,384,576]{1,2,0:T(8,128)(2,1)} %copy.66), calls=%async_computation.9 | async-start | bytes 3538944 | tf_op jit(solution)/shard_map/all_to_all | solution.py:1196
  492.8 59.1 %collective-permute-start.50 = (bf16[36,128,128]{2,1,0:T(8,128)(2,1)}, bf16[36,128,128]{2,1,0:T(8,128)(2,1)}, u32[]{:S(2)}, u32[]{:S(2)}) collective-permute-start(bf16[36,128,128]{2,1,0:T(8,128)(2,1)} %add_convert_fusion), channel_id=1, source_target_pairs={{0,8},{8,0},{1,9},{9,1},{2,10},{10,2},{3,11},{11,3},{4,12},{12,4},... | collective-permute-start | bytes 3538952 | tf_op jit(solution)/shard_map/ppermute | solution.py:1081
  536.1 38.5 %collective-permute-start.47 = (bf16[256,576]{1,0:T(8,128)(2,1)S(1)}, bf16[256,576]{1,0:T(8,128)(2,1)S(1)}, u32[]{:S(2)}, u32[]{:S(2)}) collective-permute-start(bf16[256,576]{1,0:T(8,128)(2,1)S(1)} %add_convert_fusion.7.refs_0_), channel_id=1, source_target_pairs={{0,8},{8,0},{16,24},{24,16},{1,9},{9,1},{17,25},{25,17},{2,10},{10... | collective-permute-start | bytes 884744 | tf_op jit(solution)/shard_map/ppermute | solution.py:1081
  536.2 38.4 %collective-permute-start.48 = (bf16[256,576]{1,0:T(8,128)(2,1)S(1)}, bf16[256,576]{1,0:T(8,128)(2,1)S(1)}, u32[]{:S(2)}, u32[]{:S(2)}) collective-permute-start(bf16[256,576]{1,0:T(8,128)(2,1)S(1)} %add_convert_fusion.7.refs_0_), channel_id=1, source_target_pairs={{0,16},{8,24},{16,0},{24,8},{1,17},{9,25},{17,1},{25,9},{2,18},{10... | collective-permute-start | bytes 884744 | tf_op jit(solution)/shard_map/ppermute | solution.py:1081
  538.2 36.4 %collective-permute-start.49 = (bf16[256,576]{1,0:T(8,128)(2,1)S(1)}, bf16[256,576]{1,0:T(8,128)(2,1)S(1)}, u32[]{:S(2)}, u32[]{:S(2)}) collective-permute-start(bf16[256,576]{1,0:T(8,128)(2,1)S(1)} %add_convert_fusion.7.refs_0_), channel_id=1, source_target_pairs={{0,24},{8,16},{16,8},{24,0},{1,25},{9,17},{17,9},{25,1},{2,26},{10... | collective-permute-start | bytes 884744 | tf_op jit(solution)/shard_map/ppermute | solution.py:1081
  (78 other events, 1402.3 us)
